TPU v7x, 32 devices: a whole 2x2x4 slice. The times are simulated.
32 devices in a mesh: head: 4 (over z), pool: 8 (over y, x, core).
Axes of the slice: x: 2, y: 2, z: 4, core: 2. Of those that a mesh axis runs over, the one named last changes fastest.
Arguments:
- queries: bfloat16 [80, 2048], P('pool', 'head'), may hold values from -6 to 6
- fresh_pair: bfloat16 [80, 2, 2048], P('pool', None, 'head'), may hold values from -6 to 6
- cache_blocks: bfloat16 [288, 2, 64, 2048], P('pool', None, None, 'head'), may hold values from -6 to 6
- block_table: int32 [80, 64], replicated, may hold values from -1 to 287, as said below
- lengths: int32 [80], replicated, may hold values from 65 to 4096, as said below
- residual: bfloat16 [80, 2048], P('pool'), may hold values from -6 to 6
- w_output: bfloat16 [2048, 2048], P('head'), may hold values from -0.125 to 0.125
- norm_gain: bfloat16 [2048], replicated, may hold values from 0.5 to 1.5
- routes: int32 [80, 6], replicated, may hold values from 0 to 63, all different within a row; in each aligned block of 10 rows (0 to 9, 10 to 19, ...) at most 2 rows name the same one
- route_gates: float32 [80, 6], replicated, may hold values from 0.1 to 0.6
- w_gate_up: bfloat16 [64, 2048, 2, 1408], P('pool', 'head'), may hold values from -0.125 to 0.125
- w_down: bfloat16 [64, 1408, 2048], P('pool', None, 'head'), may hold values from -0.15625 to 0.15625
- shared_gate_up: bfloat16 [1, 2048, 2, 1408], P(None, 'head'), may hold values from -0.125 to 0.125
- shared_down: bfloat16 [1, 1408, 2048], P(None, None, 'head'), may hold values from -0.15625 to 0.15625
- next_gain: bfloat16 [2048], replicated, may hold values from 0.5 to 1.5
- w_query_key_value: bfloat16 [2048, 6144], P(None, 'head'), may hold values from -0.125 to 0.125
Outputs:
- next_hidden: bfloat16 [80, 2048], P('pool')
- next_query_key_value: bfloat16 [80, 6144], P('pool', 'head')
Inputs may be any that keep to these rules, and one draw needn't show every extreme that they name: `block_table`: row r lists request r's blocks in order, then -1; 2 requests have 64 blocks and the others 2; no block is listed twice; block g lies on pool device g // 36. `lengths`: A request with n blocks holds (n - 1) * 64 + 1 to n * 64 tokens; some request holds 4096. `routes`: each row names 6 different experts; within the 10 rows of one pool device no expert is named more than 2 times, a bound that some block reaches.
All inputs are finite; a program needn't handle non-finite values.
Results may differ from a plain program's by a relative error of at most 0.025.
Values may be sent and summed in bfloat16 or wider, within the bound.
No kernel may reach another device: no remote copies, remote signals or barrier semaphores. Data moves between devices by JAX's collectives and lax.ppermute only.
A program may use at most 128 MiB of HBM per device.

v0:
```python
import math

import jax
import jax.numpy as jnp
from jax import lax
from jax.sharding import PartitionSpec as P

HD = 128


epsilon = 1e-06
floor_score = -1e30


def joined(value, axis, join):
    pieces = jax.tree.map(lambda part: lax.all_gather(part, axis), value)
    head = jax.tree.map(lambda part: part[0], pieces)
    tail = jax.tree.map(lambda part: part[1:], pieces)
    subtotal, _ = lax.scan(lambda subtotal, section: (join(subtotal, section), None), head, tail)
    return subtotal


def norm_rows(values, gain):
    mean_square = jnp.mean(values * values, axis=-1, keepdims=True)
    return values * lax.rsqrt(mean_square + epsilon) * gain.astype(jnp.float32)


def merge_parts(earlier, later):
    left_max, left_sum, left_acc = earlier
    right_max, right_sum, right_acc = later
    joint_max = jnp.maximum(left_max, right_max)
    left_scale = jnp.exp(left_max - joint_max)
    right_scale = jnp.exp(right_max - joint_max)
    return (
        joint_max,
        left_sum * left_scale + right_sum * right_scale,
        left_acc * left_scale[..., None] + right_acc * right_scale[..., None],
    )


def per_device(
    queries,
    fresh_pair,
    cache_blocks,
    block_table,
    lengths,
    residual,
    w_output,
    norm_gain,
    routes,
    route_gates,
    w_gate_up,
    w_down,
    shared_gate_up,
    shared_down,
    next_gain,
    w_query_key_value,
):
    pool_idx = lax.axis_index("pool")
    head_idx = lax.axis_index("head")
    req_dev, lane_width = queries.shape
    req_total, list_len = block_table.shape
    blk_count = cache_blocks.shape[0]
    block_len = cache_blocks.shape[2]
    head_count = lane_width // HD
    col_part = w_down.shape[2]
    col_start = head_idx * col_part
    score_scale = 1.0 / math.sqrt(HD)
    row_start = pool_idx * req_dev
    all_queries = lax.all_gather(queries, "pool", axis=0, tiled=True)
    block_ids = pool_idx * blk_count + jnp.arange(blk_count, dtype=jnp.int32)
    matches = block_table[None, :, :] == block_ids[:, None, None]
    owners_hot = jnp.any(matches, axis=2)
    block_rank = jnp.sum(
        jnp.where(matches, jnp.arange(list_len, dtype=jnp.int32)[None, None, :], 0), axis=(1, 2)
    )
    owner_length = jnp.sum(jnp.where(owners_hot, lengths[None, :], 0), axis=1)
    token_pos = block_rank[:, None] * block_len + jnp.arange(block_len, dtype=jnp.int32)[None, :]
    usable = token_pos < owner_length[:, None]
    onehot = owners_hot.astype(jnp.bfloat16)
    picked_queries = jnp.dot(onehot, all_queries, preferred_element_type=jnp.float32).astype(
        jnp.bfloat16
    )
    picked_queries = picked_queries.reshape(blk_count, head_count, HD)
    cache_keys = cache_blocks[:, 0].reshape(blk_count, block_len, head_count, HD)
    cache_values = cache_blocks[:, 1].reshape(blk_count, block_len, head_count, HD)
    scores = (
        jnp.einsum("bjhd,bhd->bjh", cache_keys, picked_queries, preferred_element_type=jnp.float32)
        * score_scale
    )
    scores = jnp.where(usable[:, :, None], scores, floor_score)
    block_max = jnp.max(scores, axis=1)
    part_max = jnp.max(
        jnp.where(owners_hot[:, :, None], block_max[:, None, :], floor_score), axis=0
    )
    block_shift = jnp.sum(jnp.where(owners_hot[:, :, None], part_max[None], 0.0), axis=1)
    weights_exp = jnp.where(usable[:, :, None], jnp.exp(scores - block_shift[:, None, :]), 0.0)
    block_total = jnp.sum(weights_exp, axis=1)
    block_acc = jnp.einsum(
        "bjh,bjhd->bhd",
        weights_exp,
        cache_values,
        preferred_element_type=jnp.float32,
        precision=lax.Precision.HIGHEST,
    )
    owner_float = owners_hot.astype(jnp.float32)
    part_sum = jnp.einsum("br,bh->rh", owner_float, block_total, precision=lax.Precision.HIGHEST)
    part_acc = jnp.einsum("br,bhd->rhd", owner_float, block_acc, precision=lax.Precision.HIGHEST)
    full_max, full_sum, full_acc = joined((part_max, part_sum, part_acc), "pool", merge_parts)
    mine_max = lax.dynamic_slice_in_dim(full_max, row_start, req_dev, 0)
    mine_sum = lax.dynamic_slice_in_dim(full_sum, row_start, req_dev, 0)
    mine_acc = lax.dynamic_slice_in_dim(full_acc, row_start, req_dev, 0)
    own_queries = queries.astype(jnp.float32).reshape(req_dev, head_count, HD)
    fresh_keys = fresh_pair[:, 0].astype(jnp.float32).reshape(req_dev, head_count, HD)
    fresh_values = fresh_pair[:, 1].astype(jnp.float32).reshape(req_dev, head_count, HD)
    fresh_score = jnp.sum(own_queries * fresh_keys, axis=-1) * score_scale
    joint_max = jnp.maximum(mine_max, fresh_score)
    old_scale = jnp.exp(mine_max - joint_max)
    fresh_weight = jnp.exp(fresh_score - joint_max)
    denominator = mine_sum * old_scale + fresh_weight
    numerator = mine_acc * old_scale[..., None] + fresh_weight[..., None] * fresh_values
    attended = (
        (numerator / denominator[..., None]).astype(jnp.bfloat16).reshape(req_dev, lane_width)
    )
    projected = jnp.dot(attended, w_output, preferred_element_type=jnp.float32)
    after_attention = residual.astype(jnp.float32) + lax.psum(
        projected.astype(jnp.bfloat16), "head"
    ).astype(jnp.float32)
    normed = norm_rows(after_attention, norm_gain).astype(jnp.bfloat16)
    normed_part = lax.dynamic_slice_in_dim(normed, col_start, col_part, 1)
    shared_pre = jnp.einsum(
        "td,sdcf->tscf", normed_part, shared_gate_up, preferred_element_type=jnp.float32
    )
    shared_pre = lax.psum(shared_pre.astype(jnp.bfloat16), "head").astype(jnp.float32)
    shared_hidden = (jax.nn.silu(shared_pre[:, :, 0]) * shared_pre[:, :, 1]).astype(jnp.bfloat16)
    shared_out = jnp.einsum(
        "tsf,sfd->td", shared_hidden, shared_down, preferred_element_type=jnp.float32
    )
    exp_dev = w_gate_up.shape[0]
    every_row = lax.all_gather(normed, "pool", axis=0, tiled=True)
    row_part = lax.dynamic_slice_in_dim(every_row, col_start, col_part, 1)
    local_ids = pool_idx * exp_dev + jnp.arange(exp_dev, dtype=jnp.int32)
    local_gate = jnp.sum(
        jnp.where(routes[:, :, None] == local_ids[None, None, :], route_gates[:, :, None], 0.0),
        axis=1,
    )
    preact = jnp.einsum("nd,edcf->necf", row_part, w_gate_up, preferred_element_type=jnp.float32)
    preact = lax.psum(preact.astype(jnp.bfloat16), "head").astype(jnp.float32)
    hidden = (jax.nn.silu(preact[:, :, 0]) * preact[:, :, 1]).astype(jnp.bfloat16)
    expert_out = jnp.einsum("nef,efd->ned", hidden, w_down, preferred_element_type=jnp.float32)
    routed = lax.psum_scatter(
        jnp.sum(expert_out * local_gate[:, :, None], axis=1).astype(jnp.bfloat16),
        "pool",
        scatter_dimension=0,
        tiled=True,
    ).astype(jnp.float32)
    ffn_full = lax.all_gather(routed + shared_out, "head", axis=1, tiled=True)
    after_ffn = after_attention + ffn_full
    next_normed = norm_rows(after_ffn, next_gain).astype(jnp.bfloat16)
    next_projection = jnp.dot(
        next_normed, w_query_key_value, preferred_element_type=jnp.float32
    ).astype(jnp.bfloat16)
    return (after_ffn.astype(jnp.bfloat16), next_projection)


def solution(mesh):
    in_specs = (
        P("pool", "head"),
        P("pool", None, "head"),
        P("pool", None, None, "head"),
        P(),
        P(),
        P("pool", None),
        P("head", None),
        P(),
        P(),
        P(),
        P("pool", "head", None, None),
        P("pool", None, "head"),
        P(None, "head", None, None),
        P(None, None, "head"),
        P(),
        P(None, "head"),
    )
    out_specs = (P("pool", None), P("pool", "head"))
    return jax.shard_map(
        per_device, mesh=mesh, in_specs=in_specs, out_specs=out_specs, check_vma=False
    )
```

profile of v0, /device:TPU:0, one launch (start us, length us, event | category | flops | bytes accessed | tf_op | source)
XLA Modules:
  0.0 354.6 jit_solution(10715752687906124707)
XLA Ops:
  7.2 1.2 compare_reduce_fusion
  8.4 1.6 fusion.37
  10.0 10.8 %all-gather.3 = bf16[8,10,512]{2,1,0:T(8,128)(2,1)S(1)} all-gather(bf16[1,10,512]{2,1,0:T(8,128)(2,1)} %bitcast.130), channel_id=1, replica_groups=mesh['head'=4,'pool'=8] {'pool'}, dimensions={0}, use_global_device_ids=true | all-gather | bytes 92160 | tf_op jit(solution)/shard_map/all_gather | solution.py:70
  20.9 0.8 select_reduce_fusion.3
  21.7 0.1 convolution_convert_fusion.2
  21.8 5.1 %fusion.71 = (bf16[36,1,64,512]{3,2,1,0:T(8,128)(2,1)}, bf16[36,1,64,512]{3,2,1,0:T(8,128)(2,1)}) fusion(bf16[36,2,64,512]{3,2,1,0:T(8,128)(2,1)} %param.20), kind=kLoop, calls=%fused_computation.92 | loop fusion | bytes 9437184 | tf_op jit(solution)/shard_map/slice | solution.py:86
  26.9 5.3 %reshape_squeeze.6 = bf16[36,64,4,128]{3,2,1,0:T(4,128)(2,1)} reshape(bf16[36,1,64,512]{3,2,1,0:T(8,128)(2,1)} %get-tuple-element.96) | data formatting | bytes 4718592 | tf_op jit(solution)/shard_map/reshape;squeeze | solution.py:85
  32.3 3.0 fusion.15
  35.3 0.1 bitcast_reduce_fusion
  35.4 0.1 select_reduce_fusion.1
  35.5 0.1 select_reduce_fusion
  35.7 0.2 fusion.69
  35.9 5.3 %reshape_squeeze.7 = bf16[36,64,4,128]{3,2,1,0:T(4,128)(2,1)} reshape(bf16[36,1,64,512]{3,2,1,0:T(8,128)(2,1)} %get-tuple-element.95) | data formatting | bytes 4718592 | tf_op jit(solution)/shard_map/reshape;squeeze | solution.py:86
  41.2 3.6 %fusion.13 = f32[36,4,1,128]{3,2,1,0:T(1,128)S(1)} fusion(f32[36,64,4,1]{1,3,2,0:T(1,128)S(1)} %bitcast.128, bf16[36,64,4,128]{3,2,1,0:T(4,128)(2,1)} %reshape_squeeze.7), kind=kOutput, calls=%fused_computation.19 | convolution fusion | flops 14155776 | bytes 2469888 | tf_op jit(solution)/shard_map/bjh,bjhd->bhd/dot_general | solution.py:99
  44.8 0.9 fusion.44
  45.8 0.2 convolution_bitcast_fusion
  46.0 8.7 %all-gather.5 = f32[8,80,4]{1,2,0:T(4,128)S(1)} all-gather(f32[1,80,4]{1,2,0:T(4,128)S(1)} %convolution_bitcast_fusion), channel_id=3, replica_groups=mesh['head'=4,'pool'=8] {'pool'}, dimensions={0}, use_global_device_ids=true | all-gather | bytes 11520 | tf_op jit(solution)/shard_map/all_gather | solution.py:16
  54.7 8.1 %all-gather.4 = f32[8,80,4]{1,2,0:T(4,128)S(1)} all-gather(f32[1,80,4]{1,2,0:T(4,128)S(1)} %bitcast.132), channel_id=2, replica_groups=mesh['head'=4,'pool'=8] {'pool'}, dimensions={0}, use_global_device_ids=true | all-gather | bytes 11520 | tf_op jit(solution)/shard_map/all_gather | solution.py:16
  63.0 7.9 %all-gather.9.cloned.1.call-done = f32[640,4,128]{2,0,1:T(8,128)} async-done(((f32[80,4,128]{2,0,1:T(8,128)}), f32[640,4,128]{2,0,1:T(8,128)}) %all-gather.9.cloned.1.call-update) | async-done | bytes 1310736 | tf_op jit(solution)/shard_map/all_gather | solution.py:16
  70.8 0.9 slice.68
  71.8 2.3 slice.71
  74.2 11.8 %while.14 = (s32[]{:T(128)}, f32[80,4]{0,1:T(4,128)S(1)}, f32[80,4]{0,1:T(4,128)S(1)}, f32[80,4,128]{2,1,0:T(4,128)S(1)}, f32[7,80,4]{1,2,0:T(4,128)S(1)}, /*ind...) while((s32[]{:T(128)}, f32[80,4]{0,1:T(4,128)S(1)}, f32[80,4]{0,1:T(4,128)S(1)}, ...), condition=%wide.region_8.9_spmd, body=%wide.region_7.8_spmd.sunk | while | flops 124802 | bytes 837213 | solution.py:19
  74.2 0.1 copy.105
  74.3 0.1 copy.106
  74.4 0.9 constant_dynamic-slice_fusion.2
  75.4 0.5 fusion.85
  75.9 0.1 copy.105
  76.0 0.1 copy.106
  76.1 0.9 constant_dynamic-slice_fusion.2
  77.0 0.5 fusion.85
  77.6 0.1 copy.105
  77.7 0.1 copy.106
  77.8 0.9 constant_dynamic-slice_fusion.2
  78.7 0.5 fusion.85
  79.5 0.9 constant_dynamic-slice_fusion.2
  80.4 0.5 fusion.85
  81.2 0.9 constant_dynamic-slice_fusion.2
  82.1 0.5 fusion.85
  82.9 0.9 constant_dynamic-slice_fusion.2
  83.8 0.5 fusion.85
  84.6 0.9 constant_dynamic-slice_fusion.2
  85.5 0.5 fusion.85
  86.0 0.1 copy.63
  86.1 0.1 copy.64
  86.2 0.1 fusion.55
  86.4 2.0 convolution_convert_fusion.1
  88.4 19.6 %psum.21 = bf16[10,2048]{1,0:T(8,128)(2,1)S(1)} all-reduce(bf16[10,2048]{1,0:T(8,128)(2,1)S(1)} %convolution_convert_fusion.1), channel_id=1, replica_groups=mesh['head'=4,'pool'=8] {'head'}, use_global_device_ids=true, to_apply=%region_10.11 | all-reduce | flops 20480 | bytes 81920 | tf_op jit(solution)/shard_map/psum | solution.py:126
  108.0 0.1 multiply_reduce_fusion.1
  108.2 0.6 copy-done.4
  108.8 10.0 %all-gather.6 = bf16[8,10,2048]{2,1,0:T(8,128)(2,1)S(1)} all-gather(bf16[1,10,2048]{2,1,0:T(8,128)(2,1)S(1)} %bitcast.123), channel_id=1, replica_groups=mesh['head'=4,'pool'=8] {'pool'}, dimensions={0}, use_global_device_ids=true | all-gather | bytes 368640 | tf_op jit(solution)/shard_map/all_gather | solution.py:140
  118.8 0.8 reshape.159
  119.7 15.7 %fusion.6 = bf16[80,8,2,1408]{3,0,2,1:T(8,128)(2,1)} fusion(bf16[8,512,2,1408]{3,2,1,0:T(2,128)(2,1)} %param.28, bf16[80,2048]{1,0:T(8,128)(2,1)} %reshape.159, s32[]{:T(128)S(6)} %select_n.47), kind=kOutput, calls=%fused_computation.12 | convolution fusion | flops 1847296000 | bytes 26755076 | tf_op jit(solution)/shard_map/nd,edcf->necf/dot_general | solution.py:147
  135.5 0.6 copy-done.8
  136.1 0.6 dynamic-slice
  137.4 1.2 fusion.20
  138.6 130.2 %all-reduce.4.cloned.1.call-done = bf16[80,8,2,1408]{3,0,2,1:T(8,128)(2,1)} async-done(((bf16[80,8,2,1408]{3,0,2,1:T(8,128)(2,1)}), bf16[80,8,2,1408]{3,0,2,1:T(8,128)(2,1)}) %all-reduce.4.cloned.1.call-update) | async-done | bytes 3604496 | tf_op jit(solution)/shard_map/psum | solution.py:148
  268.8 2.5 convert_element_type.95
  271.4 7.5 %fusion.34 = bf16[80,512]{1,0:T(8,128)(2,1)} fusion(bf16[8,1408,512]{2,1,0:T(8,128)(2,1)} %param.29, f32[80,8,2,1408]{3,0,2,1:T(8,128)S(1)} %convert_element_type.95, f32[80,8]{0,1:T(8,128)S(1)} %select_reduce_fusion.2), kind=kOutput, calls=%fused_computation.35 | convolution fusion | flops 928768000 | bytes 18827776 | tf_op jit(solution)/shard_map/nef,efd->ned/dot_general | solution.py:150
  278.9 18.0 %psum.23 = bf16[10,1,2,1408]{3,0,2,1:T(8,128)(2,1)S(1)} all-reduce(bf16[10,1,2,1408]{3,0,2,1:T(8,128)(2,1)S(1)} %fusion.20), channel_id=1, replica_groups=mesh['head'=4,'pool'=8] {'head'}, use_global_device_ids=true, to_apply=%region_16.17 | all-reduce | flops 28160 | bytes 112640 | tf_op jit(solution)/shard_map/psum | solution.py:134
  297.0 31.2 %all-reduce.6.cloned.1.call-done = bf16[80,512]{1,0:T(8,128)(2,1)} async-done(((bf16[80,512]{1,0:T(8,128)(2,1)}), bf16[80,512]{1,0:T(8,128)(2,1)}) %all-reduce.6.cloned.1.call-update) | async-done | bytes 81936
  328.1 1.0 fusion.38
  329.2 13.6 %all_gather.35 = f32[10,2048]{1,0:T(8,128)S(1)} all-gather(f32[10,512]{1,0:T(8,128)S(1)} %fusion.38), channel_id=1, replica_groups=mesh['head'=4,'pool'=8] {'head'}, dimensions={1}, use_global_device_ids=true | all-gather | bytes 102400 | tf_op jit(solution)/shard_map/all_gather | solution.py:157
  342.7 0.8 multiply_reduce_fusion
  343.5 4.5 %convolution_convert_fusion = bf16[10,1536]{1,0:T(8,128)(2,1)} fusion(bf16[2048,1536]{1,0:T(8,128)(2,1)} %param.33, f32[2048]{0:T(1024)S(1)} %convert_element_type.105, f32[10]{0:T(128)S(1)} %add_rsqrt_fusion, f32[10,2048]{1,0:T(8,128)S(1)} %all_gather.35, bf16[10,2048]{1,0:T(8,128)(2,1)S(1)} %psum.21, bf16[10,2048]{1,0:T(8,128)(2,1)S(1)} %copy-done.3), kind=kOutput, calls=%fused_computation.25 | convolution fusion | flops 63073280 | bytes 6494248 | tf_op jit(solution)/shard_map/dot_general | solution.py:160
  (67 shorter events, 1.8 us)
Async XLA Ops:
  7.2 130.2 %copy-start = (bf16[1,512,2,1408]{3,2,1,0:T(2,128)(2,1)S(1)}, bf16[1,512,2,1408]{3,2,1,0:T(2,128)(2,1)}, u32[]{:S(2)}) copy-start(bf16[1,512,2,1408]{3,2,1,0:T(2,128)(2,1)} %param.30) | copy-start | bytes 8650756
  7.2 63.7 %all-gather.9.cloned.1.call-start = ((), (), s32[]{:S(2)}) async-start(), calls=%async_computation.1 | async-start | bytes 1474560 | tf_op jit(solution)/shard_map/all_gather | solution.py:16
  41.2 4.7 %copy-start.6 = (bf16[10,512]{1,0:T(8,128)(2,1)S(1)}, bf16[10,512]{1,0:T(8,128)(2,1)}, u32[]{:S(2)}) copy-start(bf16[10,512]{1,0:T(8,128)(2,1)} %param.18) | copy-start | bytes 30724
  41.2 21.7 %copy-start.7 = (bf16[2048]{0:T(1024)(128)(2,1)S(1)}, bf16[2048]{0:T(1024)(128)(2,1)}, u32[]{:S(2)}) copy-start(bf16[2048]{0:T(1024)(128)(2,1)} %param.25) | copy-start | bytes 12292
  41.2 21.7 %copy-start.5 = (bf16[10,2,512]{2,1,0:T(2,128)(2,1)S(1)}, bf16[10,2,512]{2,1,0:T(2,128)(2,1)}, u32[]{:S(2)}) copy-start(bf16[10,2,512]{2,1,0:T(2,128)(2,1)} %param.19) | copy-start | bytes 61444
  45.8 223.1 %all-reduce.4.cloned.1.call-start = ((), (), s32[]{:S(2)}) async-start(), calls=%async_computation | async-start | bytes 7208960 | tf_op jit(solution)/shard_map/psum | solution.py:148
  86.0 21.9 %copy-start.3 = (bf16[10,2048]{1,0:T(8,128)(2,1)S(1)}, bf16[10,2048]{1,0:T(8,128)(2,1)}, u32[]{:S(2)}) copy-start(bf16[10,2048]{1,0:T(8,128)(2,1)} %param.23) | copy-start | bytes 122884
  108.2 0.6 copy-start.4
  135.4 0.7 copy-start.8
  135.4 0.7 copy-start.11
  135.4 1.9 copy-start.9
  135.4 1.9 copy-start.10
  135.4 192.7 %all-reduce.6.cloned.1.call-start = ((), (), s32[]{:S(2)}) async-start(), calls=%async_computation.2 | async-start | bytes 163840
  271.3 56.8 %copy-start.2 = (bf16[1,1408,512]{2,1,0:T(8,128)(2,1)S(1)}, bf16[1,1408,512]{2,1,0:T(8,128)(2,1)}, u32[]{:S(2)}) copy-start(bf16[1,1408,512]{2,1,0:T(8,128)(2,1)} %param.31) | copy-start | bytes 4325380
  343.5 4.5 %copy-start.1 = (bf16[1,512,2,1408]{3,2,1,0:T(2,128)(2,1)S(1)}, bf16[1,512,2,1408]{3,2,1,0:T(2,128)(2,1)}, u32[]{:S(2)}) copy-start(bf16[1,512,2,1408]{3,2,1,0:T(2,128)(2,1)} %param.30) | copy-start | bytes 8650756
Sparse Core Ops, SparseCore 0:
  45.9 24.9 all-gather.8
  135.5 133.2 all-reduce.3
  279.0 49.0 all-reduce.5
where the time goes:
time: 356 us; the launch traced here: 355 us
  waiting for transfers between devices  169 us (47%)
  blocking collectives  88.8 us (25%)
  matrix products  39.8 us (11%)
  local copies, waits for them, and re-layouts  29.9 us (8%)
  between operations  14.7 us (4%)
  other arithmetic  11.8 us (3%)
    psum x1, waiting for transfers between devices, per_device(): preact = lax.psum(preact.astype(jnp.bfloat16), 'head').astype(jnp.float32)  130 us
    unnamed x4, waiting for transfers between devices  31.2 us
    psum x1, blocking collectives, per_device(): lax.psum(projected.astype(jnp.bfloat16), 'head').astype(jnp.float32)  19.6 us
    psum x1, blocking collectives, per_device(): lax.psum(shared_pre.astype(jnp.bfloat16), 'head').astype(jnp.float32)  18 us
    all_gather x2, blocking collectives, joined(): pieces = jax.tree.map(lambda part: lax.all_gather(part, axis), value)  16.8 us
    dot_general x1, matrix products, per_device(): jnp.einsum('nd,edcf->necf', row_part, w_gate_up, preferred_element_type=j...  15.7 us
    all_gather x1, blocking collectives, per_device(): ffn_full = lax.all_gather(routed + shared_out, 'head', axis=1, tiled=True)  13.6 us
    all_gather x1, blocking collectives, per_device(): all_queries = lax.all_gather(queries, 'pool', axis=0, tiled=True)  10.8 us
  transfers between devices with their start and end apart: 3, of which 3 were waited for; matrix products, arithmetic and copies ran while one was open for 1% of the time, Pallas kernels for 0%

commit v1 on v0

v1 whole, which is shorter than its diff:
```python
import functools
import math

import jax
import jax.numpy as jnp
from jax import lax
from jax.experimental import pallas as pl
from jax.experimental.pallas import tpu as pltpu
from jax.sharding import PartitionSpec as P

HD = 128
LANES = 128
MOST = 2


epsilon = 1e-06
floor_score = -1e30
bf16 = jnp.bfloat16
f32 = jnp.float32


def swap(value, axis, distance):
    count = lax.axis_size(axis)
    return lax.ppermute(value, axis, [(i, i ^ distance) for i in range(count)])


def gather_xor(value, axis):
    count = lax.axis_size(axis)
    held = value[None]
    distance = 1
    while distance < count:
        held = jnp.concatenate([held, swap(held, axis, distance)], axis=0)
        distance *= 2
    return held


def gather_ordered(value, axis):
    held = gather_xor(value, axis)
    me = lax.axis_index(axis)
    return jnp.stack(
        [
            lax.dynamic_index_in_dim(held, me ^ place, 0, keepdims=False)
            for place in range(held.shape[0])
        ]
    )


def scatter_sum(chunks, axis):
    count = lax.axis_size(axis)
    me = lax.axis_index(axis)
    sent = [
        swap(lax.dynamic_index_in_dim(chunks, me ^ distance, 0, keepdims=False), axis, distance)
        for distance in range(1, count)
    ]
    total = lax.dynamic_index_in_dim(chunks, me, 0, keepdims=False).astype(f32)
    for piece in sent:
        total = total + piece.astype(f32)
    return total


def attention_kernel(place_ref, query_ref, cache_ref, limit_ref, fresh_ref, out_ref):
    req_total, lane_width = query_ref.shape
    blocks, _, block_len, _ = cache_ref.shape
    fresh_rows = fresh_ref.shape[1]
    tokens = blocks * block_len
    scale = 1.0 / math.sqrt(HD)
    block_of = lax.broadcasted_iota(jnp.int32, (blocks, tokens), 1) // block_len
    expand = block_of == lax.broadcasted_iota(jnp.int32, (blocks, tokens), 0)
    limits = jnp.dot(
        limit_ref[...], expand.astype(f32).astype(bf16), preferred_element_type=f32
    )
    within = lax.rem(lax.broadcasted_iota(jnp.int32, (req_total, tokens), 1), block_len)
    live = within.astype(f32) < limits
    row_ids = lax.broadcasted_iota(jnp.int32, (req_total, fresh_rows), 0)
    column_ids = lax.broadcasted_iota(jnp.int32, (req_total, fresh_rows), 1)
    req_dev = place_ref[1]
    own = jnp.logical_and(row_ids == column_ids + place_ref[0], column_ids < req_dev)
    lane = lax.broadcasted_iota(jnp.int32, (req_total, LANES), 1)
    side = jnp.zeros((req_total, LANES), f32)
    heads = lane_width // HD
    for head in range(heads):
        columns = slice(head * HD, (head + 1) * HD)
        query = query_ref[:, columns]
        keys = cache_ref[:, 0, :, columns].reshape(tokens, HD)
        values = cache_ref[:, 1, :, columns].reshape(tokens, HD)
        contract = (((1,), (1,)), ((), ()))
        scores = lax.dot_general(query, keys, contract, preferred_element_type=f32) * scale
        scores = jnp.where(live, scores, floor_score)
        new_scores = (
            lax.dot_general(query, fresh_ref[0, :, columns], contract, preferred_element_type=f32)
            * scale
        )
        new_scores = jnp.where(own, new_scores, floor_score)
        top = jnp.maximum(
            jnp.max(scores, axis=1, keepdims=True), jnp.max(new_scores, axis=1, keepdims=True)
        )
        top = top.astype(bf16).astype(f32)
        weights = jnp.where(live, jnp.exp(scores - top), 0.0)
        new_weights = jnp.where(own, jnp.exp(new_scores - top), 0.0)
        total = jnp.sum(weights, axis=1, keepdims=True) + jnp.sum(
            new_weights, axis=1, keepdims=True
        )
        mixed = jnp.dot(weights.astype(bf16), values, preferred_element_type=f32) + jnp.dot(
            new_weights.astype(bf16), fresh_ref[1, :, columns], preferred_element_type=f32
        )
        inverse = jnp.where(total > 0.0, 1.0 / jnp.where(total > 0.0, total, 1.0), 0.0)
        out_ref[:, columns] = (mixed * inverse).astype(bf16)
        coarse = total.astype(bf16).astype(f32)
        side = jnp.where(lane == head, top, side)
        side = jnp.where(lane == heads + head, coarse, side)
        side = jnp.where(lane == 2 * heads + head, total - coarse, side)
    out_ref[:, lane_width:] = side.astype(bf16)


def merge_kernel(parts_ref, weight_ref, out_ref, attended_ref):
    count, req_total, packed = parts_ref.shape
    lane_width = packed - LANES
    heads = lane_width // HD
    chunks, _, chunk_width = out_ref.shape
    lane = lax.broadcasted_iota(jnp.int32, (req_total, LANES), 1)
    sides = [parts_ref[i, :, lane_width:].astype(f32) for i in range(count)]

    def column(side, place):
        return jnp.sum(jnp.where(lane == place, side, 0.0), axis=1, keepdims=True)

    for head in range(heads):
        columns = slice(head * HD, (head + 1) * HD)
        tops = [column(side, head) for side in sides]
        totals = [column(side, heads + head) + column(side, 2 * heads + head) for side in sides]
        top = functools.reduce(jnp.maximum, tops)
        shares = [total * jnp.exp(part - top) for part, total in zip(tops, totals)]
        denominator = functools.reduce(jnp.add, shares)
        mixed = functools.reduce(
            jnp.add,
            [shares[i] * parts_ref[i, :, columns].astype(f32) for i in range(count)],
        )
        attended_ref[:, columns] = (mixed / denominator).astype(bf16)
    for chunk in range(chunks):
        out_ref[chunk] = jnp.dot(
            attended_ref[...],
            weight_ref[:, chunk * chunk_width : (chunk + 1) * chunk_width],
            preferred_element_type=f32,
        ).astype(bf16)


def norm_rows(values, gain):
    mean_square = jnp.mean(values * values, axis=-1, keepdims=True)
    return values * lax.rsqrt(mean_square + epsilon) * gain.astype(f32)


def split_float(value):
    coarse = value.astype(bf16)
    return coarse, (value - coarse.astype(f32)).astype(bf16)


def per_device(
    queries,
    fresh_pair,
    cache_blocks,
    block_table,
    lengths,
    residual,
    w_output,
    norm_gain,
    routes,
    route_gates,
    w_gate_up,
    w_down,
    shared_gate_up,
    shared_down,
    next_gain,
    w_query_key_value,
):
    pool_idx = lax.axis_index("pool")
    head_idx = lax.axis_index("head")
    pools = lax.axis_size("pool")
    head_devs = lax.axis_size("head")
    req_dev, lane_width = queries.shape
    req_total, list_len = block_table.shape
    blk_count, _, block_len, _ = cache_blocks.shape
    exp_dev, col_part, _, ffe = w_gate_up.shape
    width = residual.shape[1]
    row_start = pool_idx * req_dev
    col_start = head_idx * col_part

    residual_part = lax.dynamic_slice_in_dim(residual, col_start, col_part, 1)
    gathered = lax.all_gather(
        jnp.concatenate([queries, residual_part], axis=1), "pool", axis=0, tiled=True
    )
    all_queries = gathered[:, :lane_width]
    all_residual = gathered[:, lane_width:].astype(f32)

    block_ids = pool_idx * blk_count + jnp.arange(blk_count, dtype=jnp.int32)
    left = lengths[:, None] - jnp.arange(list_len, dtype=jnp.int32)[None, :] * block_len
    limits = jnp.sum(
        jnp.where(block_table[:, None, :] == block_ids[None, :, None], left[:, None, :], 0), axis=2
    )
    limits = jnp.clip(limits, 0, block_len).astype(bf16)
    fresh_rows = -(-req_dev // 16) * 16
    fresh = jnp.pad(jnp.swapaxes(fresh_pair, 0, 1), ((0, 0), (0, fresh_rows - req_dev), (0, 0)))
    place = jnp.stack([row_start, jnp.int32(req_dev)]).astype(jnp.int32)
    vmem = pl.BlockSpec(memory_space=pltpu.VMEM)
    partial = pl.pallas_call(
        attention_kernel,
        out_shape=jax.ShapeDtypeStruct((req_total, lane_width + LANES), bf16),
        in_specs=[pl.BlockSpec(memory_space=pltpu.SMEM)] + [vmem] * 4,
        out_specs=vmem,
        compiler_params=pltpu.CompilerParams(vmem_limit_bytes=40 * 1024 * 1024),
        name="attention",
    )(place, all_queries, cache_blocks, limits, fresh)

    parts = lax.all_gather(partial, "pool", axis=0)
    projected = pl.pallas_call(
        merge_kernel,
        out_shape=jax.ShapeDtypeStruct((head_devs, req_total, col_part), bf16),
        in_specs=[vmem] * 2,
        out_specs=vmem,
        scratch_shapes=[pltpu.VMEM((req_total, lane_width), bf16)],
        compiler_params=pltpu.CompilerParams(vmem_limit_bytes=40 * 1024 * 1024),
        name="merge_project",
    )(parts, w_output)
    after_attention = all_residual + scatter_sum(projected, "head")

    gain_part = lax.dynamic_slice_in_dim(norm_gain, col_start, col_part, 0).astype(f32)
    scaled = (after_attention * gain_part[None, :]).astype(bf16)
    squares = jnp.sum(after_attention * after_attention, axis=1, keepdims=True)
    coarse, fine = split_float(squares)
    side = jnp.pad(jnp.concatenate([coarse, fine], axis=1), ((0, 0), (0, LANES - 2)))
    rows = jnp.concatenate([scaled, side], axis=1)

    slots = min(MOST * pools, req_total)
    local_ids = pool_idx * exp_dev + jnp.arange(exp_dev, dtype=jnp.int32)
    named = routes[:, :, None] == local_ids[None, None, :]
    gate = jnp.sum(jnp.where(named, route_gates[:, :, None], 0.0), axis=1)
    chosen = jnp.any(named, axis=1)
    earlier = jnp.tril(jnp.ones((req_total, req_total), bf16), -1)
    rank = jnp.dot(earlier, chosen.astype(bf16), preferred_element_type=f32)
    slot_ids = jnp.arange(slots, dtype=jnp.int32).astype(f32)
    pick = jnp.logical_and(
        chosen.T[:, None, :], rank.T[:, None, :] == slot_ids[None, :, None]
    )
    slot_gate = jnp.sum(jnp.where(pick, gate.T[:, None, :], 0.0), axis=2)
    pick = pick.astype(bf16)

    picked = jnp.einsum("ekt,td->ekd", pick, rows, preferred_element_type=f32).astype(bf16)
    own_rows = lax.dynamic_slice_in_dim(rows, row_start, req_dev, 0)
    routed_pre = jnp.einsum(
        "ekd,edcf->ekcf", picked[:, :, :col_part], w_gate_up, preferred_element_type=f32
    ).astype(bf16)
    shared_pre = jnp.einsum(
        "td,dcf->tcf", own_rows[:, :col_part], shared_gate_up[0], preferred_element_type=f32
    ).astype(bf16)
    shared_rows = -(-req_dev // head_devs) * head_devs
    routed_payload = jnp.concatenate(
        [routed_pre.reshape(exp_dev * slots, 2 * ffe), picked[:, :, col_part:].reshape(-1, LANES)],
        axis=1,
    ).reshape(head_devs, -1, 2 * ffe + LANES)
    shared_payload = jnp.pad(
        jnp.concatenate([shared_pre.reshape(req_dev, 2 * ffe), own_rows[:, col_part:]], axis=1),
        ((0, shared_rows - req_dev), (0, 0)),
    ).reshape(head_devs, -1, 2 * ffe + LANES)
    payload = jnp.concatenate([routed_payload, shared_payload], axis=1)
    sums = scatter_sum(payload, "head")
    square_sum = sums[:, 2 * ffe : 2 * ffe + 1] + sums[:, 2 * ffe + 1 : 2 * ffe + 2]
    row_scale = lax.rsqrt(square_sum / width + epsilon)
    gates = sums[:, :ffe] * row_scale
    ups = sums[:, ffe : 2 * ffe] * row_scale
    hidden = (jax.nn.silu(gates) * ups).astype(bf16)

    all_hidden = gather_ordered(hidden, "head")
    routed_part = routed_payload.shape[1]
    routed_hidden = all_hidden[:, :routed_part].reshape(exp_dev, slots, ffe)
    shared_hidden = all_hidden[:, routed_part:].reshape(shared_rows, ffe)
    expert_out = jnp.einsum("ekf,efd->ekd", routed_hidden, w_down, preferred_element_type=f32)
    shared_out = jnp.dot(shared_hidden, shared_down[0], preferred_element_type=f32)[:req_dev]
    weighted = (expert_out * slot_gate[:, :, None]).astype(bf16)
    routed = jnp.einsum("ekt,ekd->td", pick, weighted, preferred_element_type=f32)
    pieces = lax.all_to_all(
        routed.astype(bf16).reshape(pools, req_dev, col_part), "pool", 0, 0
    )
    own_after = lax.dynamic_slice_in_dim(after_attention, row_start, req_dev, 0)
    block = own_after + shared_out + jnp.sum(pieces.astype(f32), axis=0)

    after_ffn = gather_ordered(block, "head")
    after_ffn = jnp.swapaxes(after_ffn, 0, 1).reshape(req_dev, width)
    next_normed = norm_rows(after_ffn, next_gain).astype(bf16)
    next_projection = jnp.dot(
        next_normed, w_query_key_value, preferred_element_type=f32
    ).astype(bf16)
    return (after_ffn.astype(bf16), next_projection)


def solution(mesh):
    in_specs = (
        P("pool", "head"),
        P("pool", None, "head"),
        P("pool", None, None, "head"),
        P(),
        P(),
        P("pool", None),
        P("head", None),
        P(),
        P(),
        P(),
        P("pool", "head", None, None),
        P("pool", None, "head"),
        P(None, "head", None, None),
        P(None, None, "head"),
        P(),
        P(None, "head"),
    )
    out_specs = (P("pool", None), P("pool", "head"))
    return jax.shard_map(
        per_device, mesh=mesh, in_specs=in_specs, out_specs=out_specs, check_vma=False
    )
```

time: 356 us -> 141 us (0.40)
  waiting for transfers between devices: 169 us -> 43.8 us
  blocking collectives: 88.8 us -> 21.3 us
  starting transfers between devices: 0.12 us -> 18.7 us
  local copies, waits for them, and re-layouts: 29.9 us -> 13.2 us
  between operations: 14.7 us -> 1.04 us
  matrix products: 39.8 us -> 27.9 us
  Pallas kernels: 0 us -> 4.8 us
    psum x1 -> x0, waiting for transfers between devices: 130 us -> none  [per_device(): preact = lax.psum(preact.astype(jnp.bfloat16), 'head').astype(jnp.float32)]
    ppermute x0 -> x10, waiting for transfers between devices: none -> 39.2 us  [swap(): return lax.ppermute(value, axis, [(i, i ^ distance) for i in range(count)])]
    psum x2 -> x0, blocking collectives: 37.6 us -> none  [the longest x1 19.6 us: per_device(): lax.psum(projected.astype(jnp.bfloat16), 'head').astype(jnp.float32)]
    unnamed x4 -> x0, waiting for transfers between devices: 31.2 us -> none
    all_gather x5 -> x2, blocking collectives: 51.2 us -> 21.3 us  [the longest x1 10.8 us: per_device(): lax.all_gather(jnp.concatenate([queries, residual_part], axis=1), 'pool',...]
    ppermute x0 -> x10, starting transfers between devices: none -> 15.3 us  [swap(): return lax.ppermute(value, axis, [(i, i ^ distance) for i in range(count)])]
    dot_general x11 -> x7, matrix products: 39.8 us -> 27.9 us  [the longest x1 13.6 us: per_device(): jnp.einsum('ekd,edcf->ekcf', picked[:, :, :col_part], w_gate_up, preferre...]
    another operation x2 -> x0, local copies, waits for them, and re-layouts: 10.6 us -> none  [the longest x1 5.3 us: per_device(): cache_blocks[:, 0].reshape(blk_count, block_len, head_count, HD)]
  transfers between devices with their start and end apart: 3 -> 11, of which waited for: 3 -> 8; matrix products, arithmetic and copies ran while one was open for 1% -> 3% of each run, Pallas kernels for 0% -> 0%
where the time goes in v1:
time: 141 us
  waiting for transfers between devices  43.8 us (31%)
  matrix products  27.9 us (20%)
  blocking collectives  21.3 us (15%)
  starting transfers between devices  18.7 us (13%)
  local copies, waits for them, and re-layouts  13.2 us (9%)
  other arithmetic  9.89 us (7%)
  Pallas kernels  4.8 us (3%)
    ppermute x10, waiting for transfers between devices, swap(): return lax.ppermute(value, axis, [(i, i ^ distance) for i in range(count)])  39.2 us
    ppermute x10, starting transfers between devices, swap(): return lax.ppermute(value, axis, [(i, i ^ distance) for i in range(count)])  15.3 us
    dot_general x1, matrix products, per_device(): jnp.einsum('ekd,edcf->ekcf', picked[:, :, :col_part], w_gate_up, preferre...  13.6 us
    all_gather x1, blocking collectives, per_device(): lax.all_gather(jnp.concatenate([queries, residual_part], axis=1), 'pool',...  10.8 us
    all_gather x1, blocking collectives, per_device(): parts = lax.all_gather(partial, 'pool', axis=0)  10.5 us
    dot_general x1, matrix products, per_device(): jnp.einsum('ekt,ekd->td', pick, weighted, preferred_element_type=f32)  6.04 us
    unnamed x38, local copies, waits for them, and re-layouts  5.8 us
    all_to_all x1, waiting for transfers between devices, per_device(): lax.all_to_all(routed.astype(bf16).reshape(pools, req_dev, col_part), 'po...  4.65 us
  transfers between devices with their start and end apart: 11, of which 8 were waited for; matrix products, arithmetic and copies ran while one was open for 3% of the time, Pallas kernels for 0%

profile of v1, /device:TPU:0, one launch (start us, length us, event | category | flops | bytes accessed | tf_op | source)
XLA Modules:
  0.0 140.6 jit_solution(6983811257166136451)
XLA Ops:
  0.7 0.9 constant_dynamic-slice_fusion.8
  1.6 0.7 maximum_bitcast_fusion.1
  2.3 10.8 %all-gather.1 = bf16[8,10,1024]{2,1,0:T(8,128)(2,1)S(1)} all-gather(bf16[1,10,1024]{2,1,0:T(8,128)(2,1)S(1)} %maximum_bitcast_fusion.1), channel_id=1, replica_groups=mesh['head'=4,'pool'=8] {'pool'}, dimensions={0}, use_global_device_ids=true | all-gather | bytes 184320 | tf_op jit(solution)/shard_map/all_gather | solution.py:187
  13.1 0.7 broadcast_subtract_fusion
  13.9 1.0 select_reduce_fusion
  14.9 0.1 copy.68
  15.0 0.7 copy.114
  15.7 0.1 pad_add_fusion.place_ref
  15.8 2.3 %copy-done.1 = bf16[36,2,64,512]{3,2,1,0:T(8,128)(2,1)S(1)} copy-done((bf16[36,2,64,512]{3,2,1,0:T(8,128)(2,1)S(1)}, bf16[36,2,64,512]{3,2,1,0:T(8,128)(2,1)}, u32[]{:S(2)}) %copy-start.1) | copy-done | bytes 4718616
  18.1 3.3 %attention.1 = bf16[80,640]{1,0:T(8,128)(2,1)S(1)} custom-call(s32[2]{0:T(128)S(1)} %pad_add_fusion.place_ref, bf16[80,512]{1,0:T(8,128)(2,1)S(1)} %slice.54.query_ref, bf16[36,2,64,512]{3,2,1,0:T(8,128)(2,1)S(1)} %copy-done.1, bf16[80,36]{1,0:T(8,128)(2,1)S(1)} %clamp_convert_fusion.limit_ref, bf16[2,16,512]{2,1,0:T(8,128)(2,1)S(1)} %pad.12.fresh_ref), custom_call_target="tpu_custom_call" | custom-call | tf_op jit(solution)/shard_map/attention/pallas_call | solution.py:203
  21.4 10.5 %all-gather = bf16[640,640]{1,0:T(8,128)(2,1)S(1)} all-gather(bf16[80,640]{1,0:T(8,128)(2,1)S(1)} %attention.1), channel_id=2, replica_groups=mesh['head'=4,'pool'=8] {'pool'}, dimensions={0}, use_global_device_ids=true | all-gather | bytes 921600 | tf_op jit(solution)/shard_map/all_gather | solution.py:212
  32.0 1.5 %merge_project.1 = bf16[4,80,512]{2,1,0:T(8,128)(2,1)S(1)} custom-call(bf16[8,80,640]{2,1,0:T(8,128)(2,1)S(1)} %bitcast.77, bf16[512,2048]{1,0:T(8,128)(2,1)S(1)} %copy-done.2), custom_call_target="tpu_custom_call" | custom-call | tf_op jit(solution)/shard_map/merge_project/pallas_call | solution.py:213
  33.5 0.7 dynamic-slice_bitcast_fusion.5
  34.2 1.6 %collective-permute-start = (bf16[80,512]{1,0:T(8,128)(2,1)}, bf16[80,512]{1,0:T(8,128)(2,1)S(1)}, u32[]{:S(2)}, u32[]{:S(2)}) collective-permute-start(bf16[80,512]{1,0:T(8,128)(2,1)} %get-tuple-element.11), channel_id=1, source_target_pairs={{0,8},{8,0},{16,24},{24,16},{1,9},{9,1},{17,25},{25,17},{2,10},{10... | collective-permute-start | bytes 245768 | tf_op jit(solution)/shard_map/ppermute | solution.py:24
  35.8 2.6 %collective-permute-start.1 = (bf16[80,512]{1,0:T(8,128)(2,1)}, bf16[80,512]{1,0:T(8,128)(2,1)S(1)}, u32[]{:S(2)}, u32[]{:S(2)}) collective-permute-start(bf16[80,512]{1,0:T(8,128)(2,1)} %get-tuple-element.13), channel_id=1, source_target_pairs={{0,16},{8,24},{16,0},{24,8},{1,17},{9,25},{17,1},{25,9},{2,18},{10... | collective-permute-start | bytes 245768 | tf_op jit(solution)/shard_map/ppermute | solution.py:24
  38.4 0.2 collective-permute-start.2
  38.6 0.5 iota_add_fusion
  39.1 0.8 dynamic-slice_convert_fusion
  39.9 0.5 copy-done.14
  40.4 0.1 compare_reduce_fusion
  40.5 0.8 fusion.40
  41.4 0.6 iota_convert_fusion
  42.0 3.5 %collective-permute-done.1 = bf16[80,512]{1,0:T(8,128)(2,1)S(1)} collective-permute-done((bf16[80,512]{1,0:T(8,128)(2,1)}, bf16[80,512]{1,0:T(8,128)(2,1)S(1)}, u32[]{:S(2)}, u32[]{:S(2)}) %collective-permute-start.1) | collective-permute-done | bytes 81952 | tf_op jit(solution)/shard_map/ppermute | solution.py:24
  45.5 0.6 copy-done.7
  46.1 1.0 multiply_convert_fusion
  47.1 0.7 copy-done.5
  47.8 0.1 multiply_reduce_fusion
  47.9 0.1 copy.70
  48.1 0.9 convolution_convert_fusion.1
  49.0 13.6 %fusion.4 = bf16[8,16,2,1408]{3,1,2,0:T(8,128)(2,1)S(1)} fusion(bf16[8,512,2,1408]{3,2,1,0:T(2,128)(2,1)} %param.26, bf16[8,16,640]{2,1,0:T(8,128)(2,1)S(1)} %convolution_convert_fusion.1), kind=kOutput, calls=%fused_computation.4 | convolution fusion | flops 369459200 | bytes 23920640 | tf_op jit(solution)/shard_map/ekd,edcf->ekcf/dot_general | solution.py:247
  62.6 1.4 %copy.72 = bf16[8,16,2,1408]{3,2,1,0:T(2,128)(2,1)} copy(bf16[8,16,2,1408]{3,1,2,0:T(8,128)(2,1)S(1)} %fusion.4) | data formatting | bytes 1441792 | tf_op jit(solution)/shard_map/convert_element_type | solution.py:249
  64.0 3.0 %concatenate.40 = bf16[4,32,2816]{2,1,0:T(8,128)(2,1)} reshape(bf16[8,16,2,1408]{3,2,1,0:T(2,128)(2,1)} %copy.72) | data formatting | bytes 1441792 | tf_op jit(solution)/shard_map/concatenate | solution.py:254
  67.0 0.5 fusion.7
  67.7 0.1 dynamic-slice.1
  67.9 1.2 pad_maximum_fusion
  69.1 0.1 dynamic-slice_bitcast_fusion.2
  69.1 1.2 collective-permute-start.3
  70.4 2.1 %collective-permute-start.4 = (bf16[35,2944]{1,0:T(8,128)(2,1)S(1)}, bf16[35,2944]{1,0:T(8,128)(2,1)S(1)}, u32[]{:S(2)}, u32[]{:S(2)}) collective-permute-start(bf16[35,2944]{1,0:T(8,128)(2,1)S(1)} %get-tuple-element.6), channel_id=1, source_target_pairs={{0,16},{8,24},{16,0},{24,8},{1,17},{9,25},{17,1},{25,9},{2,18},{10... | collective-permute-start | bytes 618248 | tf_op jit(solution)/shard_map/ppermute | solution.py:24
  72.5 1.1 collective-permute-start.5
  73.6 5.9 %collective-permute-done.3 = bf16[35,2944]{1,0:T(8,128)(2,1)S(1)} collective-permute-done((bf16[35,2944]{1,0:T(8,128)(2,1)S(1)}, bf16[35,2944]{1,0:T(8,128)(2,1)S(1)}, u32[]{:S(2)}, u32[]{:S(2)}) %collective-permute-start.3) | collective-permute-done | bytes 206112 | tf_op jit(solution)/shard_map/ppermute | solution.py:24
  79.5 10.5 %collective-permute-done.4 = bf16[35,2944]{1,0:T(8,128)(2,1)S(1)} collective-permute-done((bf16[35,2944]{1,0:T(8,128)(2,1)S(1)}, bf16[35,2944]{1,0:T(8,128)(2,1)S(1)}, u32[]{:S(2)}, u32[]{:S(2)}) %collective-permute-start.4) | collective-permute-done | bytes 206112 | tf_op jit(solution)/shard_map/ppermute | solution.py:24
  90.0 0.1 fusion.15
  90.2 0.2 fusion.45
  90.3 0.2 fusion.25
  90.5 3.9 %collective-permute-start.6 = (bf16[1,35,1408]{2,1,0:T(8,128)(2,1)S(1)}, bf16[1,35,1408]{2,1,0:T(8,128)(2,1)S(1)}, u32[]{:S(2)}, u32[]{:S(2)}) collective-permute-start(bf16[1,35,1408]{2,1,0:T(8,128)(2,1)S(1)} %fusion.25), channel_id=1, source_target_pairs={{0,8},{8,0},{16,24},{24,16},{1,9},{9,1},{17,25},{25,17},{2,10},{10... | collective-permute-start | bytes 295688 | tf_op jit(solution)/shard_map/ppermute | solution.py:24
  94.4 2.8 %collective-permute-done.6 = bf16[1,35,1408]{2,1,0:T(8,128)(2,1)S(1)} collective-permute-done((bf16[1,35,1408]{2,1,0:T(8,128)(2,1)S(1)}, bf16[1,35,1408]{2,1,0:T(8,128)(2,1)S(1)}, u32[]{:S(2)}, u32[]{:S(2)}) %collective-permute-start.6) | collective-permute-done | bytes 98592 | tf_op jit(solution)/shard_map/ppermute | solution.py:24
  97.2 2.5 %collective-permute-start.7 = (bf16[2,35,1408]{2,1,0:T(8,128)(2,1)S(1)}, bf16[2,35,1408]{2,1,0:T(8,128)(2,1)S(1)}, u32[]{:S(2)}, u32[]{:S(2)}) collective-permute-start(bf16[2,35,1408]{2,1,0:T(8,128)(2,1)S(1)} %pad_maximum_fusion.5), channel_id=1, source_target_pairs={{0,16},{8,24},{16,0},{24,8},{1,17},{9,25},{17,1},{25,9},{2,18},{10... | collective-permute-start | bytes 591368 | tf_op jit(solution)/shard_map/ppermute | solution.py:24
  99.7 0.1 fusion.39
  99.8 0.8 select_reduce_fusion.1
  100.6 7.3 %collective-permute-done.7 = bf16[2,35,1408]{2,1,0:T(8,128)(2,1)S(1)} collective-permute-done((bf16[2,35,1408]{2,1,0:T(8,128)(2,1)S(1)}, bf16[2,35,1408]{2,1,0:T(8,128)(2,1)S(1)}, u32[]{:S(2)}, u32[]{:S(2)}) %collective-permute-start.7) | collective-permute-done | bytes 197152 | tf_op jit(solution)/shard_map/ppermute | solution.py:24
  107.9 0.1 pad_maximum_fusion.1
  108.0 0.6 copy-done.3
  108.7 6.0 %fusion.13 = bf16[80,512]{1,0:T(8,128)(2,1)S(1)} fusion(bf16[8,16,1408]{2,1,0:T(8,128)(2,1)S(1)} %bitcast.78, bf16[8,1408,512]{2,1,0:T(8,128)(2,1)} %param.27, f32[8,16]{1,0:T(8,128)} %select_reduce_fusion.1, f32[8,80]{1,0:T(8,128)} %copy-done.8, f32[16]{0:T(128)} %iota_convert_fusion, pred[8,80]{1,0:T(8,128)(4,1)} %bitcast.89), kind=kOutput, calls=%fused_computation.14 | convolution fusion | flops 195227648 | bytes 11980480 | tf_op jit(solution)/shard_map/ekt,ekd->td/dot_general | solution.py:277
  114.7 0.7 reshape.118
  115.4 3.4 %all-to-all-start = ((bf16[8,10,512]{2,1,0:T(8,128)(2,1)}), bf16[8,10,512]{2,1,0:T(8,128)(2,1)S(1)}, u32[]{:S(2)}, u32[]{:S(2)}) async-start(bf16[8,10,512]{2,1,0:T(8,128)(2,1)} %reshape.118), calls=%async_computation | async-start | bytes 262144 | tf_op jit(solution)/shard_map/all_to_all | solution.py:278
  118.8 0.8 pad_maximum_fusion.8
  119.6 4.6 %all-to-all-done = bf16[8,10,512]{2,1,0:T(8,128)(2,1)S(1)} async-done(((bf16[8,10,512]{2,1,0:T(8,128)(2,1)}), bf16[8,10,512]{2,1,0:T(8,128)(2,1)S(1)}, u32[]{:S(2)}, u32[]{:S(2)}) %all-to-all-start) | async-done | bytes 81952 | tf_op jit(solution)/shard_map/all_to_all | solution.py:278
  124.3 1.7 %add_bitcast_fusion = f32[1,10,512]{2,1,0:T(8,128)S(1)} fusion(f32[10,512]{1,0:T(8,128)S(1)} %convert_reduce_fusion, f32[80,512]{1,0:T(8,128)} %copy-done.5, s32[]{:T(128)S(6)} %select_n.58, bf16[1,1408,512]{2,1,0:T(8,128)(2,1)} %param.29, bf16[12,1408]{1,0:T(8,128)(2,1)S(1)} %reshape.116), kind=kOutput, calls=%fused_computation.68 | convolution fusion | flops 14428160 | bytes 1537028 | tf_op jit(solution)/shard_map/dot_general | solution.py:275
  126.0 3.9 %collective-permute-done.8 = f32[1,10,512]{2,1,0:T(8,128)S(1)} collective-permute-done((f32[1,10,512]{2,1,0:T(8,128)S(1)}, f32[1,10,512]{2,1,0:T(8,128)S(1)}, u32[]{:S(2)}, u32[]{:S(2)}) %collective-permute-start.8) | collective-permute-done | bytes 20512 | tf_op jit(solution)/shard_map/ppermute | solution.py:24
  129.9 0.1 collective-permute-start.9
  130.0 5.3 %collective-permute-done.9 = f32[2,10,512]{2,1,0:T(8,128)S(1)} collective-permute-done((f32[2,10,512]{2,1,0:T(8,128)S(1)}, f32[2,10,512]{2,1,0:T(8,128)S(1)}, u32[]{:S(2)}, u32[]{:S(2)}) %collective-permute-start.9) | collective-permute-done | bytes 40992 | tf_op jit(solution)/shard_map/ppermute | solution.py:24
  135.3 0.1 multiply_reduce_fusion.1
  135.6 0.6 convert_element_type.152
  136.2 4.4 %convolution_convert_fusion = bf16[10,1536]{1,0:T(8,128)(2,1)} fusion(bf16[2048,1536]{1,0:T(8,128)(2,1)} %param.31, f32[10,2048]{1,0:T(8,128)S(1)} %bitcast.80, f32[2048]{0:T(1024)S(1)} %convert_element_type.153, f32[10]{0:T(128)S(1)} %add_rsqrt_fusion), kind=kOutput, calls=%fused_computation.6 | convolution fusion | flops 62991360 | bytes 6412328 | tf_op jit(solution)/shard_map/dot_general | solution.py:287
  (63 shorter events, 0.8 us)
Async XLA Ops:
  0.6 66.4 %copy-start = (bf16[1,512,2,1408]{3,2,1,0:T(2,128)(2,1)S(1)}, bf16[1,512,2,1408]{3,2,1,0:T(2,128)(2,1)}, u32[]{:S(2)}) copy-start(bf16[1,512,2,1408]{3,2,1,0:T(2,128)(2,1)} %param.28) | copy-start | bytes 8650756
  15.8 2.3 %copy-start.1 = (bf16[36,2,64,512]{3,2,1,0:T(8,128)(2,1)S(1)}, bf16[36,2,64,512]{3,2,1,0:T(8,128)(2,1)}, u32[]{:S(2)}) copy-start(bf16[36,2,64,512]{3,2,1,0:T(8,128)(2,1)} %cache_ref.1) | copy-start | bytes 14155780
  18.1 13.8 %copy-start.2 = (bf16[512,2048]{1,0:T(8,128)(2,1)S(1)}, bf16[512,2048]{1,0:T(8,128)(2,1)}, u32[]{:S(2)}) copy-start(bf16[512,2048]{1,0:T(8,128)(2,1)} %weight_ref.1) | copy-start | bytes 6291460
  21.4 19.0 %copy-start.9 = (s32[80,6]{0,1:T(8,128)S(1)}, s32[80,6]{0,1:T(8,128)}, u32[]{:S(2)}) copy-start(s32[80,6]{0,1:T(8,128)} %param.24) | copy-start | bytes 5764
  34.2 7.8 %collective-permute-start = (bf16[80,512]{1,0:T(8,128)(2,1)}, bf16[80,512]{1,0:T(8,128)(2,1)S(1)}, u32[]{:S(2)}, u32[]{:S(2)}) collective-permute-start(bf16[80,512]{1,0:T(8,128)(2,1)} %get-tuple-element.11), channel_id=1, source_target_pairs={{0,8},{8,0},{16,24},{24,16},{1,9},{9,1},{17,25},{25,17},{2,10},{10... | collective-permute-start | bytes 245768 | tf_op jit(solution)/shard_map/ppermute | solution.py:24
  35.8 9.7 %collective-permute-start.1 = (bf16[80,512]{1,0:T(8,128)(2,1)}, bf16[80,512]{1,0:T(8,128)(2,1)S(1)}, u32[]{:S(2)}, u32[]{:S(2)}) collective-permute-start(bf16[80,512]{1,0:T(8,128)(2,1)} %get-tuple-element.13), channel_id=1, source_target_pairs={{0,16},{8,24},{16,0},{24,8},{1,17},{9,25},{17,1},{25,9},{2,18},{10... | collective-permute-start | bytes 245768 | tf_op jit(solution)/shard_map/ppermute | solution.py:24
  38.4 7.7 %collective-permute-start.2 = (bf16[80,512]{1,0:T(8,128)(2,1)}, bf16[80,512]{1,0:T(8,128)(2,1)}, u32[]{:S(2)}, u32[]{:S(2)}) collective-permute-start(bf16[80,512]{1,0:T(8,128)(2,1)} %get-tuple-element.12), channel_id=1, source_target_pairs={{0,24},{8,16},{16,8},{24,0},{1,25},{9,17},{17,9},{25,1},{2,26},{10... | collective-permute-start | bytes 245768 | tf_op jit(solution)/shard_map/ppermute | solution.py:24
  39.9 0.5 copy-start.14
  40.5 59.3 %copy-start.10 = (pred[80,8]{0,1:T(8,128)(4,1)}, pred[80,8]{0,1:T(8,128)(4,1)S(1)}, u32[]{:S(2)}) copy-start(pred[80,8]{0,1:T(8,128)(4,1)S(1)} %compare_reduce_fusion) | copy-start | bytes 1924
  41.4 58.4 %copy-start.8 = (f32[8,80]{1,0:T(8,128)}, f32[8,80]{1,0:T(8,128)S(1)}, u32[]{:S(2)}) copy-start(f32[8,80]{1,0:T(8,128)S(1)} %fusion.40) | copy-start | bytes 7684
  45.5 0.6 copy-start.7
  47.1 0.7 copy-start.5
  49.0 13.6 %copy-start.6 = (bf16[8,16,640]{2,1,0:T(8,128)(2,1)}, bf16[8,16,640]{2,1,0:T(8,128)(2,1)S(1)}, u32[]{:S(2)}) copy-start(bf16[8,16,640]{2,1,0:T(8,128)(2,1)S(1)} %convolution_convert_fusion.1) | copy-start | bytes 491524
  64.0 3.9 %slice-start = ((bf16[8,16,640]{2,1,0:T(8,128)(2,1)}), bf16[8,16,128]{2,1,0:T(8,128)(2,1)S(1)}, s32[]{:S(2)}) async-start(bf16[8,16,640]{2,1,0:T(8,128)(2,1)} %copy-done.6), calls=%async_computation.1 | async-start | bytes 65536 | tf_op jit(solution)/shard_map/slice | solution.py:255
  67.8 31.9 %copy-start.11 = (f32[80,6]{0,1:T(8,128)S(1)}, f32[80,6]{0,1:T(8,128)}, u32[]{:S(2)}) copy-start(f32[80,6]{0,1:T(8,128)} %param.25) | copy-start | bytes 5764
  67.8 31.9 %copy-start.15 = (s32[8]{0:T(128)S(1)}, s32[8]{0:T(128)}, u32[]{:S(2)}) copy-start(s32[8]{0:T(128)} %copy-done.14) | copy-start | bytes 100
  67.9 32.0 %copy-start.13 = (f32[16]{0:T(128)S(1)}, f32[16]{0:T(128)}, u32[]{:S(2)}) copy-start(f32[16]{0:T(128)} %iota_convert_fusion) | copy-start | bytes 196
  69.1 10.4 %collective-permute-start.3 = (bf16[35,2944]{1,0:T(8,128)(2,1)S(1)}, bf16[35,2944]{1,0:T(8,128)(2,1)S(1)}, u32[]{:S(2)}, u32[]{:S(2)}) collective-permute-start(bf16[35,2944]{1,0:T(8,128)(2,1)S(1)} %get-tuple-element.4), channel_id=1, source_target_pairs={{0,8},{8,0},{16,24},{24,16},{1,9},{9,1},{17,25},{25,17},{2,10},{10... | collective-permute-start | bytes 618248 | tf_op jit(solution)/shard_map/ppermute | solution.py:24
  70.4 19.7 %collective-permute-start.4 = (bf16[35,2944]{1,0:T(8,128)(2,1)S(1)}, bf16[35,2944]{1,0:T(8,128)(2,1)S(1)}, u32[]{:S(2)}, u32[]{:S(2)}) collective-permute-start(bf16[35,2944]{1,0:T(8,128)(2,1)S(1)} %get-tuple-element.6), channel_id=1, source_target_pairs={{0,16},{8,24},{16,0},{24,8},{1,17},{9,25},{17,1},{25,9},{2,18},{10... | collective-permute-start | bytes 618248 | tf_op jit(solution)/shard_map/ppermute | solution.py:24
  72.5 17.6 %collective-permute-start.5 = (bf16[35,2944]{1,0:T(8,128)(2,1)S(1)}, bf16[35,2944]{1,0:T(8,128)(2,1)S(1)}, u32[]{:S(2)}, u32[]{:S(2)}) collective-permute-start(bf16[35,2944]{1,0:T(8,128)(2,1)S(1)} %get-tuple-element.5), channel_id=1, source_target_pairs={{0,24},{8,16},{16,8},{24,0},{1,25},{9,17},{17,9},{25,1},{2,26},{10... | collective-permute-start | bytes 618248 | tf_op jit(solution)/shard_map/ppermute | solution.py:24
  90.5 6.6 %collective-permute-start.6 = (bf16[1,35,1408]{2,1,0:T(8,128)(2,1)S(1)}, bf16[1,35,1408]{2,1,0:T(8,128)(2,1)S(1)}, u32[]{:S(2)}, u32[]{:S(2)}) collective-permute-start(bf16[1,35,1408]{2,1,0:T(8,128)(2,1)S(1)} %fusion.25), channel_id=1, source_target_pairs={{0,8},{8,0},{16,24},{24,16},{1,9},{9,1},{17,25},{25,17},{2,10},{10... | collective-permute-start | bytes 295688 | tf_op jit(solution)/shard_map/ppermute | solution.py:24
  97.2 10.7 %collective-permute-start.7 = (bf16[2,35,1408]{2,1,0:T(8,128)(2,1)S(1)}, bf16[2,35,1408]{2,1,0:T(8,128)(2,1)S(1)}, u32[]{:S(2)}, u32[]{:S(2)}) collective-permute-start(bf16[2,35,1408]{2,1,0:T(8,128)(2,1)S(1)} %pad_maximum_fusion.5), channel_id=1, source_target_pairs={{0,16},{8,24},{16,0},{24,8},{1,17},{9,25},{17,1},{25,9},{2,18},{10... | collective-permute-start | bytes 591368 | tf_op jit(solution)/shard_map/ppermute | solution.py:24
  108.0 0.7 copy-start.3
  108.0 0.7 copy-start.4
  114.7 15.2 %copy-start.12 = (bf16[2048]{0:T(1024)(128)(2,1)S(1)}, bf16[2048]{0:T(1024)(128)(2,1)}, u32[]{:S(2)}) copy-start(bf16[2048]{0:T(1024)(128)(2,1)} %param.30) | copy-start | bytes 12292
  115.4 8.8 %all-to-all-start = ((bf16[8,10,512]{2,1,0:T(8,128)(2,1)}), bf16[8,10,512]{2,1,0:T(8,128)(2,1)S(1)}, u32[]{:S(2)}, u32[]{:S(2)}) async-start(bf16[8,10,512]{2,1,0:T(8,128)(2,1)} %reshape.118), calls=%async_computation | async-start | bytes 262144 | tf_op jit(solution)/shard_map/all_to_all | solution.py:278
  125.9 3.9 %collective-permute-start.8 = (f32[1,10,512]{2,1,0:T(8,128)S(1)}, f32[1,10,512]{2,1,0:T(8,128)S(1)}, u32[]{:S(2)}, u32[]{:S(2)}) collective-permute-start(f32[1,10,512]{2,1,0:T(8,128)S(1)} %add_bitcast_fusion), channel_id=1, source_target_pairs={{0,8},{8,0},{16,24},{24,16},{1,9},{9,1},{17,25},{25,17},{2,10},{10... | collective-permute-start | bytes 61448 | tf_op jit(solution)/shard_map/ppermute | solution.py:24
  129.9 5.4 %collective-permute-start.9 = (f32[2,10,512]{2,1,0:T(8,128)S(1)}, f32[2,10,512]{2,1,0:T(8,128)S(1)}, u32[]{:S(2)}, u32[]{:S(2)}) collective-permute-start(f32[2,10,512]{2,1,0:T(8,128)S(1)} %pad_maximum_fusion.7), channel_id=1, source_target_pairs={{0,16},{8,24},{16,0},{24,8},{1,17},{9,25},{17,1},{25,9},{2,18},{10... | collective-permute-start | bytes 122888 | tf_op jit(solution)/shard_map/ppermute | solution.py:24

commit v2 on v0

v2 whole, which is shorter than its diff:
```python
import functools
import math

import jax
import jax.numpy as jnp
from jax import lax
from jax.experimental import pallas as pl
from jax.experimental.pallas import tpu as pltpu
from jax.sharding import PartitionSpec as P

HD = 128
LANES = 128
TILE = 16
MOST = 2
SPLIT = 4


epsilon = 1e-06
floor_score = -1e30
bf16 = jnp.bfloat16
f32 = jnp.float32
over_rows = (((0,), (0,)), ((), ()))
VMEM = pl.BlockSpec(memory_space=pltpu.VMEM)
FAR = pl.BlockSpec(memory_space=pltpu.HBM)


def iota(shape, dim):
    return lax.broadcasted_iota(jnp.int32, shape, dim)


def one_hot(mask):
    return mask.astype(f32).astype(bf16)


def dot(left, right):
    return jnp.dot(left, right, preferred_element_type=f32)


def call(kernel, name, outs, args, scratch=(), copies=(), far=(), megabytes=4, moved=1e5):
    semaphores = [pltpu.SemaphoreType.DMA((count,)) for count in copies]
    return pl.pallas_call(
        kernel,
        out_shape=[jax.ShapeDtypeStruct(shape, dtype) for shape, dtype in outs],
        in_specs=[FAR if i in far else VMEM for i in range(len(args))],
        out_specs=[VMEM] * len(outs),
        scratch_shapes=[pltpu.VMEM(shape, dtype) for shape, dtype in scratch] + semaphores,
        compiler_params=pltpu.CompilerParams(vmem_limit_bytes=int(megabytes * 2**20)),
        cost_estimate=pl.CostEstimate(
            flops=1000, bytes_accessed=int(moved), transcendentals=0
        ),
        name=name,
    )(*args)


def swap(value, axis, distance):
    count = lax.axis_size(axis)
    return lax.ppermute(value, axis, [(i, i ^ distance) for i in range(count)])


def start_weights(distance, slots, weight_ref, out_ref, semaphores):
    count, depth = out_ref.shape[:2]
    part = weight_ref.shape[0] * slots // lax.axis_size("head")
    first = (lax.axis_index("head") ^ distance) * part // slots
    rows = depth // SPLIT
    copies = [
        pltpu.make_async_copy(
            weight_ref.at[first + i, pl.ds(k * rows, rows)],
            out_ref.at[i, pl.ds(k * rows, rows)],
            semaphores.at[i * SPLIT + k],
        )
        for i in range(count)
        for k in range(SPLIT)
    ]
    for copy in copies:
        copy.start()
    return copies


def start_all_weights(distances, slots, weight_ref, out_refs, semaphores):
    copies = []
    for place, (distance, out_ref) in enumerate(zip(distances, out_refs)):
        count = out_ref.shape[0] * SPLIT
        own = semaphores.at[pl.ds(place * count, count)]
        copies += start_weights(distance, slots, weight_ref, out_ref, own)
    return copies


def setup_kernel(
    table_ref,
    length_ref,
    given_query_ref,
    given_fresh_ref,
    given_residual_ref,
    cache_ref,
    bias_ref,
    query_ref,
    fresh_ref,
    residual_ref,
):
    query_ref[...] = given_query_ref[...]
    fresh_ref[...] = given_fresh_ref[...]
    lane_width = residual_ref.shape[1]
    start = pl.multiple_of(lax.axis_index("head") * lane_width, LANES)
    residual_ref[...] = given_residual_ref[:, pl.ds(start, lane_width)]
    pool_idx = lax.axis_index("pool")
    blocks, _, block_len, _ = cache_ref.shape
    list_len, req_total = table_ref.shape
    tokens = blocks * block_len
    table = table_ref[...] - pool_idx * blocks
    left = length_ref[...] - iota((list_len, req_total), 0) * block_len
    block_row = iota((LANES, req_total), 0)
    limits = jnp.zeros((LANES, req_total), f32)
    for block in range(blocks):
        found = jnp.sum(jnp.where(table == block, left, 0).astype(f32), axis=0, keepdims=True)
        limits = jnp.where(block_row == block, found, limits)
    limits = jnp.clip(limits, 0.0, float(block_len)).astype(bf16)
    expand = iota((LANES, tokens), 1) // block_len == iota((LANES, tokens), 0)
    limits = lax.dot_general(limits, one_hot(expand), over_rows, preferred_element_type=f32)
    within = lax.rem(iota((1, tokens), 1), block_len).astype(f32)
    bias_ref[...] = jnp.where(within < limits, 0.0, floor_score)


def attention_kernel(
    order,
    cache_ref,
    bias_ref,
    fresh_ref,
    residual_ref,
    *refs,
):
    *query_refs, out_ref, queries_ref = refs
    blocks, _, block_len, _ = cache_ref.shape
    pool_idx = lax.axis_index("pool")
    pools, req_dev, lane_width = queries_ref.shape
    req_total = pools * req_dev
    tokens = blocks * block_len
    scale = 1.0 / math.sqrt(HD)
    bias = bias_ref[...]
    pieces = [ref[i] for ref in query_refs for i in range(ref.shape[0])]
    for distance, piece in zip(order, pieces):
        queries_ref[pool_idx ^ distance] = piece.astype(f32)
    queries = jnp.concatenate([queries_ref[i] for i in range(pools)], axis=0).astype(bf16)
    own = iota((req_total, req_dev), 0) == iota((req_total, req_dev), 1) + pool_idx * req_dev
    lane = iota((req_total, LANES), 1)
    side = jnp.zeros((req_total, LANES), f32)
    heads = lane_width // HD
    contract = (((1,), (1,)), ((), ()))
    for head in range(heads):
        columns = slice(head * HD, (head + 1) * HD)
        query = queries[:, columns]
        keys = cache_ref[:, 0, :, columns].reshape(tokens, HD)
        scores = lax.dot_general(query, keys, contract, preferred_element_type=f32) * scale
        scores = jnp.where(bias < 0.0, floor_score, scores)
        new_scores = (
            lax.dot_general(query, fresh_ref[:, 0, columns], contract, preferred_element_type=f32)
            * scale
        )
        new_scores = jnp.where(own, new_scores, floor_score)
        top = jnp.maximum(
            jnp.max(scores, axis=1, keepdims=True), jnp.max(new_scores, axis=1, keepdims=True)
        )
        top = top.astype(bf16).astype(f32)
        weights = jnp.where(bias < 0.0, 0.0, jnp.exp(scores - top))
        new_weights = jnp.where(own, jnp.exp(new_scores - top), 0.0)
        total = jnp.sum(weights, axis=1, keepdims=True) + jnp.sum(
            new_weights, axis=1, keepdims=True
        )
        values = cache_ref[:, 1, :, columns].reshape(tokens, HD)
        mixed = dot(weights.astype(bf16), values) + dot(
            new_weights.astype(bf16), fresh_ref[:, 1, columns]
        )
        inverse = jnp.where(total > 0.0, 1.0 / jnp.where(total > 0.0, total, 1.0), 0.0)
        out_ref[:req_total, columns] = (mixed * inverse).astype(bf16)
        coarse = total.astype(bf16).astype(f32)
        side = jnp.where(lane == head, top, side)
        side = jnp.where(lane == heads + head, coarse, side)
        side = jnp.where(lane == 2 * heads + head, total - coarse, side)
    out_ref[:req_total, lane_width:] = side.astype(bf16)
    out_ref[req_total:, :] = jnp.zeros((out_ref.shape[0] - req_total, out_ref.shape[1]), bf16)
    out_ref[req_total : req_total + req_dev, :lane_width] = residual_ref[...]


def merge_kernel(req_dev, parts_ref, weight_ref, *refs):
    out_refs, attended_ref = refs[:-1], refs[-1]
    count, _, packed = parts_ref.shape
    req_total, col_part = out_refs[0].shape
    lane_width = packed - LANES
    heads = lane_width // HD
    me = lax.axis_index("head")
    lane = iota((req_total, LANES), 1)
    sides = [parts_ref[i, :req_total, lane_width:].astype(f32) for i in range(count)]

    def column(side, place):
        return jnp.sum(jnp.where(lane == place, side, 0.0), axis=1, keepdims=True)

    for head in range(heads):
        columns = slice(head * HD, (head + 1) * HD)
        tops = [column(side, head) for side in sides]
        totals = [column(side, heads + head) + column(side, 2 * heads + head) for side in sides]
        top = functools.reduce(jnp.maximum, tops)
        shares = [total * jnp.exp(part - top) for part, total in zip(tops, totals)]
        denominator = functools.reduce(jnp.add, shares)
        mixed = functools.reduce(
            jnp.add,
            [shares[i] * parts_ref[i, :req_total, columns].astype(f32) for i in range(count)],
        )
        attended_ref[:, columns] = (mixed / denominator).astype(bf16)
    for distance, out_ref in enumerate(out_refs):
        start = pl.multiple_of((me ^ distance) * col_part, LANES)
        projected = dot(attended_ref[...], weight_ref[:, pl.ds(start, col_part)])
        out_ref[...] = projected.astype(out_ref.dtype)
    for i in range(count):
        rows = slice(i * req_dev, (i + 1) * req_dev)
        residual = parts_ref[i, req_total : req_total + req_dev, :col_part].astype(f32)
        out_refs[0][rows, :] = out_refs[0][rows, :] + residual


def routing_kernel(
    distances,
    slots,
    req_dev,
    routes_ref,
    gates_ref,
    far_weight_ref,
    pick_ref,
    coarse_ref,
    fine_ref,
    spread_ref,
    *refs,
):
    weight_refs, semaphores = refs[:-1], refs[-1]
    fetched = start_all_weights(distances, slots, far_weight_ref, weight_refs, semaphores)
    top_k, req_total = routes_ref.shape
    slot_total = coarse_ref.shape[0]
    extra = pick_ref.shape[0] - slot_total
    pool_idx = lax.axis_index("pool")
    expert = iota((slot_total, req_total), 0) // slots + pool_idx * (slot_total // slots)
    rank = lax.rem(iota((slot_total, req_total), 0), slots).astype(f32)
    chosen = jnp.zeros((slot_total, req_total), f32)
    gate = jnp.zeros((slot_total, req_total), f32)
    for k in range(top_k):
        match = routes_ref[k : k + 1, :] == expert
        chosen = jnp.where(match, 1.0, chosen)
        gate = jnp.where(match, gates_ref[k : k + 1, :], gate)
    earlier = iota((req_total, req_total), 0) < iota((req_total, req_total), 1)
    place = dot(chosen.astype(bf16), one_hot(earlier))
    pick = jnp.where(place == rank, chosen, 0.0)
    pick_ref[:slot_total, :] = pick.astype(bf16)
    own_place = iota((extra, req_total), 0)
    own = iota((extra, req_total), 1) == own_place + pool_idx * req_dev
    pick_ref[slot_total:, :] = one_hot(jnp.logical_and(own, own_place < req_dev))
    gate = gate * pick
    coarse = gate.astype(bf16)
    coarse_ref[...] = coarse
    fine_ref[...] = (gate - coarse.astype(f32)).astype(bf16)
    spread_ref[...] = one_hot(iota(spread_ref.shape, 1) == 2 * iota(spread_ref.shape, 0))
    for copy in fetched:
        copy.wait()


def gain_columns(gain_ref, part, count):
    gains = gain_ref[...].astype(f32)
    rows = iota(gains.shape, 0)
    first = part * (count // LANES)
    return jnp.concatenate(
        [
            jnp.sum(jnp.where(rows == first + i, gains, 0.0), axis=0, keepdims=True)
            for i in range(count // LANES)
        ],
        axis=1,
    )


def prepare_kernel(req_dev, gain_ref, pick_ref, spread_ref, own_sum_ref, *refs):
    received, (gate_ref, up_ref, side_ref, after_ref, all_ref) = refs[:-5], refs[-5:]
    req_total, col_part = own_sum_ref.shape
    after = own_sum_ref[...]
    for part in received:
        after = after + part[...].astype(f32)
    for place in range(all_ref.shape[0]):
        all_ref[place] = after[place * req_dev : (place + 1) * req_dev]
    after_ref[...] = all_ref[lax.axis_index("pool")]
    gains = gain_columns(gain_ref, lax.axis_index("head"), col_part)
    scaled = (after * gains).astype(bf16)
    squares = jnp.sum(after * after, axis=1, keepdims=True)
    coarse = squares.astype(bf16).astype(f32)
    lane = iota((req_total, LANES), 1)
    side = jnp.where(lane == 0, coarse, jnp.where(lane == 1, squares - coarse, 0.0))
    pick = pick_ref[...]
    picked = dot(pick, scaled).astype(bf16)
    side_ref[...] = dot(pick, side.astype(bf16)).astype(bf16)
    spread = dot(picked, spread_ref[...])
    gate_ref[...] = spread.astype(bf16)
    up_ref[...] = pltpu.roll(spread, 1, 1).astype(bf16)


def gate_up(lhs, weight, out_ref, rows, side):
    count, ffe = lhs.shape[0] // 2, weight.shape[1]
    sums = dot(lhs, weight)
    out_ref[rows, :ffe] = sums[:count].astype(out_ref.dtype)
    out_ref[rows, ffe : 2 * ffe] = sums[count:].astype(out_ref.dtype)
    out_ref[rows, 2 * ffe :] = side.astype(out_ref.dtype)


def expert_kernel(distance, slots, gate_ref, up_ref, side_ref, weight_ref, *refs):
    refs = list(refs)
    head_devs = lax.axis_size("head")
    if distance == 0:
        near_ref, semaphores = refs[-2:]
        refs = refs[:-2]
        fetched = start_weights(distance, slots, weight_ref, near_ref, semaphores)
        weight_ref = near_ref
        for copy in fetched:
            copy.wait()
    _, depth, _, ffe = weight_ref.shape
    target = lax.axis_index("head") ^ distance
    if distance == head_devs - 1:
        shared_weight_ref, out_ref, shared_ref, all_ref = refs
        extra, share = all_ref.shape[0], shared_ref.shape[1]
        first_extra = gate_ref.shape[0] - extra
        lhs = jnp.concatenate([gate_ref[first_extra:, :], up_ref[first_extra:, :]], axis=0)
        gate_up(
            lhs,
            shared_weight_ref[0].reshape(2 * depth, ffe),
            all_ref,
            slice(0, extra),
            side_ref[first_extra:, :],
        )
        for place in range(head_devs):
            shared_ref[place] = all_ref[place * share : (place + 1) * share, :]
    else:
        shared_ref, out_ref = refs[0], refs[-1]
        share = shared_ref.shape[1]
    part = out_ref.shape[0] - share
    each = min(slots, part)
    for i in range(part // each):
        rows = pl.ds(pl.multiple_of(target * part + i * each, TILE), each)
        lhs = jnp.concatenate([gate_ref[rows, :], up_ref[rows, :]], axis=0)
        weight = weight_ref[i].reshape(2 * depth, ffe)
        gate_up(lhs, weight, out_ref, slice(i * each, (i + 1) * each), side_ref[rows, :])
    out_ref[part:, :] = shared_ref[target].astype(bf16)


def add_kernel(own_ref, received_ref, out_ref):
    out_ref[...] = (own_ref[...].astype(f32) + received_ref[...].astype(f32)).astype(bf16)


def hidden_kernel(width, *refs):
    parts, out_ref = refs[:-1], refs[-1]
    ffe = out_ref.shape[1]

    def total(columns):
        return functools.reduce(jnp.add, [part[:, columns].astype(f32) for part in parts])

    side = total(slice(2 * ffe, 2 * ffe + LANES))
    row_scale = lax.rsqrt((side[:, 0:1] + side[:, 1:2]) / width + epsilon)
    gates = total(slice(0, ffe)) * row_scale
    ups = total(slice(ffe, 2 * ffe)) * row_scale
    out_ref[...] = (gates / (1.0 + jnp.exp(-gates)) * ups).astype(bf16)


def down_rows(distance, slots, hidden_ref, weight_ref):
    part = weight_ref.shape[0] * slots // lax.axis_size("head")
    each = min(slots, part)
    first = (lax.axis_index("head") ^ distance) * part
    return [
        dot(hidden_ref[i * each : (i + 1) * each, :], weight_ref[(first + i * each) // slots])
        for i in range(part // each)
    ]


def down_kernel(distance, slots, hidden_ref, weight_ref, out_ref):
    out_ref[...] = jnp.concatenate(down_rows(distance, slots, hidden_ref, weight_ref), axis=0)


def combine_kernel(distance, slots, coarse_ref, fine_ref, weight_ref, shared_weight_ref, *refs):
    head_devs = lax.axis_size("head")
    hidden_refs, done_refs = refs[:head_devs], refs[head_devs : 2 * head_devs - 1]
    routed_ref, shared_ref, rows_ref = refs[2 * head_devs - 1 :]
    me = lax.axis_index("head")
    part = weight_ref.shape[0] * slots // head_devs
    last = jnp.concatenate(
        down_rows(distance, slots, hidden_refs[distance], weight_ref), axis=0
    )
    done = {j: ref for j, ref in zip([j for j in range(head_devs) if j != distance], done_refs)}
    for j in range(head_devs):
        rows = pl.ds(pl.multiple_of((me ^ j) * part, TILE), part)
        rows_ref[rows, :] = last if j == distance else done[j][...]
    values = rows_ref[...]
    coarse = values.astype(bf16)
    fine = (values - coarse.astype(f32)).astype(bf16)
    def weighted(gates, rows):
        return lax.dot_general(gates, rows, over_rows, preferred_element_type=f32)

    gates = coarse_ref[...]
    routed = weighted(gates, coarse) + (weighted(gates, fine) + weighted(fine_ref[...], coarse))
    pools, req_dev, _ = routed_ref.shape
    for place in range(pools):
        routed_ref[place] = routed[place * req_dev : (place + 1) * req_dev].astype(bf16)
    share = shared_ref.shape[1]
    shared = jnp.concatenate([ref[part:, :].astype(f32) for ref in hidden_refs], axis=0)
    shared = dot(shared.astype(bf16), shared_weight_ref[0])
    for j in range(head_devs):
        shared_ref[me ^ j] = shared[j * share : (j + 1) * share]


def block_kernel(pieces_ref, shared_ref, after_ref, out_ref):
    req_dev = after_ref.shape[0]
    shared = jnp.concatenate([shared_ref[i] for i in range(shared_ref.shape[0])], axis=0)
    total = after_ref[...] + shared[:req_dev]
    for place in range(pieces_ref.shape[0]):
        total = total + pieces_ref[place].astype(f32)
    out_ref[...] = total.astype(bf16)


def join_kernel(*refs):
    place = 0
    for ref in refs[:-1]:
        count = ref.shape[0]
        refs[-1][place : place + count] = ref[...]
        place += count


def project_kernel(gain_ref, weight_ref, *refs):
    block_refs, (hidden_ref, out_ref) = refs[:-2], refs[-2:]
    me = lax.axis_index("head")
    blocks = [ref[...].astype(f32) for ref in block_refs]
    req_dev, col_part = blocks[0].shape
    width = hidden_ref.shape[1]
    squares = [jnp.sum(block * block, axis=1, keepdims=True) for block in blocks]
    row_scale = lax.rsqrt(functools.reduce(jnp.add, squares) / width + epsilon)
    total = jnp.zeros(out_ref.shape, f32)
    for distance, block in enumerate(blocks):
        start = pl.multiple_of((me ^ distance) * col_part, LANES)
        columns = pl.ds(start, col_part)
        hidden_ref[:, columns] = block.astype(bf16)
        gains = gain_columns(gain_ref, me ^ distance, col_part)
        normed = (block * row_scale * gains).astype(bf16)
        total = total + dot(normed, weight_ref[columns, :])
    out_ref[...] = total.astype(bf16)


def per_device(
    queries,
    fresh_pair,
    cache_blocks,
    block_table,
    lengths,
    residual,
    w_output,
    norm_gain,
    routes,
    route_gates,
    w_gate_up,
    w_down,
    shared_gate_up,
    shared_down,
    next_gain,
    w_query_key_value,
):
    pools = lax.axis_size("pool")
    head_devs = lax.axis_size("head")
    req_dev, lane_width = queries.shape
    req_total = block_table.shape[0]
    blk_count, _, block_len, _ = cache_blocks.shape
    exp_dev, col_part, _, ffe = w_gate_up.shape
    width = residual.shape[1]
    slots = min(MOST * pools, req_total)
    slot_total = exp_dev * slots
    extra = -(-req_dev // TILE) * TILE
    padded = -(-req_dev // TILE) * TILE + req_total
    small = pools <= 8
    distances = list(range(1, head_devs))
    piece_experts = max(1, exp_dev // head_devs)
    fetch_shape = ((piece_experts, col_part, 2, ffe), bf16)
    fetched = list(reversed(range(1, head_devs)))

    queries = queries[None]
    bias, own_queries, fresh, residual_part = call(
        setup_kernel,
        "setup",
        [
            ((req_total, blk_count * block_len), f32),
            (queries.shape, bf16),
            (fresh_pair.shape, bf16),
            ((req_dev, col_part), bf16),
        ],
        [block_table.T, lengths[None, :], queries, fresh_pair, residual, cache_blocks],
        megabytes=4 + 16 * req_total * blk_count * block_len / 2**20,
    )
    if small:
        order = list(range(0, pools, 2))
        pieces = [own_queries] + [swap(queries, "pool", d) for d in order[1:]]
        (joined,) = call(
            join_kernel, "join_queries", [((len(order), req_dev, lane_width), bf16)], pieces
        )
        pieces = [joined, swap(joined, "pool", 1)]
        order = order + [d + 1 for d in order]
    else:
        step = 1
        order, pieces = [0], [queries]
        while step < pools:
            whole = queries if step == 1 else jnp.concatenate(pieces, axis=0)
            pieces.append(swap(whole, "pool", step))
            order += [d ^ step for d in order]
            step *= 2
    (partial,) = call(
        functools.partial(attention_kernel, order),
        "attention",
        [((padded, lane_width + LANES), bf16)],
        [cache_blocks, bias, fresh, residual_part] + pieces,
        scratch=[((pools, req_dev, lane_width), f32)],
        megabytes=4 + 32 * req_total * blk_count * block_len / 2**20,
    )
    parts = lax.all_gather(partial, "pool", axis=0)
    sums = call(
        functools.partial(merge_kernel, req_dev),
        "merge_project",
        [((req_total, col_part), f32)] + [((req_total, col_part), bf16)] * (head_devs - 1),
        [parts, w_output],
        scratch=[((req_total, lane_width), bf16)],
        megabytes=5 + 12 * pools * req_total * LANES / 2**20,
    )
    pick, gate_coarse, gate_fine, spread, *weights = call(
        functools.partial(routing_kernel, fetched, slots, req_dev),
        "routing",
        [
            ((slot_total + extra, req_total), bf16),
            ((slot_total, req_total), bf16),
            ((slot_total, req_total), bf16),
            ((col_part, 2 * col_part), bf16),
        ]
        + [fetch_shape] * len(fetched),
        [routes.T, route_gates.T, w_gate_up],
        far=[2],
        copies=[len(fetched) * piece_experts * SPLIT],
        megabytes=24,
        moved=2e7,
    )
    weights = dict(zip(fetched, weights))
    received = {d: swap(sums[d], "head", d) for d in reversed(distances)}
    gate_rows, up_rows, side, own_after = call(
        functools.partial(prepare_kernel, req_dev),
        "prepare",
        [
            ((slot_total + extra, 2 * col_part), bf16),
            ((slot_total + extra, 2 * col_part), bf16),
            ((slot_total + extra, LANES), bf16),
            ((req_dev, col_part), f32),
        ],
        [norm_gain.reshape(-1, LANES), pick, spread, sums[0]] + [received[d] for d in distances],
        scratch=[((pools, req_dev, col_part), f32)],
        megabytes=6,
    )

    piece = slot_total // head_devs + extra // head_devs
    piece_shape = ((piece, 2 * ffe + LANES), bf16)
    shared_shape = ((head_devs, extra // head_devs, 2 * ffe + LANES), f32)
    shared_rows = None
    last = head_devs - 1

    def experts(distance, after=()):
        nonlocal shared_rows
        args = [gate_rows, up_rows, side, weights.get(distance, w_gate_up)]
        outs, scratch, copies, far = [piece_shape], [], [], []
        if distance == last:
            args, outs = args + [shared_gate_up], outs + [shared_shape]
            scratch = [((extra, 2 * ffe + LANES), f32)]
        else:
            args = args + [shared_rows] + list(after)
        if distance == 0:
            scratch, copies, far = [fetch_shape], [piece_experts * SPLIT], [3]
        mine, *shared = call(
            functools.partial(expert_kernel, distance, slots),
            f"experts_{distance}",
            outs,
            args,
            scratch=scratch,
            copies=copies,
            far=far,
            megabytes=32 if distance == 0 else 10,
        )
        if shared:
            (shared_rows,) = shared
        return mine

    if head_devs == 4:
        near = swap(experts(3), "head", 1)
        own_near = experts(1)
        near_own = swap(own_near, "head", 1)
        (pair,) = call(add_kernel, "add_pair", [piece_shape], [experts(2, [own_near]), near])
        parts = [experts(0, [pair]), swap(pair, "head", 2), near_own]
    else:
        parts = [swap(experts(d), "head", d) for d in reversed(range(1, head_devs))]
        parts = [experts(0)] + parts
    (hidden,) = call(
        functools.partial(hidden_kernel, width), "hidden", [((piece, ffe), bf16)], parts
    )
    hiddens = {0: hidden}
    for d in distances:
        hiddens[d] = swap(hidden, "head", d)
    done = []
    for d in range(last):
        done += call(
            functools.partial(down_kernel, d, slots),
            f"down_{d}",
            [((slot_total // head_devs, col_part), f32)],
            [hiddens[d], w_down],
            megabytes=6,
            )
    routed, shared_out = call(
        functools.partial(combine_kernel, last, slots),
        "combine",
        [((pools, req_dev, col_part), bf16), ((head_devs, extra // head_devs, col_part), f32)],
        [gate_coarse, gate_fine, w_down, shared_down]
        + [hiddens[d] for d in range(head_devs)]
        + done,
        scratch=[((slot_total, col_part), f32)],
        megabytes=6,
    )
    pieces = lax.all_to_all(routed, "pool", 0, 0)
    (block,) = call(
        block_kernel,
        "block",
        [((req_dev, col_part), bf16)],
        [pieces, shared_out, own_after],
        megabytes=4,
    )
    blocks = [block] + [swap(block, "head", d) for d in distances]
    next_hidden, next_projection = call(
        project_kernel,
        "project",
        [((req_dev, width), bf16), ((req_dev, w_query_key_value.shape[1]), bf16)],
        [next_gain.reshape(-1, LANES), w_query_key_value] + blocks,
        megabytes=6,
    )
    return (next_hidden, next_projection)


def solution(mesh):
    in_specs = (
        P("pool", "head"),
        P("pool", None, "head"),
        P("pool", None, None, "head"),
        P(),
        P(),
        P("pool", None),
        P("head", None),
        P(),
        P(),
        P(),
        P("pool", "head", None, None),
        P("pool", None, "head"),
        P(None, "head", None, None),
        P(None, None, "head"),
        P(),
        P(None, "head"),
    )
    out_specs = (P("pool", None), P("pool", "head"))
    return jax.shard_map(
        per_device, mesh=mesh, in_specs=in_specs, out_specs=out_specs, check_vma=False
    )
```

time: 356 us -> 92.5 us (0.26)
  waiting for transfers between devices: 169 us -> 16.7 us
  blocking collectives: 88.8 us -> 19.5 us
  matrix products: 39.8 us -> 0 us
  Pallas kernels: 0 us -> 25.7 us
  local copies, waits for them, and re-layouts: 29.9 us -> 6.54 us
  starting transfers between devices: 0.12 us -> 22.8 us
  between operations: 14.7 us -> 0.87 us
  other arithmetic: 11.8 us -> 0.01 us
    psum x1 -> x0, waiting for transfers between devices: 130 us -> none  [per_device(): preact = lax.psum(preact.astype(jnp.bfloat16), 'head').astype(jnp.float32)]
    dot_general x11 -> x0, matrix products: 39.8 us -> none  [the longest x1 15.7 us: per_device(): jnp.einsum('nd,edcf->necf', row_part, w_gate_up, preferred_element_type=j...]
    all_gather x5 -> x1, blocking collectives: 51.2 us -> 11.4 us  [per_device(): parts = lax.all_gather(partial, 'pool', axis=0)]
    psum x2 -> x0, blocking collectives: 37.6 us -> none  [the longest x1 19.6 us: per_device(): lax.psum(projected.astype(jnp.bfloat16), 'head').astype(jnp.float32)]
    unnamed x4 -> x0, waiting for transfers between devices: 31.2 us -> none
    pallas_call x0 -> x18, Pallas kernels: none -> 25.7 us  [call(): pl.pallas_call(kernel, out_shape=[jax.ShapeDtypeStruct(shape, dtype) for...]
    ppermute x0 -> x16, starting transfers between devices: none -> 22.8 us  [swap(): return lax.ppermute(value, axis, [(i, i ^ distance) for i in range(count)])]
    ppermute x0 -> x16, waiting for transfers between devices: none -> 16.7 us  [swap(): return lax.ppermute(value, axis, [(i, i ^ distance) for i in range(count)])]
  transfers between devices with their start and end apart: 3 -> 16, of which waited for: 3 -> 9; matrix products, arithmetic and copies ran while one was open for 1% -> 0% of each run, Pallas kernels for 0% -> 17%
where the time goes in v2:
time: 92.5 us; the launch traced here: 92 us
  Pallas kernels  25.7 us (28%)
  starting transfers between devices  22.8 us (25%)
  blocking collectives  19.5 us (21%)
  waiting for transfers between devices  16.7 us (18%)
  local copies, waits for them, and re-layouts  6.54 us (7%)
    pallas_call x18, Pallas kernels, call(): pl.pallas_call(kernel, out_shape=[jax.ShapeDtypeStruct(shape, dtype) for...  25.7 us
    ppermute x16, starting transfers between devices, swap(): return lax.ppermute(value, axis, [(i, i ^ distance) for i in range(count)])  22.8 us
    ppermute x16, waiting for transfers between devices, swap(): return lax.ppermute(value, axis, [(i, i ^ distance) for i in range(count)])  16.7 us
    all_gather x1, blocking collectives, per_device(): parts = lax.all_gather(partial, 'pool', axis=0)  11.4 us
    all_to_all x1, blocking collectives, per_device(): pieces = lax.all_to_all(routed, 'pool', 0, 0)  8.11 us
    unnamed x38, local copies, waits for them, and re-layouts  6.54 us
  transfers between devices with their start and end apart: 16, of which 9 were waited for; matrix products, arithmetic and copies ran while one was open for 0% of the time, Pallas kernels for 17%

profile of v2, /device:TPU:0, one launch (start us, length us, event | category | flops | bytes accessed | tf_op | source)
XLA Modules:
  0.0 92.0 jit_solution(1936562754021328932)
XLA Ops:
  0.6 4.0 %collective-permute-start.2 = (bf16[1,10,512]{2,1,0:T(8,128)(2,1)}, bf16[1,10,512]{2,1,0:T(8,128)(2,1)S(1)}, u32[]{:S(2)}, u32[]{:S(2)}) collective-permute-start(bf16[1,10,512]{2,1,0:T(8,128)(2,1)} %bitcast.14), channel_id=1, source_target_pairs={{0,6},{1,7},{2,4},{3,5},{4,2},{5,3},{6,0},{7,1},{8,14},{9,15},{10,... | collective-permute-start | bytes 30728 | tf_op jit(solution)/shard_map/ppermute | solution.py:57
  4.6 0.5 collective-permute-start.1
  5.1 0.1 collective-permute-start
  5.2 2.3 %copy-done = bf16[36,2,64,512]{3,2,1,0:T(8,128)(2,1)S(1)} copy-done((bf16[36,2,64,512]{3,2,1,0:T(8,128)(2,1)S(1)}, bf16[36,2,64,512]{3,2,1,0:T(8,128)(2,1)}, u32[]{:S(2)}) %copy-start) | copy-done | bytes 4718616
  7.6 0.8 copy-done.5
  8.4 0.8 copy-done.6
  9.2 0.7 copy-done.7
  9.9 0.7 copy-done.8
  10.6 0.7 copy-done.13
  11.3 0.5 setup.1
  11.8 0.0 copy-start.11
  11.8 0.0 copy-start.12
  11.8 0.0 collective-permute-done.2.refs_3_
  11.8 0.0 collective-permute-done.1.refs_2_
  11.8 0.0 collective-permute-done.refs_1_
  11.8 0.1 collective-permute-start.3
  11.9 1.2 %collective-permute-done.3.refs_1_ = bf16[4,10,512]{2,1,0:T(8,128)(2,1)S(1)} collective-permute-done((bf16[4,10,512]{2,1,0:T(8,128)(2,1)S(1)}, bf16[4,10,512]{2,1,0:T(8,128)(2,1)S(1)}, u32[]{:S(2)}, u32[]{:S(2)}) %collective-permute-start.3) | collective-permute-done | bytes 40992 | tf_op jit(solution)/shard_map/ppermute | solution.py:57
  13.2 0.4 copy-done.1
  13.6 2.9 %attention.1 = bf16[96,640]{1,0:T(8,128)(2,1)S(1)} custom-call(bf16[36,2,64,512]{3,2,1,0:T(8,128)(2,1)S(1)} %copy-done.1, f32[80,2304]{1,0:T(8,128)S(1)} %get-tuple-element.29.bias_ref, bf16[10,2,512]{2,1,0:T(2,128)(2,1)S(1)} %get-tuple-element.30.fresh_ref, bf16[10,512]{1,0:T(8,128)(2,1)S(1)} %get-tuple-element.31.residual_ref, ...), custom_call_target="tpu_custom_call" | custom-call | flops 1000 | bytes 100000 | tf_op jit(solution)/shard_map/attention/pallas_call | solution.py:41
  16.5 11.4 %all-gather = bf16[768,640]{1,0:T(8,128)(2,1)S(1)} all-gather(bf16[96,640]{1,0:T(8,128)(2,1)S(1)} %attention.1), channel_id=2, replica_groups=mesh['head'=4,'pool'=8] {'pool'}, dimensions={0}, use_global_device_ids=true | all-gather | bytes 1105920 | tf_op jit(solution)/shard_map/all_gather | solution.py:515
  27.9 1.5 %merge_project.1 = (f32[80,512]{1,0:T(8,128)S(1)}, bf16[80,512]{1,0:T(8,128)(2,1)S(1)}, bf16[80,512]{1,0:T(8,128)(2,1)S(1)}, bf16[80,512]{1,0:T(8,128)(2,1)S(1)}) custom-call(bf16[8,96,640]{2,1,0:T(8,128)(2,1)S(1)} %bitcast.12, bf16[512,2048]{1,0:T(8,128)(2,1)S(1)} %copy-done.3), custom_call_target="tpu_custom_call" | custom-call | flops 1000 | bytes 100000 | tf_op jit(solution)/shard_map/merge_project/pallas_call | solution.py:41
  29.4 1.7 %collective-permute-start.4 = (bf16[80,512]{1,0:T(8,128)(2,1)S(1)}, bf16[80,512]{1,0:T(8,128)(2,1)S(1)}, u32[]{:S(2)}, u32[]{:S(2)}) collective-permute-start(bf16[80,512]{1,0:T(8,128)(2,1)S(1)} %get-tuple-element.34), channel_id=1, source_target_pairs={{0,8},{8,0},{16,24},{24,16},{1,9},{9,1},{17,25},{25,17},{2,10},{10... | collective-permute-start | bytes 245768 | tf_op jit(solution)/shard_map/ppermute | solution.py:57
  31.1 2.6 %collective-permute-start.5 = (bf16[80,512]{1,0:T(8,128)(2,1)S(1)}, bf16[80,512]{1,0:T(8,128)(2,1)S(1)}, u32[]{:S(2)}, u32[]{:S(2)}) collective-permute-start(bf16[80,512]{1,0:T(8,128)(2,1)S(1)} %get-tuple-element.35), channel_id=1, source_target_pairs={{0,16},{8,24},{16,0},{24,8},{1,17},{9,25},{17,1},{25,9},{2,18},{10... | collective-permute-start | bytes 245768 | tf_op jit(solution)/shard_map/ppermute | solution.py:57
  33.7 0.2 collective-permute-start.6
  33.9 0.0 copy-done.12
  33.9 6.8 %routing.1 = (bf16[144,80]{1,0:T(8,128)(2,1)S(1)}, bf16[128,80]{1,0:T(8,128)(2,1)S(1)}, bf16[128,80]{1,0:T(8,128)(2,1)S(1)}, bf16[512,1024]{1,0:T(8,128)(2,1)S(1...) custom-call(s32[6,80]{1,0:T(8,128)S(1)} %bitcast.20, ...), custom_call_target="tpu_custom_call" | custom-call | flops 1000 | bytes 20000000 | tf_op jit(solution)/shard_map/routing/pallas_call | solution.py:41
  40.7 0.0 collective-permute-done.4.refs_0_
  40.7 0.0 collective-permute-done.5.refs_1_
  40.7 0.0 collective-permute-done.6.refs_2_
  40.7 0.0 copy-done.9
  40.7 0.6 prepare.1
  41.3 1.9 %experts_3.1 = (bf16[36,2944]{1,0:T(8,128)(2,1)S(1)}, f32[4,4,2944]{2,1,0:T(4,128)S(1)}) custom-call(bf16[144,1024]{1,0:T(8,128)(2,1)S(1)} %get-tuple-element.37.gate_ref, bf16[144,1024]{1,0:T(8,128)(2,1)S(1)} %get-tuple-element.38.up_ref, bf16[144,128]{1,0:T(8,128)(2,1)S(1)} %get-tuple-element.39.side_ref, ...), custom_call_target="tpu_custom_call" | custom-call | flops 1000 | bytes 100000 | tf_op jit(solution)/shard_map/experts_3/pallas_call | solution.py:41
  43.3 1.6 %collective-permute-start.7 = (bf16[36,2944]{1,0:T(8,128)(2,1)S(1)}, bf16[36,2944]{1,0:T(8,128)(2,1)S(1)}, u32[]{:S(2)}, u32[]{:S(2)}) collective-permute-start(bf16[36,2944]{1,0:T(8,128)(2,1)S(1)} %get-tuple-element.44), channel_id=1, source_target_pairs={{0,8},{8,0},{16,24},{24,16},{1,9},{9,1},{17,25},{25,17},{2,10},{10... | collective-permute-start | bytes 635912 | tf_op jit(solution)/shard_map/ppermute | solution.py:57
  44.8 1.3 %experts_1.1.refs_1_ = bf16[36,2944]{1,0:T(8,128)(2,1)S(1)} custom-call(bf16[144,1024]{1,0:T(8,128)(2,1)S(1)} %get-tuple-element.37.gate_ref, bf16[144,1024]{1,0:T(8,128)(2,1)S(1)} %get-tuple-element.38.up_ref, bf16[144,128]{1,0:T(8,128)(2,1)S(1)} %get-tuple-element.39.side_ref, bf16[2,512,2,1408]{3,2,1,0:T(2,128)(2,1)S(1)} %get-tuple-element.43.weight_ref, ...), custom_call_target="tpu_custom_call" | custom-call | flops 1000 | bytes 100000 | tf_op jit(solution)/shard_map/experts_1/pallas_call | solution.py:41
  46.2 0.6 collective-permute-start.9
  46.7 1.3 %experts_2.1.own_ref = bf16[36,2944]{1,0:T(8,128)(2,1)S(1)} custom-call(bf16[144,1024]{1,0:T(8,128)(2,1)S(1)} %get-tuple-element.37.gate_ref, bf16[144,1024]{1,0:T(8,128)(2,1)S(1)} %get-tuple-element.38.up_ref, bf16[144,128]{1,0:T(8,128)(2,1)S(1)} %get-tuple-element.39.side_ref, bf16[2,512,2,1408]{3,2,1,0:T(2,128)(2,1)S(1)} %get-tuple-element.42.weight_ref, ...), custom_call_target="tpu_custom_call" | custom-call | flops 1000 | bytes 100000 | tf_op jit(solution)/shard_map/experts_2/pallas_call | solution.py:41
  48.1 3.9 %collective-permute-done.7.received_ref = bf16[36,2944]{1,0:T(8,128)(2,1)S(1)} collective-permute-done((bf16[36,2944]{1,0:T(8,128)(2,1)S(1)}, bf16[36,2944]{1,0:T(8,128)(2,1)S(1)}, u32[]{:S(2)}, u32[]{:S(2)}) %collective-permute-start.7) | collective-permute-done | bytes 212000 | tf_op jit(solution)/shard_map/ppermute | solution.py:57
  52.0 0.1 add_pair.1.refs_1_
  52.0 0.0 slice-start.1
  52.1 0.0 slice-start.2
  52.1 2.6 %collective-permute-start.8 = (bf16[36,2944]{1,0:T(8,128)(2,1)S(1)}, bf16[36,2944]{1,0:T(8,128)(2,1)S(1)}, u32[]{:S(2)}, u32[]{:S(2)}) collective-permute-start(bf16[36,2944]{1,0:T(8,128)(2,1)S(1)} %add_pair.1.refs_1_), channel_id=1, source_target_pairs={{0,16},{8,24},{16,0},{24,8},{1,17},{9,25},{17,1},{25,9},{2,18},{10... | collective-permute-start | bytes 635912 | tf_op jit(solution)/shard_map/ppermute | solution.py:57
  54.6 4.6 %experts_0.1.refs_0_ = bf16[36,2944]{1,0:T(8,128)(2,1)S(1)} custom-call(bf16[144,1024]{1,0:T(8,128)(2,1)S(1)} %get-tuple-element.37.gate_ref, bf16[144,1024]{1,0:T(8,128)(2,1)S(1)} %get-tuple-element.38.up_ref, bf16[144,128]{1,0:T(8,128)(2,1)S(1)} %get-tuple-element.39.side_ref, bf16[8,512,2,1408]{3,2,1,0:T(2,128)(2,1)} %weight_ref.8, ...), custom_call_target="tpu_custom_call" | custom-call | flops 1000 | bytes 100000 | tf_op jit(solution)/shard_map/experts_0/pallas_call | solution.py:41
  59.2 0.2 collective-permute-done.9.refs_2_
  59.4 5.4 %collective-permute-done.8.refs_1_ = bf16[36,2944]{1,0:T(8,128)(2,1)S(1)} collective-permute-done((bf16[36,2944]{1,0:T(8,128)(2,1)S(1)}, bf16[36,2944]{1,0:T(8,128)(2,1)S(1)}, u32[]{:S(2)}, u32[]{:S(2)}) %collective-permute-start.8) | collective-permute-done | bytes 212000 | tf_op jit(solution)/shard_map/ppermute | solution.py:57
  64.8 0.2 hidden.1.hidden_ref.refs_0_
  65.0 0.1 collective-permute-start.11
  65.1 3.5 %collective-permute-start.10 = (bf16[36,1408]{1,0:T(8,128)(2,1)S(1)}, bf16[36,1408]{1,0:T(8,128)(2,1)S(1)}, u32[]{:S(2)}, u32[]{:S(2)}) collective-permute-start(bf16[36,1408]{1,0:T(8,128)(2,1)S(1)} %hidden.1.hidden_ref.refs_0_), channel_id=1, source_target_pairs={{0,8},{8,0},{16,24},{24,16},{1,9},{9,1},{17,25},{25,17},{2,10},{10... | collective-permute-start | bytes 304136 | tf_op jit(solution)/shard_map/ppermute | solution.py:57
  68.6 0.9 collective-permute-start.12
  69.5 0.5 down_0.1.refs_4_
  70.0 2.5 %collective-permute-done.11.hidden_ref.refs_2_ = bf16[36,1408]{1,0:T(8,128)(2,1)S(1)} collective-permute-done((bf16[36,1408]{1,0:T(8,128)(2,1)S(1)}, bf16[36,1408]{1,0:T(8,128)(2,1)S(1)}, u32[]{:S(2)}, u32[]{:S(2)}) %collective-permute-start.11) | collective-permute-done | bytes 101408 | tf_op jit(solution)/shard_map/ppermute | solution.py:57
  72.5 0.5 down_2.1.refs_6_
  73.0 0.0 collective-permute-done.10.hidden_ref.refs_1_
  73.0 0.0 slice-start.3
  73.0 0.5 down_1.1.refs_5_
  73.5 1.7 %collective-permute-done.12.refs_3_ = bf16[36,1408]{1,0:T(8,128)(2,1)S(1)} collective-permute-done((bf16[36,1408]{1,0:T(8,128)(2,1)S(1)}, bf16[36,1408]{1,0:T(8,128)(2,1)S(1)}, u32[]{:S(2)}, u32[]{:S(2)}) %collective-permute-start.12) | collective-permute-done | bytes 101408 | tf_op jit(solution)/shard_map/ppermute | solution.py:57
  75.2 0.9 combine.1
  76.1 8.1 %all_to_all.5.pieces_ref = bf16[8,10,512]{2,1,0:T(8,128)(2,1)S(1)} all-to-all(bf16[8,10,512]{2,1,0:T(8,128)(2,1)S(1)} %get-tuple-element.45), channel_id=1, replica_groups=mesh['head'=4,'pool'=8] {'pool'}, dimensions={0} | all-to-all | bytes 163840 | tf_op jit(solution)/shard_map/all_to_all | solution.py:621
  84.2 1.3 %collective-permute-start.15 = (bf16[10,512]{1,0:T(8,128)(2,1)S(1)}, bf16[10,512]{1,0:T(8,128)(2,1)S(1)}, u32[]{:S(2)}, u32[]{:S(2)}) collective-permute-start(bf16[10,512]{1,0:T(8,128)(2,1)S(1)} %block.1.refs_0_), channel_id=1, source_target_pairs={{0,24},{8,16},{16,8},{24,0},{1,25},{9,17},{17,9},{25,1},{2,26},{10... | collective-permute-start | bytes 30728 | tf_op jit(solution)/shard_map/ppermute | solution.py:57
  85.5 0.0 collective-permute-start.14
  85.5 3.2 %collective-permute-start.13 = (bf16[10,512]{1,0:T(8,128)(2,1)S(1)}, bf16[10,512]{1,0:T(8,128)(2,1)S(1)}, u32[]{:S(2)}, u32[]{:S(2)}) collective-permute-start(bf16[10,512]{1,0:T(8,128)(2,1)S(1)} %block.1.refs_0_), channel_id=1, source_target_pairs={{0,8},{8,0},{16,24},{24,16},{1,9},{9,1},{17,25},{25,17},{2,10},{10... | collective-permute-start | bytes 30728 | tf_op jit(solution)/shard_map/ppermute | solution.py:57
  88.7 1.2 %collective-permute-done.15.refs_3_ = bf16[10,512]{1,0:T(8,128)(2,1)S(1)} collective-permute-done((bf16[10,512]{1,0:T(8,128)(2,1)S(1)}, bf16[10,512]{1,0:T(8,128)(2,1)S(1)}, u32[]{:S(2)}, u32[]{:S(2)}) %collective-permute-start.15) | collective-permute-done | bytes 10272 | tf_op jit(solution)/shard_map/ppermute | solution.py:57
  89.9 0.4 collective-permute-done.14.refs_2_
  90.2 0.2 collective-permute-done.13.refs_1_
  90.4 1.6 %project.1 = (bf16[10,2048]{1,0:T(8,128)(2,1)}, bf16[10,1536]{1,0:T(8,128)(2,1)}) custom-call(bf16[16,128]{1,0:T(8,128)(2,1)S(1)} %bitcast.19, bf16[2048,1536]{1,0:T(8,128)(2,1)S(1)} %bitcast.11, bf16[10,512]{1,0:T(8,128)(2,1)S(1)} %block.1.refs_0_, bf16[10,512]{1,0:T(8,128)(2,1)S(1)} %collective-permute-done.13.refs_1_, ...), custom_call_target="tpu_custom_call" | custom-call | flops 1000 | bytes 100000 | tf_op jit(solution)/shard_map/project/pallas_call | solution.py:41
  (28 shorter events, 0.1 us)
Async XLA Ops:
  0.6 11.2 %collective-permute-start.2 = (bf16[1,10,512]{2,1,0:T(8,128)(2,1)}, bf16[1,10,512]{2,1,0:T(8,128)(2,1)S(1)}, u32[]{:S(2)}, u32[]{:S(2)}) collective-permute-start(bf16[1,10,512]{2,1,0:T(8,128)(2,1)} %bitcast.14), channel_id=1, source_target_pairs={{0,6},{1,7},{2,4},{3,5},{4,2},{5,3},{6,0},{7,1},{8,14},{9,15},{10,... | collective-permute-start | bytes 30728 | tf_op jit(solution)/shard_map/ppermute | solution.py:57
  4.6 7.2 %collective-permute-start.1 = (bf16[1,10,512]{2,1,0:T(8,128)(2,1)}, bf16[1,10,512]{2,1,0:T(8,128)(2,1)S(1)}, u32[]{:S(2)}, u32[]{:S(2)}) collective-permute-start(bf16[1,10,512]{2,1,0:T(8,128)(2,1)} %bitcast.15), channel_id=1, source_target_pairs={{0,4},{1,5},{2,6},{3,7},{4,0},{5,1},{6,2},{7,3},{8,12},{9,13},{10,... | collective-permute-start | bytes 30728 | tf_op jit(solution)/shard_map/ppermute | solution.py:57
  5.1 6.7 %collective-permute-start = (bf16[1,10,512]{2,1,0:T(8,128)(2,1)}, bf16[1,10,512]{2,1,0:T(8,128)(2,1)S(1)}, u32[]{:S(2)}, u32[]{:S(2)}) collective-permute-start(bf16[1,10,512]{2,1,0:T(8,128)(2,1)} %bitcast.16), channel_id=1, source_target_pairs={{0,2},{1,3},{2,0},{3,1},{4,6},{5,7},{6,4},{7,5},{8,10},{9,11},{10,... | collective-permute-start | bytes 30728 | tf_op jit(solution)/shard_map/ppermute | solution.py:57
  5.2 2.3 %copy-start = (bf16[36,2,64,512]{3,2,1,0:T(8,128)(2,1)S(1)}, bf16[36,2,64,512]{3,2,1,0:T(8,128)(2,1)}, u32[]{:S(2)}) copy-start(bf16[36,2,64,512]{3,2,1,0:T(8,128)(2,1)} %cache_ref.3) | copy-start | bytes 14155780
  7.6 0.8 copy-start.5
  8.4 0.8 copy-start.6
  9.2 0.7 copy-start.7
  9.9 0.7 copy-start.8
  10.6 0.7 copy-start.13
  11.3 2.3 %copy-start.1 = (bf16[36,2,64,512]{3,2,1,0:T(8,128)(2,1)S(1)}, bf16[36,2,64,512]{3,2,1,0:T(8,128)(2,1)}, u32[]{:S(2)}) copy-start(bf16[36,2,64,512]{3,2,1,0:T(8,128)(2,1)} %cache_ref.3) | copy-start | bytes 14155780
  11.3 16.6 %copy-start.3 = (bf16[512,2048]{1,0:T(8,128)(2,1)S(1)}, bf16[512,2048]{1,0:T(8,128)(2,1)}, u32[]{:S(2)}) copy-start(bf16[512,2048]{1,0:T(8,128)(2,1)} %weight_ref.7) | copy-start | bytes 6291460
  11.8 22.1 %copy-start.11 = (s32[80,6]{0,1:T(8,128)S(1)}, s32[80,6]{0,1:T(8,128)}, u32[]{:S(2)}) copy-start(s32[80,6]{0,1:T(8,128)} %param.24) | copy-start | bytes 5764
  11.8 22.1 %copy-start.12 = (f32[80,6]{0,1:T(8,128)S(1)}, f32[80,6]{0,1:T(8,128)}, u32[]{:S(2)}) copy-start(f32[80,6]{0,1:T(8,128)} %param.25) | copy-start | bytes 5764
  11.8 1.3 %collective-permute-start.3 = (bf16[4,10,512]{2,1,0:T(8,128)(2,1)S(1)}, bf16[4,10,512]{2,1,0:T(8,128)(2,1)S(1)}, u32[]{:S(2)}, u32[]{:S(2)}) collective-permute-start(bf16[4,10,512]{2,1,0:T(8,128)(2,1)S(1)} %join_queries.1.refs_0_), channel_id=1, source_target_pairs={{0,1},{1,0},{2,3},{3,2},{4,5},{5,4},{6,7},{7,6},{8,9},{9,8},{10,11... | collective-permute-start | bytes 122888 | tf_op jit(solution)/shard_map/ppermute | solution.py:57
  29.4 11.3 %collective-permute-start.4 = (bf16[80,512]{1,0:T(8,128)(2,1)S(1)}, bf16[80,512]{1,0:T(8,128)(2,1)S(1)}, u32[]{:S(2)}, u32[]{:S(2)}) collective-permute-start(bf16[80,512]{1,0:T(8,128)(2,1)S(1)} %get-tuple-element.34), channel_id=1, source_target_pairs={{0,8},{8,0},{16,24},{24,16},{1,9},{9,1},{17,25},{25,17},{2,10},{10... | collective-permute-start | bytes 245768 | tf_op jit(solution)/shard_map/ppermute | solution.py:57
  31.1 9.6 %collective-permute-start.5 = (bf16[80,512]{1,0:T(8,128)(2,1)S(1)}, bf16[80,512]{1,0:T(8,128)(2,1)S(1)}, u32[]{:S(2)}, u32[]{:S(2)}) collective-permute-start(bf16[80,512]{1,0:T(8,128)(2,1)S(1)} %get-tuple-element.35), channel_id=1, source_target_pairs={{0,16},{8,24},{16,0},{24,8},{1,17},{9,25},{17,1},{25,9},{2,18},{10... | collective-permute-start | bytes 245768 | tf_op jit(solution)/shard_map/ppermute | solution.py:57
  33.7 7.1 %collective-permute-start.6 = (bf16[80,512]{1,0:T(8,128)(2,1)S(1)}, bf16[80,512]{1,0:T(8,128)(2,1)S(1)}, u32[]{:S(2)}, u32[]{:S(2)}) collective-permute-start(bf16[80,512]{1,0:T(8,128)(2,1)S(1)} %get-tuple-element.36), channel_id=1, source_target_pairs={{0,24},{8,16},{16,8},{24,0},{1,25},{9,17},{17,9},{25,1},{2,26},{10... | collective-permute-start | bytes 245768 | tf_op jit(solution)/shard_map/ppermute | solution.py:57
  33.9 6.8 %copy-start.9 = (bf16[2048]{0:T(1024)(128)(2,1)S(1)}, bf16[2048]{0:T(1024)(128)(2,1)}, u32[]{:S(2)}) copy-start(bf16[2048]{0:T(1024)(128)(2,1)} %param.23) | copy-start | bytes 12292
  33.9 7.4 %copy-start.2 = (bf16[1,512,2,1408]{3,2,1,0:T(2,128)(2,1)S(1)}, bf16[1,512,2,1408]{3,2,1,0:T(2,128)(2,1)}, u32[]{:S(2)}) copy-start(bf16[1,512,2,1408]{3,2,1,0:T(2,128)(2,1)} %refs_0_.1) | copy-start | bytes 8650756
  43.3 8.7 %collective-permute-start.7 = (bf16[36,2944]{1,0:T(8,128)(2,1)S(1)}, bf16[36,2944]{1,0:T(8,128)(2,1)S(1)}, u32[]{:S(2)}, u32[]{:S(2)}) collective-permute-start(bf16[36,2944]{1,0:T(8,128)(2,1)S(1)} %get-tuple-element.44), channel_id=1, source_target_pairs={{0,8},{8,0},{16,24},{24,16},{1,9},{9,1},{17,25},{25,17},{2,10},{10... | collective-permute-start | bytes 635912 | tf_op jit(solution)/shard_map/ppermute | solution.py:57
  46.2 13.2 %collective-permute-start.9 = (bf16[36,2944]{1,0:T(8,128)(2,1)S(1)}, bf16[36,2944]{1,0:T(8,128)(2,1)S(1)}, u32[]{:S(2)}, u32[]{:S(2)}) collective-permute-start(bf16[36,2944]{1,0:T(8,128)(2,1)S(1)} %experts_1.1.refs_1_), channel_id=1, source_target_pairs={{0,8},{8,0},{16,24},{24,16},{1,9},{9,1},{17,25},{25,17},{2,10},{10... | collective-permute-start | bytes 635912 | tf_op jit(solution)/shard_map/ppermute | solution.py:57
  52.0 17.5 %slice-start = ((s8[11534336]{0:T(1024)(128)(4,1)}), s8[4194304]{0:T(1024)(128)(4,1)S(1)}, s32[]{:S(2)}) async-start(s8[11534336]{0:T(1024)(128)(4,1)} %bitcast.8), calls=%async_computation.1 | async-start | bytes 8388608
  52.0 17.4 %slice-start.1 = ((s8[11534336]{0:T(1024)(128)(4,1)}), s8[4194304]{0:T(1024)(128)(4,1)S(1)}, s32[]{:S(2)}) async-start(s8[11534336]{0:T(1024)(128)(4,1)} %bitcast.8), calls=%async_computation.2 | async-start | bytes 8388608
  52.1 17.4 %slice-start.2 = ((s8[11534336]{0:T(1024)(128)(4,1)}), s8[3145728]{0:T(1024)(128)(4,1)S(1)}, s32[]{:S(2)}) async-start(s8[11534336]{0:T(1024)(128)(4,1)} %bitcast.8), calls=%async_computation.3 | async-start | bytes 6291456
  52.1 12.7 %collective-permute-start.8 = (bf16[36,2944]{1,0:T(8,128)(2,1)S(1)}, bf16[36,2944]{1,0:T(8,128)(2,1)S(1)}, u32[]{:S(2)}, u32[]{:S(2)}) collective-permute-start(bf16[36,2944]{1,0:T(8,128)(2,1)S(1)} %add_pair.1.refs_1_), channel_id=1, source_target_pairs={{0,16},{8,24},{16,0},{24,8},{1,17},{9,25},{17,1},{25,9},{2,18},{10... | collective-permute-start | bytes 635912 | tf_op jit(solution)/shard_map/ppermute | solution.py:57
  65.0 7.5 %collective-permute-start.11 = (bf16[36,1408]{1,0:T(8,128)(2,1)S(1)}, bf16[36,1408]{1,0:T(8,128)(2,1)S(1)}, u32[]{:S(2)}, u32[]{:S(2)}) collective-permute-start(bf16[36,1408]{1,0:T(8,128)(2,1)S(1)} %hidden.1.hidden_ref.refs_0_), channel_id=1, source_target_pairs={{0,16},{8,24},{16,0},{24,8},{1,17},{9,25},{17,1},{25,9},{2,18},{10... | collective-permute-start | bytes 304136 | tf_op jit(solution)/shard_map/ppermute | solution.py:57
  65.1 7.9 %collective-permute-start.10 = (bf16[36,1408]{1,0:T(8,128)(2,1)S(1)}, bf16[36,1408]{1,0:T(8,128)(2,1)S(1)}, u32[]{:S(2)}, u32[]{:S(2)}) collective-permute-start(bf16[36,1408]{1,0:T(8,128)(2,1)S(1)} %hidden.1.hidden_ref.refs_0_), channel_id=1, source_target_pairs={{0,8},{8,0},{16,24},{24,16},{1,9},{9,1},{17,25},{25,17},{2,10},{10... | collective-permute-start | bytes 304136 | tf_op jit(solution)/shard_map/ppermute | solution.py:57
  68.6 6.6 %collective-permute-start.12 = (bf16[36,1408]{1,0:T(8,128)(2,1)S(1)}, bf16[36,1408]{1,0:T(8,128)(2,1)S(1)}, u32[]{:S(2)}, u32[]{:S(2)}) collective-permute-start(bf16[36,1408]{1,0:T(8,128)(2,1)S(1)} %hidden.1.hidden_ref.refs_0_), channel_id=1, source_target_pairs={{0,24},{8,16},{16,8},{24,0},{1,25},{9,17},{17,9},{25,1},{2,26},{10... | collective-permute-start | bytes 304136 | tf_op jit(solution)/shard_map/ppermute | solution.py:57
  73.0 2.2 %copy-start.4 = (bf16[1,1408,512]{2,1,0:T(8,128)(2,1)S(1)}, bf16[1,1408,512]{2,1,0:T(8,128)(2,1)}, u32[]{:S(2)}) copy-start(bf16[1,1408,512]{2,1,0:T(8,128)(2,1)} %shared_weight_ref.1) | copy-start | bytes 4325380
  73.0 17.4 %slice-start.3 = ((s8[6291456]{0:T(1024)(128)(4,1)}), s8[4194304]{0:T(1024)(128)(4,1)S(1)}, s32[]{:S(2)}) async-start(s8[6291456]{0:T(1024)(128)(4,1)} %bitcast.10), calls=%async_computation.4 | async-start | bytes 8388608
  75.2 15.2 %slice-start.4 = ((s8[6291456]{0:T(1024)(128)(4,1)}), s8[2097152]{0:T(1024)(128)(4,1)S(1)}, s32[]{:S(2)}) async-start(s8[6291456]{0:T(1024)(128)(4,1)} %bitcast.10), calls=%async_computation.5 | async-start | bytes 4194304
  75.2 15.2 %copy-start.10 = (bf16[2048]{0:T(1024)(128)(2,1)S(1)}, bf16[2048]{0:T(1024)(128)(2,1)}, u32[]{:S(2)}) copy-start(bf16[2048]{0:T(1024)(128)(2,1)} %param.30) | copy-start | bytes 12292
  84.2 5.7 %collective-permute-start.15 = (bf16[10,512]{1,0:T(8,128)(2,1)S(1)}, bf16[10,512]{1,0:T(8,128)(2,1)S(1)}, u32[]{:S(2)}, u32[]{:S(2)}) collective-permute-start(bf16[10,512]{1,0:T(8,128)(2,1)S(1)} %block.1.refs_0_), channel_id=1, source_target_pairs={{0,24},{8,16},{16,8},{24,0},{1,25},{9,17},{17,9},{25,1},{2,26},{10... | collective-permute-start | bytes 30728 | tf_op jit(solution)/shard_map/ppermute | solution.py:57
  85.5 4.7 %collective-permute-start.14 = (bf16[10,512]{1,0:T(8,128)(2,1)S(1)}, bf16[10,512]{1,0:T(8,128)(2,1)S(1)}, u32[]{:S(2)}, u32[]{:S(2)}) collective-permute-start(bf16[10,512]{1,0:T(8,128)(2,1)S(1)} %block.1.refs_0_), channel_id=1, source_target_pairs={{0,16},{8,24},{16,0},{24,8},{1,17},{9,25},{17,1},{25,9},{2,18},{10... | collective-permute-start | bytes 30728 | tf_op jit(solution)/shard_map/ppermute | solution.py:57
  85.5 4.9 %collective-permute-start.13 = (bf16[10,512]{1,0:T(8,128)(2,1)S(1)}, bf16[10,512]{1,0:T(8,128)(2,1)S(1)}, u32[]{:S(2)}, u32[]{:S(2)}) collective-permute-start(bf16[10,512]{1,0:T(8,128)(2,1)S(1)} %block.1.refs_0_), channel_id=1, source_target_pairs={{0,8},{8,0},{16,24},{24,16},{1,9},{9,1},{17,25},{25,17},{2,10},{10... | collective-permute-start | bytes 30728 | tf_op jit(solution)/shard_map/ppermute | solution.py:57

commit v3 on v2

--- a/solution.py
+++ b/solution.py
@@ -13,6 +13,7 @@
 TILE = 16
 MOST = 2
 SPLIT = 4
+HALF = LANES // 2
 
 
 epsilon = 1e-06
@@ -21,6 +22,7 @@
 f32 = jnp.float32
 over_rows = (((0,), (0,)), ((), ()))
 VMEM = pl.BlockSpec(memory_space=pltpu.VMEM)
+SMEM = pl.BlockSpec(memory_space=pltpu.SMEM)
 FAR = pl.BlockSpec(memory_space=pltpu.HBM)
 
 
@@ -34,6 +36,10 @@
 
 def dot(left, right):
     return jnp.dot(left, right, preferred_element_type=f32)
+
+
+def place(shape):
+    return SMEM if shape == (1,) else VMEM
 
 
 def call(kernel, name, outs, args, scratch=(), copies=(), far=(), megabytes=4, moved=1e5):
@@ -41,8 +47,8 @@
     return pl.pallas_call(
         kernel,
         out_shape=[jax.ShapeDtypeStruct(shape, dtype) for shape, dtype in outs],
-        in_specs=[FAR if i in far else VMEM for i in range(len(args))],
-        out_specs=[VMEM] * len(outs),
+        in_specs=[FAR if i in far else place(arg.shape) for i, arg in enumerate(args)],
+        out_specs=[place(shape) for shape, _ in outs],
         scratch_shapes=[pltpu.VMEM(shape, dtype) for shape, dtype in scratch] + semaphores,
         compiler_params=pltpu.CompilerParams(vmem_limit_bytes=int(megabytes * 2**20)),
         cost_estimate=pl.CostEstimate(
@@ -85,25 +91,12 @@
     return copies
 
 
-def setup_kernel(
-    table_ref,
-    length_ref,
-    given_query_ref,
-    given_fresh_ref,
-    given_residual_ref,
-    cache_ref,
-    bias_ref,
-    query_ref,
-    fresh_ref,
-    residual_ref,
-):
-    query_ref[...] = given_query_ref[...]
-    fresh_ref[...] = given_fresh_ref[...]
-    lane_width = residual_ref.shape[1]
-    start = pl.multiple_of(lax.axis_index("head") * lane_width, LANES)
-    residual_ref[...] = given_residual_ref[:, pl.ds(start, lane_width)]
+def early_kernel(*refs):
+    refs[-1][0] = 0
+
+
+def setup_kernel(blocks, block_len, early_ref, table_ref, length_ref, bias_ref):
     pool_idx = lax.axis_index("pool")
-    blocks, _, block_len, _ = cache_ref.shape
     list_len, req_total = table_ref.shape
     tokens = blocks * block_len
     table = table_ref[...] - pool_idx * blocks
@@ -170,25 +163,28 @@
             new_weights.astype(bf16), fresh_ref[:, 1, columns]
         )
         inverse = jnp.where(total > 0.0, 1.0 / jnp.where(total > 0.0, total, 1.0), 0.0)
-        out_ref[:req_total, columns] = (mixed * inverse).astype(bf16)
+        out_ref[:, columns] = (mixed * inverse).astype(bf16)
         coarse = total.astype(bf16).astype(f32)
         side = jnp.where(lane == head, top, side)
         side = jnp.where(lane == heads + head, coarse, side)
         side = jnp.where(lane == 2 * heads + head, total - coarse, side)
-    out_ref[:req_total, lane_width:] = side.astype(bf16)
-    out_ref[req_total:, :] = jnp.zeros((out_ref.shape[0] - req_total, out_ref.shape[1]), bf16)
-    out_ref[req_total : req_total + req_dev, :lane_width] = residual_ref[...]
+    out_ref[:, lane_width:] = side.astype(bf16)
+    start = pl.multiple_of(lax.axis_index("head") * lane_width, LANES)
+    residual = residual_ref[:, pl.ds(start, lane_width)]
+    for i in range(lane_width // HALF):
+        rows = slice(i * req_dev, (i + 1) * req_dev)
+        out_ref[rows, lane_width + HALF :] = residual[:, i * HALF : (i + 1) * HALF]
 
 
 def merge_kernel(req_dev, parts_ref, weight_ref, *refs):
     out_refs, attended_ref = refs[:-1], refs[-1]
-    count, _, packed = parts_ref.shape
-    req_total, col_part = out_refs[0].shape
+    count, req_total, packed = parts_ref.shape
+    col_part = out_refs[0].shape[1]
     lane_width = packed - LANES
     heads = lane_width // HD
     me = lax.axis_index("head")
     lane = iota((req_total, LANES), 1)
-    sides = [parts_ref[i, :req_total, lane_width:].astype(f32) for i in range(count)]
+    sides = [parts_ref[i, :, lane_width:].astype(f32) for i in range(count)]
 
     def column(side, place):
         return jnp.sum(jnp.where(lane == place, side, 0.0), axis=1, keepdims=True)
@@ -202,17 +198,19 @@
         denominator = functools.reduce(jnp.add, shares)
         mixed = functools.reduce(
             jnp.add,
-            [shares[i] * parts_ref[i, :req_total, columns].astype(f32) for i in range(count)],
+            [shares[i] * parts_ref[i, :, columns].astype(f32) for i in range(count)],
         )
         attended_ref[:, columns] = (mixed / denominator).astype(bf16)
     for distance, out_ref in enumerate(out_refs):
         start = pl.multiple_of((me ^ distance) * col_part, LANES)
         projected = dot(attended_ref[...], weight_ref[:, pl.ds(start, col_part)])
         out_ref[...] = projected.astype(out_ref.dtype)
-    for i in range(count):
+    for i, side in enumerate(sides):
         rows = slice(i * req_dev, (i + 1) * req_dev)
-        residual = parts_ref[i, req_total : req_total + req_dev, :col_part].astype(f32)
-        out_refs[0][rows, :] = out_refs[0][rows, :] + residual
+        pieces = [
+            side[k * req_dev : (k + 1) * req_dev, HALF:] for k in range(lane_width // HALF)
+        ]
+        out_refs[0][rows, :] = out_refs[0][rows, :] + jnp.concatenate(pieces, axis=1)
 
 
 def routing_kernel(
@@ -221,6 +219,7 @@
     req_dev,
     routes_ref,
     gates_ref,
+    after_ref,
     far_weight_ref,
     pick_ref,
     coarse_ref,
@@ -341,8 +340,9 @@
     out_ref[part:, :] = shared_ref[target].astype(bf16)
 
 
-def add_kernel(own_ref, received_ref, out_ref):
+def add_kernel(own_ref, received_ref, later_ref, out_ref, sent_ref):
     out_ref[...] = (own_ref[...].astype(f32) + received_ref[...].astype(f32)).astype(bf16)
+    sent_ref[...] = later_ref[...]
 
 
 def hidden_kernel(width, *refs):
@@ -413,31 +413,37 @@
     out_ref[...] = total.astype(bf16)
 
 
-def join_kernel(*refs):
-    place = 0
-    for ref in refs[:-1]:
-        count = ref.shape[0]
-        refs[-1][place : place + count] = ref[...]
-        place += count
-
-
-def project_kernel(gain_ref, weight_ref, *refs):
-    block_refs, (hidden_ref, out_ref) = refs[:-2], refs[-2:]
+def join_kernel(bias_ref, *refs):
+    for place, ref in enumerate(refs[:-1]):
+        refs[-1][place] = ref[0]
+
+
+def project_kernel(distances, width, gain_ref, weight_ref, *refs):
     me = lax.axis_index("head")
-    blocks = [ref[...].astype(f32) for ref in block_refs]
-    req_dev, col_part = blocks[0].shape
-    width = hidden_ref.shape[1]
-    squares = [jnp.sum(block * block, axis=1, keepdims=True) for block in blocks]
-    row_scale = lax.rsqrt(functools.reduce(jnp.add, squares) / width + epsilon)
-    total = jnp.zeros(out_ref.shape, f32)
-    for distance, block in enumerate(blocks):
-        start = pl.multiple_of((me ^ distance) * col_part, LANES)
-        columns = pl.ds(start, col_part)
-        hidden_ref[:, columns] = block.astype(bf16)
-        gains = gain_columns(gain_ref, me ^ distance, col_part)
-        normed = (block * row_scale * gains).astype(bf16)
-        total = total + dot(normed, weight_ref[columns, :])
-    out_ref[...] = total.astype(bf16)
+    count = len(distances)
+    block_refs, refs = refs[:count], refs[count:]
+    if distances[0] == 0:
+        total_ref, side_ref = refs
+        total, squares = jnp.zeros(total_ref.shape, f32), 0.0
+    else:
+        own_ref, given_total_ref, given_side_ref, hidden_ref, out_ref = refs
+        total, squares = given_total_ref[...], given_side_ref[:, 0:1]
+    for distance, ref in zip(distances, block_refs):
+        block = ref[...].astype(f32)
+        req_dev, col_part = block.shape
+        columns = pl.ds(pl.multiple_of((me ^ distance) * col_part, LANES), col_part)
+        if distances[0] != 0:
+            hidden_ref[:, columns] = ref[...]
+        squares = squares + jnp.sum(block * block, axis=1, keepdims=True)
+        scaled = (block * gain_columns(gain_ref, me ^ distance, col_part)).astype(bf16)
+        total = total + dot(scaled, weight_ref[columns, :])
+    if distances[0] == 0:
+        total_ref[...] = total
+        side_ref[...] = jnp.broadcast_to(squares, side_ref.shape)
+    else:
+        columns = pl.ds(pl.multiple_of(me * col_part, LANES), col_part)
+        hidden_ref[:, columns] = own_ref[...]
+        out_ref[...] = (total * lax.rsqrt(squares / width + epsilon)).astype(bf16)
 
 
 def per_device(
@@ -468,7 +474,6 @@
     slots = min(MOST * pools, req_total)
     slot_total = exp_dev * slots
     extra = -(-req_dev // TILE) * TILE
-    padded = -(-req_dev // TILE) * TILE + req_total
     small = pools <= 8
     distances = list(range(1, head_devs))
     piece_experts = max(1, exp_dev // head_devs)
@@ -476,23 +481,32 @@
     fetched = list(reversed(range(1, head_devs)))
 
     queries = queries[None]
-    bias, own_queries, fresh, residual_part = call(
-        setup_kernel,
+    table, counts = block_table.T, lengths[None, :]
+    later = [queries, table, counts, cache_blocks, fresh_pair, residual, w_gate_up]
+    (early,) = call(
+        early_kernel,
+        "early",
+        [((1,), jnp.int32)],
+        later,
+        far=range(len(later)),
+        megabytes=59,
+    )
+    (bias,) = call(
+        functools.partial(setup_kernel, blk_count, block_len),
         "setup",
-        [
-            ((req_total, blk_count * block_len), f32),
-            (queries.shape, bf16),
-            (fresh_pair.shape, bf16),
-            ((req_dev, col_part), bf16),
-        ],
-        [block_table.T, lengths[None, :], queries, fresh_pair, residual, cache_blocks],
+        [((req_total, blk_count * block_len), f32)],
+        [early, table, counts],
         megabytes=4 + 16 * req_total * blk_count * block_len / 2**20,
     )
     if small:
         order = list(range(0, pools, 2))
-        pieces = [own_queries] + [swap(queries, "pool", d) for d in order[1:]]
+        pieces = [queries] + [swap(queries, "pool", d) for d in order[1:]]
         (joined,) = call(
-            join_kernel, "join_queries", [((len(order), req_dev, lane_width), bf16)], pieces
+            join_kernel,
+            "join_queries",
+            [((len(order), req_dev, lane_width), bf16)],
+            [bias] + pieces,
+            far=[0],
         )
         pieces = [joined, swap(joined, "pool", 1)]
         order = order + [d + 1 for d in order]
@@ -507,8 +521,8 @@
     (partial,) = call(
         functools.partial(attention_kernel, order),
         "attention",
-        [((padded, lane_width + LANES), bf16)],
-        [cache_blocks, bias, fresh, residual_part] + pieces,
+        [((req_total, lane_width + LANES), bf16)],
+        [cache_blocks, bias, fresh_pair, residual] + pieces,
         scratch=[((pools, req_dev, lane_width), f32)],
         megabytes=4 + 32 * req_total * blk_count * block_len / 2**20,
     )
@@ -531,8 +545,8 @@
             ((col_part, 2 * col_part), bf16),
         ]
         + [fetch_shape] * len(fetched),
-        [routes.T, route_gates.T, w_gate_up],
-        far=[2],
+        [routes.T, route_gates.T, sums[0], w_gate_up],
+        far=[3],
         copies=[len(fetched) * piece_experts * SPLIT],
         megabytes=24,
         moved=2e7,
@@ -587,9 +601,14 @@
     if head_devs == 4:
         near = swap(experts(3), "head", 1)
         own_near = experts(1)
-        near_own = swap(own_near, "head", 1)
-        (pair,) = call(add_kernel, "add_pair", [piece_shape], [experts(2, [own_near]), near])
-        parts = [experts(0, [pair]), swap(pair, "head", 2), near_own]
+        pair, own_near = call(
+            add_kernel,
+            "add_pair",
+            [piece_shape, piece_shape],
+            [experts(2, [own_near]), near, own_near],
+        )
+        far = swap(pair, "head", 2)
+        parts = [experts(0, [pair]), far, swap(own_near, "head", 1)]
     else:
         parts = [swap(experts(d), "head", d) for d in reversed(range(1, head_devs))]
         parts = [experts(0)] + parts
@@ -627,11 +646,20 @@
         megabytes=4,
     )
     blocks = [block] + [swap(block, "head", d) for d in distances]
+    last_args = [next_gain.reshape(-1, LANES), w_query_key_value]
+    out_width = w_query_key_value.shape[1]
+    total, squares = call(
+        functools.partial(project_kernel, [0], width),
+        "project_own",
+        [((req_dev, out_width), f32), ((req_dev, LANES), f32)],
+        last_args + [block],
+        megabytes=6,
+    )
     next_hidden, next_projection = call(
-        project_kernel,
+        functools.partial(project_kernel, distances, width),
         "project",
-        [((req_dev, width), bf16), ((req_dev, w_query_key_value.shape[1]), bf16)],
-        [next_gain.reshape(-1, LANES), w_query_key_value] + blocks,
+        [((req_dev, width), bf16), ((req_dev, out_width), bf16)],
+        last_args + blocks[1:] + [block, total, squares],
         megabytes=6,
     )
     return (next_hidden, next_projection)

time: 92.5 us -> 87 us (0.941)
  local copies, waits for them, and re-layouts: 6.54 us -> 0.27 us
  Pallas kernels: 25.7 us -> 27.1 us
  starting transfers between devices: 22.8 us -> 23.8 us
    unnamed x38 -> x36, local copies, waits for them, and re-layouts: 6.54 us -> 0.27 us
    pallas_call x18 -> x20, Pallas kernels: 25.7 us -> 27.1 us  [call(): pl.pallas_call(kernel, out_shape=[jax.ShapeDtypeStruct(shape, dtype) for...]
    ppermute x16, starting transfers between devices: 22.8 us -> 23.8 us  [swap(): return lax.ppermute(value, axis, [(i, i ^ distance) for i in range(count)])]
  transfers between devices with their start and end apart: 16 -> 16, of which waited for: 9 -> 10; matrix products, arithmetic and copies ran while one was open for 0% -> 0% of each run, Pallas kernels for 17% -> 21%
where the time goes in v3:
time: 87 us; the launch traced here: 86.8 us
  Pallas kernels  27.1 us (31%)
  starting transfers between devices  23.8 us (27%)
  blocking collectives  18.8 us (22%)
  waiting for transfers between devices  16 us (18%)
    pallas_call x20, Pallas kernels, call(): pl.pallas_call(kernel, out_shape=[jax.ShapeDtypeStruct(shape, dtype) for...  27.1 us
    ppermute x16, starting transfers between devices, swap(): return lax.ppermute(value, axis, [(i, i ^ distance) for i in range(count)])  23.8 us
    ppermute x16, waiting for transfers between devices, swap(): return lax.ppermute(value, axis, [(i, i ^ distance) for i in range(count)])  16 us
    all_gather x1, blocking collectives, per_device(): parts = lax.all_gather(partial, 'pool', axis=0)  10.7 us
    all_to_all x1, blocking collectives, per_device(): pieces = lax.all_to_all(routed, 'pool', 0, 0)  8.06 us
  transfers between devices with their start and end apart: 16, of which 10 were waited for; matrix products, arithmetic and copies ran while one was open for 0% of the time, Pallas kernels for 21%

profile of v3, /device:TPU:0, one launch (start us, length us, event | category | flops | bytes accessed | tf_op | source)
XLA Modules:
  0.0 86.8 jit_solution(11763300891698215330)
XLA Ops:
  0.6 4.0 %collective-permute-start.2 = (bf16[1,10,512]{2,1,0:T(8,128)(2,1)}, bf16[1,10,512]{2,1,0:T(8,128)(2,1)S(1)}, u32[]{:S(2)}, u32[]{:S(2)}) collective-permute-start(bf16[1,10,512]{2,1,0:T(8,128)(2,1)} %bitcast.15), channel_id=1, source_target_pairs={{0,6},{1,7},{2,4},{3,5},{4,2},{5,3},{6,0},{7,1},{8,14},{9,15},{10,... | collective-permute-start | bytes 30728 | tf_op jit(solution)/shard_map/ppermute | solution.py:63
  4.6 0.5 collective-permute-start.1
  5.1 0.1 collective-permute-start
  5.2 0.0 copy-start.4
  5.3 0.0 copy-start.6
  5.3 0.5 early.1.early_ref
  5.8 0.2 copy-done.5
  6.0 0.0 copy-done.12
  6.0 1.5 %setup.1.bias_ref = f32[80,2304]{1,0:T(8,128)S(1)} custom-call(s32[1]{0:T(128)} %early.1.early_ref, s32[64,80]{1,0:T(8,128)S(1)} %bitcast.14, s32[1,80]{1,0:T(1,128)S(1)} %bitcast.26), custom_call_target="tpu_custom_call" | custom-call | flops 1000 | bytes 100000 | tf_op jit(solution)/shard_map/setup/pallas_call | solution.py:47
  7.6 0.0 collective-permute-done.2.refs_3_
  7.6 1.0 %collective-permute-done.1.refs_2_ = bf16[1,10,512]{2,1,0:T(8,128)(2,1)S(1)} collective-permute-done((bf16[1,10,512]{2,1,0:T(8,128)(2,1)}, bf16[1,10,512]{2,1,0:T(8,128)(2,1)S(1)}, u32[]{:S(2)}, u32[]{:S(2)}) %collective-permute-start.1) | collective-permute-done | bytes 10272 | tf_op jit(solution)/shard_map/ppermute | solution.py:63
  8.5 0.5 collective-permute-done.refs_1_
  9.0 0.0 copy-done.7
  9.1 0.1 collective-permute-start.3
  9.1 1.2 %collective-permute-done.3.refs_1_ = bf16[4,10,512]{2,1,0:T(8,128)(2,1)S(1)} collective-permute-done((bf16[4,10,512]{2,1,0:T(8,128)(2,1)S(1)}, bf16[4,10,512]{2,1,0:T(8,128)(2,1)S(1)}, u32[]{:S(2)}, u32[]{:S(2)}) %collective-permute-start.3) | collective-permute-done | bytes 40992 | tf_op jit(solution)/shard_map/ppermute | solution.py:63
  10.4 0.0 copy-done
  10.4 0.0 copy-done.4
  10.4 0.0 copy-done.6
  10.4 2.7 %attention.1 = bf16[80,640]{1,0:T(8,128)(2,1)S(1)} custom-call(bf16[36,2,64,512]{3,2,1,0:T(8,128)(2,1)S(1)} %copy-done, f32[80,2304]{1,0:T(8,128)S(1)} %setup.1.bias_ref, bf16[10,2,512]{2,1,0:T(2,128)(2,1)S(1)} %copy-done.6, bf16[10,2048]{1,0:T(8,128)(2,1)S(1)} %copy-done.4, bf16[4,10,512]{2,1,0:T(8,128)(2,1)S(1)} %join_queries.1.refs_0_, ...), custom_call_target="tpu_custom_call" | custom-call | flops 1000 | bytes 100000 | tf_op jit(solution)/shard_map/attention/pallas_call | solution.py:47
  13.1 10.7 %all-gather = bf16[640,640]{1,0:T(8,128)(2,1)S(1)} all-gather(bf16[80,640]{1,0:T(8,128)(2,1)S(1)} %attention.1), channel_id=2, replica_groups=mesh['head'=4,'pool'=8] {'pool'}, dimensions={0}, use_global_device_ids=true | all-gather | bytes 921600 | tf_op jit(solution)/shard_map/all_gather | solution.py:529
  23.8 1.5 %merge_project.1 = (f32[80,512]{1,0:T(8,128)S(1)}, bf16[80,512]{1,0:T(8,128)(2,1)S(1)}, bf16[80,512]{1,0:T(8,128)(2,1)S(1)}, bf16[80,512]{1,0:T(8,128)(2,1)S(1)}) custom-call(bf16[8,80,640]{2,1,0:T(8,128)(2,1)S(1)} %bitcast.12, bf16[512,2048]{1,0:T(8,128)(2,1)S(1)} %copy-done.2), custom_call_target="tpu_custom_call" | custom-call | flops 1000 | bytes 100000 | tf_op jit(solution)/shard_map/merge_project/pallas_call | solution.py:47
  25.4 1.6 %collective-permute-start.4 = (bf16[80,512]{1,0:T(8,128)(2,1)S(1)}, bf16[80,512]{1,0:T(8,128)(2,1)S(1)}, u32[]{:S(2)}, u32[]{:S(2)}) collective-permute-start(bf16[80,512]{1,0:T(8,128)(2,1)S(1)} %get-tuple-element.30), channel_id=1, source_target_pairs={{0,8},{8,0},{16,24},{24,16},{1,9},{9,1},{17,25},{25,17},{2,10},{10... | collective-permute-start | bytes 245768 | tf_op jit(solution)/shard_map/ppermute | solution.py:63
  27.0 2.6 %collective-permute-start.5 = (bf16[80,512]{1,0:T(8,128)(2,1)S(1)}, bf16[80,512]{1,0:T(8,128)(2,1)S(1)}, u32[]{:S(2)}, u32[]{:S(2)}) collective-permute-start(bf16[80,512]{1,0:T(8,128)(2,1)S(1)} %get-tuple-element.31), channel_id=1, source_target_pairs={{0,16},{8,24},{16,0},{24,8},{1,17},{9,25},{17,1},{25,9},{2,18},{10... | collective-permute-start | bytes 245768 | tf_op jit(solution)/shard_map/ppermute | solution.py:63
  29.6 0.2 collective-permute-start.6
  29.8 0.0 copy-done.11
  29.8 6.8 %routing.1 = (bf16[144,80]{1,0:T(8,128)(2,1)S(1)}, bf16[128,80]{1,0:T(8,128)(2,1)S(1)}, bf16[128,80]{1,0:T(8,128)(2,1)S(1)}, bf16[512,1024]{1,0:T(8,128)(2,1)S(1...) custom-call(s32[6,80]{1,0:T(8,128)S(1)} %bitcast.23, ...), custom_call_target="tpu_custom_call" | custom-call | flops 1000 | bytes 20000000 | tf_op jit(solution)/shard_map/routing/pallas_call | solution.py:47
  36.6 0.0 collective-permute-done.4.refs_0_
  36.6 0.0 collective-permute-done.5.refs_1_
  36.7 0.0 collective-permute-done.6.refs_2_
  36.7 0.6 prepare.1
  37.2 1.9 %experts_3.1 = (bf16[36,2944]{1,0:T(8,128)(2,1)S(1)}, f32[4,4,2944]{2,1,0:T(4,128)S(1)}) custom-call(bf16[144,1024]{1,0:T(8,128)(2,1)S(1)} %get-tuple-element.33.gate_ref, bf16[144,1024]{1,0:T(8,128)(2,1)S(1)} %get-tuple-element.34.up_ref, bf16[144,128]{1,0:T(8,128)(2,1)S(1)} %get-tuple-element.35.side_ref, ...), custom_call_target="tpu_custom_call" | custom-call | flops 1000 | bytes 100000 | tf_op jit(solution)/shard_map/experts_3/pallas_call | solution.py:47
  39.2 1.6 %collective-permute-start.7 = (bf16[36,2944]{1,0:T(8,128)(2,1)S(1)}, bf16[36,2944]{1,0:T(8,128)(2,1)S(1)}, u32[]{:S(2)}, u32[]{:S(2)}) collective-permute-start(bf16[36,2944]{1,0:T(8,128)(2,1)S(1)} %get-tuple-element.40), channel_id=1, source_target_pairs={{0,8},{8,0},{16,24},{24,16},{1,9},{9,1},{17,25},{25,17},{2,10},{10... | collective-permute-start | bytes 635912 | tf_op jit(solution)/shard_map/ppermute | solution.py:63
  40.8 1.3 %experts_1.1.refs_1_.later_ref = bf16[36,2944]{1,0:T(8,128)(2,1)S(1)} custom-call(bf16[144,1024]{1,0:T(8,128)(2,1)S(1)} %get-tuple-element.33.gate_ref, bf16[144,1024]{1,0:T(8,128)(2,1)S(1)} %get-tuple-element.34.up_ref, bf16[144,128]{1,0:T(8,128)(2,1)S(1)} %get-tuple-element.35.side_ref, bf16[2,512,2,1408]{3,2,1,0:T(2,128)(2,1)S(1)} %get-tuple-element.39.weight_ref, ...), custom_call_target="tpu_custom_call" | custom-call | flops 1000 | bytes 100000 | tf_op jit(solution)/shard_map/experts_1/pallas_call | solution.py:47
  42.1 1.3 %experts_2.1.own_ref = bf16[36,2944]{1,0:T(8,128)(2,1)S(1)} custom-call(bf16[144,1024]{1,0:T(8,128)(2,1)S(1)} %get-tuple-element.33.gate_ref, bf16[144,1024]{1,0:T(8,128)(2,1)S(1)} %get-tuple-element.34.up_ref, bf16[144,128]{1,0:T(8,128)(2,1)S(1)} %get-tuple-element.35.side_ref, bf16[2,512,2,1408]{3,2,1,0:T(2,128)(2,1)S(1)} %get-tuple-element.38.weight_ref, ...), custom_call_target="tpu_custom_call" | custom-call | flops 1000 | bytes 100000 | tf_op jit(solution)/shard_map/experts_2/pallas_call | solution.py:47
  43.4 3.0 %collective-permute-done.7.received_ref = bf16[36,2944]{1,0:T(8,128)(2,1)S(1)} collective-permute-done((bf16[36,2944]{1,0:T(8,128)(2,1)S(1)}, bf16[36,2944]{1,0:T(8,128)(2,1)S(1)}, u32[]{:S(2)}, u32[]{:S(2)}) %collective-permute-start.7) | collective-permute-done | bytes 212000 | tf_op jit(solution)/shard_map/ppermute | solution.py:63
  46.5 0.1 add_pair.1
  46.5 1.5 %collective-permute-start.9 = (bf16[36,2944]{1,0:T(8,128)(2,1)S(1)}, bf16[36,2944]{1,0:T(8,128)(2,1)S(1)}, u32[]{:S(2)}, u32[]{:S(2)}) collective-permute-start(bf16[36,2944]{1,0:T(8,128)(2,1)S(1)} %get-tuple-element.42), channel_id=1, source_target_pairs={{0,8},{8,0},{16,24},{24,16},{1,9},{9,1},{17,25},{25,17},{2,10},{10... | collective-permute-start | bytes 635912 | tf_op jit(solution)/shard_map/ppermute | solution.py:63
  48.0 2.7 %collective-permute-start.8 = (bf16[36,2944]{1,0:T(8,128)(2,1)S(1)}, bf16[36,2944]{1,0:T(8,128)(2,1)S(1)}, u32[]{:S(2)}, u32[]{:S(2)}) collective-permute-start(bf16[36,2944]{1,0:T(8,128)(2,1)S(1)} %get-tuple-element.41.refs_1_), channel_id=1, source_target_pairs={{0,16},{8,24},{16,0},{24,8},{1,17},{9,25},{17,1},{25,9},{2,18},{10... | collective-permute-start | bytes 635912 | tf_op jit(solution)/shard_map/ppermute | solution.py:63
  50.7 4.5 %experts_0.1.refs_0_ = bf16[36,2944]{1,0:T(8,128)(2,1)S(1)} custom-call(bf16[144,1024]{1,0:T(8,128)(2,1)S(1)} %get-tuple-element.33.gate_ref, bf16[144,1024]{1,0:T(8,128)(2,1)S(1)} %get-tuple-element.34.up_ref, bf16[144,128]{1,0:T(8,128)(2,1)S(1)} %get-tuple-element.35.side_ref, bf16[8,512,2,1408]{3,2,1,0:T(2,128)(2,1)} %weight_ref.9, ...), custom_call_target="tpu_custom_call" | custom-call | flops 1000 | bytes 100000 | tf_op jit(solution)/shard_map/experts_0/pallas_call | solution.py:47
  55.3 2.5 %collective-permute-done.9.refs_2_ = bf16[36,2944]{1,0:T(8,128)(2,1)S(1)} collective-permute-done((bf16[36,2944]{1,0:T(8,128)(2,1)S(1)}, bf16[36,2944]{1,0:T(8,128)(2,1)S(1)}, u32[]{:S(2)}, u32[]{:S(2)}) %collective-permute-start.9) | collective-permute-done | bytes 212000 | tf_op jit(solution)/shard_map/ppermute | solution.py:63
  57.7 2.5 %collective-permute-done.8.refs_1_ = bf16[36,2944]{1,0:T(8,128)(2,1)S(1)} collective-permute-done((bf16[36,2944]{1,0:T(8,128)(2,1)S(1)}, bf16[36,2944]{1,0:T(8,128)(2,1)S(1)}, u32[]{:S(2)}, u32[]{:S(2)}) %collective-permute-start.8) | collective-permute-done | bytes 212000 | tf_op jit(solution)/shard_map/ppermute | solution.py:63
  60.2 0.2 hidden.1.hidden_ref.refs_0_
  60.4 0.2 collective-permute-start.11
  60.6 2.8 %collective-permute-start.10 = (bf16[36,1408]{1,0:T(8,128)(2,1)S(1)}, bf16[36,1408]{1,0:T(8,128)(2,1)S(1)}, u32[]{:S(2)}, u32[]{:S(2)}) collective-permute-start(bf16[36,1408]{1,0:T(8,128)(2,1)S(1)} %hidden.1.hidden_ref.refs_0_), channel_id=1, source_target_pairs={{0,8},{8,0},{16,24},{24,16},{1,9},{9,1},{17,25},{25,17},{2,10},{10... | collective-permute-start | bytes 304136 | tf_op jit(solution)/shard_map/ppermute | solution.py:63
  63.4 1.5 %collective-permute-start.12 = (bf16[36,1408]{1,0:T(8,128)(2,1)S(1)}, bf16[36,1408]{1,0:T(8,128)(2,1)S(1)}, u32[]{:S(2)}, u32[]{:S(2)}) collective-permute-start(bf16[36,1408]{1,0:T(8,128)(2,1)S(1)} %hidden.1.hidden_ref.refs_0_), channel_id=1, source_target_pairs={{0,24},{8,16},{16,8},{24,0},{1,25},{9,17},{17,9},{25,1},{2,26},{10... | collective-permute-start | bytes 304136 | tf_op jit(solution)/shard_map/ppermute | solution.py:63
  64.9 0.0 slice-done.1
  64.9 0.5 down_0.1.refs_4_
  65.4 2.0 %collective-permute-done.11.hidden_ref.refs_2_ = bf16[36,1408]{1,0:T(8,128)(2,1)S(1)} collective-permute-done((bf16[36,1408]{1,0:T(8,128)(2,1)S(1)}, bf16[36,1408]{1,0:T(8,128)(2,1)S(1)}, u32[]{:S(2)}, u32[]{:S(2)}) %collective-permute-start.11) | collective-permute-done | bytes 101408 | tf_op jit(solution)/shard_map/ppermute | solution.py:63
  67.4 0.5 down_2.1.refs_6_
  67.9 0.0 collective-permute-done.10.hidden_ref.refs_1_
  67.9 0.0 slice-start.3
  67.9 0.5 down_1.1.refs_5_
  68.4 1.5 %collective-permute-done.12.refs_3_ = bf16[36,1408]{1,0:T(8,128)(2,1)S(1)} collective-permute-done((bf16[36,1408]{1,0:T(8,128)(2,1)S(1)}, bf16[36,1408]{1,0:T(8,128)(2,1)S(1)}, u32[]{:S(2)}, u32[]{:S(2)}) %collective-permute-start.12) | collective-permute-done | bytes 101408 | tf_op jit(solution)/shard_map/ppermute | solution.py:63
  69.9 0.9 %combine.1 = (bf16[8,10,512]{2,1,0:T(8,128)(2,1)S(1)}, f32[4,4,512]{2,1,0:T(4,128)S(1)}) custom-call(bf16[128,80]{1,0:T(8,128)(2,1)S(1)} %get-tuple-element.26.coarse_ref, bf16[128,80]{1,0:T(8,128)(2,1)S(1)} %get-tuple-element.27.fine_ref, bf16[8,1408,512]{2,1,0:T(8,128)(2,1)S(1)} %bitcast.9, bf16[1,1408,512]{2,1,0:T(8,128)(2,1)S(1)} %copy-done.3, ...), custom_call_target="tpu_custom_call" | custom-call | flops 1000 | bytes 100000 | tf_op jit(solution)/shard_map/combine/pallas_call | solution.py:47
  70.8 8.1 %all_to_all.5.pieces_ref = bf16[8,10,512]{2,1,0:T(8,128)(2,1)S(1)} all-to-all(bf16[8,10,512]{2,1,0:T(8,128)(2,1)S(1)} %get-tuple-element.43), channel_id=1, replica_groups=mesh['head'=4,'pool'=8] {'pool'}, dimensions={0} | all-to-all | bytes 163840 | tf_op jit(solution)/shard_map/all_to_all | solution.py:640
  78.9 1.9 %collective-permute-start.15 = (bf16[10,512]{1,0:T(8,128)(2,1)S(1)}, bf16[10,512]{1,0:T(8,128)(2,1)S(1)}, u32[]{:S(2)}, u32[]{:S(2)}) collective-permute-start(bf16[10,512]{1,0:T(8,128)(2,1)S(1)} %block.1.refs_0_.refs_3_), channel_id=1, source_target_pairs={{0,24},{8,16},{16,8},{24,0},{1,25},{9,17},{17,9},{25,1},{2,26},{10... | collective-permute-start | bytes 30728 | tf_op jit(solution)/shard_map/ppermute | solution.py:63
  80.8 0.0 collective-permute-start.14
  80.8 2.6 %collective-permute-start.13 = (bf16[10,512]{1,0:T(8,128)(2,1)S(1)}, bf16[10,512]{1,0:T(8,128)(2,1)S(1)}, u32[]{:S(2)}, u32[]{:S(2)}) collective-permute-start(bf16[10,512]{1,0:T(8,128)(2,1)S(1)} %block.1.refs_0_.refs_3_), channel_id=1, source_target_pairs={{0,8},{8,0},{16,24},{24,16},{1,9},{9,1},{17,25},{25,17},{2,10},{10... | collective-permute-start | bytes 30728 | tf_op jit(solution)/shard_map/ppermute | solution.py:63
  83.4 0.0 copy-done.8
  83.4 0.3 project_own.1
  83.7 0.8 collective-permute-done.15.refs_2_
  84.5 0.9 %collective-permute-done.14.refs_1_ = bf16[10,512]{1,0:T(8,128)(2,1)S(1)} collective-permute-done((bf16[10,512]{1,0:T(8,128)(2,1)S(1)}, bf16[10,512]{1,0:T(8,128)(2,1)S(1)}, u32[]{:S(2)}, u32[]{:S(2)}) %collective-permute-start.14) | collective-permute-done | bytes 10272 | tf_op jit(solution)/shard_map/ppermute | solution.py:63
  85.4 0.0 collective-permute-done.13.refs_0_
  85.4 1.4 %project.1 = (bf16[10,2048]{1,0:T(8,128)(2,1)}, bf16[10,1536]{1,0:T(8,128)(2,1)}) custom-call(bf16[16,128]{1,0:T(8,128)(2,1)S(1)} %bitcast.21, bf16[2048,1536]{1,0:T(8,128)(2,1)S(1)} %bitcast.11, bf16[10,512]{1,0:T(8,128)(2,1)S(1)} %collective-permute-done.13.refs_0_, bf16[10,512]{1,0:T(8,128)(2,1)S(1)} %collective-permute-done.14.refs_1_, ...), custom_call_target="tpu_custom_call" | custom-call | flops 1000 | bytes 100000 | tf_op jit(solution)/shard_map/project/pallas_call | solution.py:47
  (28 shorter events, 0.1 us)
Async XLA Ops:
  0.6 6.9 %collective-permute-start.2 = (bf16[1,10,512]{2,1,0:T(8,128)(2,1)}, bf16[1,10,512]{2,1,0:T(8,128)(2,1)S(1)}, u32[]{:S(2)}, u32[]{:S(2)}) collective-permute-start(bf16[1,10,512]{2,1,0:T(8,128)(2,1)} %bitcast.15), channel_id=1, source_target_pairs={{0,6},{1,7},{2,4},{3,5},{4,2},{5,3},{6,0},{7,1},{8,14},{9,15},{10,... | collective-permute-start | bytes 30728 | tf_op jit(solution)/shard_map/ppermute | solution.py:63
  4.6 3.9 %collective-permute-start.1 = (bf16[1,10,512]{2,1,0:T(8,128)(2,1)}, bf16[1,10,512]{2,1,0:T(8,128)(2,1)S(1)}, u32[]{:S(2)}, u32[]{:S(2)}) collective-permute-start(bf16[1,10,512]{2,1,0:T(8,128)(2,1)} %bitcast.16), channel_id=1, source_target_pairs={{0,4},{1,5},{2,6},{3,7},{4,0},{5,1},{6,2},{7,3},{8,12},{9,13},{10,... | collective-permute-start | bytes 30728 | tf_op jit(solution)/shard_map/ppermute | solution.py:63
  5.1 3.9 %collective-permute-start = (bf16[1,10,512]{2,1,0:T(8,128)(2,1)}, bf16[1,10,512]{2,1,0:T(8,128)(2,1)S(1)}, u32[]{:S(2)}, u32[]{:S(2)}) collective-permute-start(bf16[1,10,512]{2,1,0:T(8,128)(2,1)} %bitcast.17), channel_id=1, source_target_pairs={{0,2},{1,3},{2,0},{3,1},{4,6},{5,7},{6,4},{7,5},{8,10},{9,11},{10,... | collective-permute-start | bytes 30728 | tf_op jit(solution)/shard_map/ppermute | solution.py:63
  5.2 0.8 copy-start.5
  5.2 0.8 copy-start.12
  5.2 3.8 %copy-start.7 = (bf16[10,512]{1,0:T(8,128)(2,1)S(1)}, bf16[10,512]{1,0:T(8,128)(2,1)}, u32[]{:S(2)}) copy-start(bf16[10,512]{1,0:T(8,128)(2,1)} %param.16) | copy-start | bytes 30724
  5.2 5.1 %copy-start = (bf16[36,2,64,512]{3,2,1,0:T(8,128)(2,1)S(1)}, bf16[36,2,64,512]{3,2,1,0:T(8,128)(2,1)}, u32[]{:S(2)}) copy-start(bf16[36,2,64,512]{3,2,1,0:T(8,128)(2,1)} %cache_ref.1) | copy-start | bytes 14155780
  5.2 5.1 %copy-start.4 = (bf16[10,2048]{1,0:T(8,128)(2,1)S(1)}, bf16[10,2048]{1,0:T(8,128)(2,1)}, u32[]{:S(2)}) copy-start(bf16[10,2048]{1,0:T(8,128)(2,1)} %residual_ref.1) | copy-start | bytes 122884
  5.3 5.1 %copy-start.6 = (bf16[10,2,512]{2,1,0:T(2,128)(2,1)S(1)}, bf16[10,2,512]{2,1,0:T(2,128)(2,1)}, u32[]{:S(2)}) copy-start(bf16[10,2,512]{2,1,0:T(2,128)(2,1)} %fresh_ref.1) | copy-start | bytes 61444
  6.0 17.9 %copy-start.2 = (bf16[512,2048]{1,0:T(8,128)(2,1)S(1)}, bf16[512,2048]{1,0:T(8,128)(2,1)}, u32[]{:S(2)}) copy-start(bf16[512,2048]{1,0:T(8,128)(2,1)} %weight_ref.8) | copy-start | bytes 6291460
  6.0 23.8 %copy-start.10 = (s32[80,6]{0,1:T(8,128)S(1)}, s32[80,6]{0,1:T(8,128)}, u32[]{:S(2)}) copy-start(s32[80,6]{0,1:T(8,128)} %param.24) | copy-start | bytes 5764
  6.0 23.8 %copy-start.11 = (f32[80,6]{0,1:T(8,128)S(1)}, f32[80,6]{0,1:T(8,128)}, u32[]{:S(2)}) copy-start(f32[80,6]{0,1:T(8,128)} %param.25) | copy-start | bytes 5764
  9.1 1.3 %collective-permute-start.3 = (bf16[4,10,512]{2,1,0:T(8,128)(2,1)S(1)}, bf16[4,10,512]{2,1,0:T(8,128)(2,1)S(1)}, u32[]{:S(2)}, u32[]{:S(2)}) collective-permute-start(bf16[4,10,512]{2,1,0:T(8,128)(2,1)S(1)} %join_queries.1.refs_0_), channel_id=1, source_target_pairs={{0,1},{1,0},{2,3},{3,2},{4,5},{5,4},{6,7},{7,6},{8,9},{9,8},{10,11... | collective-permute-start | bytes 122888 | tf_op jit(solution)/shard_map/ppermute | solution.py:63
  25.4 11.3 %collective-permute-start.4 = (bf16[80,512]{1,0:T(8,128)(2,1)S(1)}, bf16[80,512]{1,0:T(8,128)(2,1)S(1)}, u32[]{:S(2)}, u32[]{:S(2)}) collective-permute-start(bf16[80,512]{1,0:T(8,128)(2,1)S(1)} %get-tuple-element.30), channel_id=1, source_target_pairs={{0,8},{8,0},{16,24},{24,16},{1,9},{9,1},{17,25},{25,17},{2,10},{10... | collective-permute-start | bytes 245768 | tf_op jit(solution)/shard_map/ppermute | solution.py:63
  27.0 9.6 %collective-permute-start.5 = (bf16[80,512]{1,0:T(8,128)(2,1)S(1)}, bf16[80,512]{1,0:T(8,128)(2,1)S(1)}, u32[]{:S(2)}, u32[]{:S(2)}) collective-permute-start(bf16[80,512]{1,0:T(8,128)(2,1)S(1)} %get-tuple-element.31), channel_id=1, source_target_pairs={{0,16},{8,24},{16,0},{24,8},{1,17},{9,25},{17,1},{25,9},{2,18},{10... | collective-permute-start | bytes 245768 | tf_op jit(solution)/shard_map/ppermute | solution.py:63
  29.6 7.1 %collective-permute-start.6 = (bf16[80,512]{1,0:T(8,128)(2,1)S(1)}, bf16[80,512]{1,0:T(8,128)(2,1)S(1)}, u32[]{:S(2)}, u32[]{:S(2)}) collective-permute-start(bf16[80,512]{1,0:T(8,128)(2,1)S(1)} %get-tuple-element.32), channel_id=1, source_target_pairs={{0,24},{8,16},{16,8},{24,0},{1,25},{9,17},{17,9},{25,1},{2,26},{10... | collective-permute-start | bytes 245768 | tf_op jit(solution)/shard_map/ppermute | solution.py:63
  29.8 6.8 %copy-start.9 = (bf16[2048]{0:T(1024)(128)(2,1)S(1)}, bf16[2048]{0:T(1024)(128)(2,1)}, u32[]{:S(2)}) copy-start(bf16[2048]{0:T(1024)(128)(2,1)} %param.23) | copy-start | bytes 12292
  29.8 7.4 %copy-start.1 = (bf16[1,512,2,1408]{3,2,1,0:T(2,128)(2,1)S(1)}, bf16[1,512,2,1408]{3,2,1,0:T(2,128)(2,1)}, u32[]{:S(2)}) copy-start(bf16[1,512,2,1408]{3,2,1,0:T(2,128)(2,1)} %refs_0_.1) | copy-start | bytes 8650756
  39.2 7.3 %collective-permute-start.7 = (bf16[36,2944]{1,0:T(8,128)(2,1)S(1)}, bf16[36,2944]{1,0:T(8,128)(2,1)S(1)}, u32[]{:S(2)}, u32[]{:S(2)}) collective-permute-start(bf16[36,2944]{1,0:T(8,128)(2,1)S(1)} %get-tuple-element.40), channel_id=1, source_target_pairs={{0,8},{8,0},{16,24},{24,16},{1,9},{9,1},{17,25},{25,17},{2,10},{10... | collective-permute-start | bytes 635912 | tf_op jit(solution)/shard_map/ppermute | solution.py:63
  46.5 11.2 %collective-permute-start.9 = (bf16[36,2944]{1,0:T(8,128)(2,1)S(1)}, bf16[36,2944]{1,0:T(8,128)(2,1)S(1)}, u32[]{:S(2)}, u32[]{:S(2)}) collective-permute-start(bf16[36,2944]{1,0:T(8,128)(2,1)S(1)} %get-tuple-element.42), channel_id=1, source_target_pairs={{0,8},{8,0},{16,24},{24,16},{1,9},{9,1},{17,25},{25,17},{2,10},{10... | collective-permute-start | bytes 635912 | tf_op jit(solution)/shard_map/ppermute | solution.py:63
  48.0 16.9 %slice-start = ((s8[11534336]{0:T(1024)(128)(4,1)}), s8[4194304]{0:T(1024)(128)(4,1)S(1)}, s32[]{:S(2)}) async-start(s8[11534336]{0:T(1024)(128)(4,1)} %bitcast.8), calls=%async_computation.1 | async-start | bytes 8388608
  48.0 16.9 %slice-start.1 = ((s8[11534336]{0:T(1024)(128)(4,1)}), s8[4194304]{0:T(1024)(128)(4,1)S(1)}, s32[]{:S(2)}) async-start(s8[11534336]{0:T(1024)(128)(4,1)} %bitcast.8), calls=%async_computation.2 | async-start | bytes 8388608
  48.0 16.9 %slice-start.2 = ((s8[11534336]{0:T(1024)(128)(4,1)}), s8[3145728]{0:T(1024)(128)(4,1)S(1)}, s32[]{:S(2)}) async-start(s8[11534336]{0:T(1024)(128)(4,1)} %bitcast.8), calls=%async_computation.3 | async-start | bytes 6291456
  48.0 12.2 %collective-permute-start.8 = (bf16[36,2944]{1,0:T(8,128)(2,1)S(1)}, bf16[36,2944]{1,0:T(8,128)(2,1)S(1)}, u32[]{:S(2)}, u32[]{:S(2)}) collective-permute-start(bf16[36,2944]{1,0:T(8,128)(2,1)S(1)} %get-tuple-element.41.refs_1_), channel_id=1, source_target_pairs={{0,16},{8,24},{16,0},{24,8},{1,17},{9,25},{17,1},{25,9},{2,18},{10... | collective-permute-start | bytes 635912 | tf_op jit(solution)/shard_map/ppermute | solution.py:63
  60.4 7.0 %collective-permute-start.11 = (bf16[36,1408]{1,0:T(8,128)(2,1)S(1)}, bf16[36,1408]{1,0:T(8,128)(2,1)S(1)}, u32[]{:S(2)}, u32[]{:S(2)}) collective-permute-start(bf16[36,1408]{1,0:T(8,128)(2,1)S(1)} %hidden.1.hidden_ref.refs_0_), channel_id=1, source_target_pairs={{0,16},{8,24},{16,0},{24,8},{1,17},{9,25},{17,1},{25,9},{2,18},{10... | collective-permute-start | bytes 304136 | tf_op jit(solution)/shard_map/ppermute | solution.py:63
  60.6 7.3 %collective-permute-start.10 = (bf16[36,1408]{1,0:T(8,128)(2,1)S(1)}, bf16[36,1408]{1,0:T(8,128)(2,1)S(1)}, u32[]{:S(2)}, u32[]{:S(2)}) collective-permute-start(bf16[36,1408]{1,0:T(8,128)(2,1)S(1)} %hidden.1.hidden_ref.refs_0_), channel_id=1, source_target_pairs={{0,8},{8,0},{16,24},{24,16},{1,9},{9,1},{17,25},{25,17},{2,10},{10... | collective-permute-start | bytes 304136 | tf_op jit(solution)/shard_map/ppermute | solution.py:63
  63.4 6.6 %collective-permute-start.12 = (bf16[36,1408]{1,0:T(8,128)(2,1)S(1)}, bf16[36,1408]{1,0:T(8,128)(2,1)S(1)}, u32[]{:S(2)}, u32[]{:S(2)}) collective-permute-start(bf16[36,1408]{1,0:T(8,128)(2,1)S(1)} %hidden.1.hidden_ref.refs_0_), channel_id=1, source_target_pairs={{0,24},{8,16},{16,8},{24,0},{1,25},{9,17},{17,9},{25,1},{2,26},{10... | collective-permute-start | bytes 304136 | tf_op jit(solution)/shard_map/ppermute | solution.py:63
  67.9 2.0 %copy-start.3 = (bf16[1,1408,512]{2,1,0:T(8,128)(2,1)S(1)}, bf16[1,1408,512]{2,1,0:T(8,128)(2,1)}, u32[]{:S(2)}) copy-start(bf16[1,1408,512]{2,1,0:T(8,128)(2,1)} %shared_weight_ref.1) | copy-start | bytes 4325380
  67.9 15.5 %slice-start.3 = ((s8[6291456]{0:T(1024)(128)(4,1)}), s8[4194304]{0:T(1024)(128)(4,1)S(1)}, s32[]{:S(2)}) async-start(s8[6291456]{0:T(1024)(128)(4,1)} %bitcast.10), calls=%async_computation.4 | async-start | bytes 8388608
  69.9 13.4 %slice-start.4 = ((s8[6291456]{0:T(1024)(128)(4,1)}), s8[2097152]{0:T(1024)(128)(4,1)S(1)}, s32[]{:S(2)}) async-start(s8[6291456]{0:T(1024)(128)(4,1)} %bitcast.10), calls=%async_computation.5 | async-start | bytes 4194304
  69.9 13.4 %copy-start.8 = (bf16[2048]{0:T(1024)(128)(2,1)S(1)}, bf16[2048]{0:T(1024)(128)(2,1)}, u32[]{:S(2)}) copy-start(bf16[2048]{0:T(1024)(128)(2,1)} %param.30) | copy-start | bytes 12292
  78.9 5.6 %collective-permute-start.15 = (bf16[10,512]{1,0:T(8,128)(2,1)S(1)}, bf16[10,512]{1,0:T(8,128)(2,1)S(1)}, u32[]{:S(2)}, u32[]{:S(2)}) collective-permute-start(bf16[10,512]{1,0:T(8,128)(2,1)S(1)} %block.1.refs_0_.refs_3_), channel_id=1, source_target_pairs={{0,24},{8,16},{16,8},{24,0},{1,25},{9,17},{17,9},{25,1},{2,26},{10... | collective-permute-start | bytes 30728 | tf_op jit(solution)/shard_map/ppermute | solution.py:63
  80.8 4.6 %collective-permute-start.14 = (bf16[10,512]{1,0:T(8,128)(2,1)S(1)}, bf16[10,512]{1,0:T(8,128)(2,1)S(1)}, u32[]{:S(2)}, u32[]{:S(2)}) collective-permute-start(bf16[10,512]{1,0:T(8,128)(2,1)S(1)} %block.1.refs_0_.refs_3_), channel_id=1, source_target_pairs={{0,16},{8,24},{16,0},{24,8},{1,17},{9,25},{17,1},{25,9},{2,18},{10... | collective-permute-start | bytes 30728 | tf_op jit(solution)/shard_map/ppermute | solution.py:63
  80.8 4.6 %collective-permute-start.13 = (bf16[10,512]{1,0:T(8,128)(2,1)S(1)}, bf16[10,512]{1,0:T(8,128)(2,1)S(1)}, u32[]{:S(2)}, u32[]{:S(2)}) collective-permute-start(bf16[10,512]{1,0:T(8,128)(2,1)S(1)} %block.1.refs_0_.refs_3_), channel_id=1, source_target_pairs={{0,8},{8,0},{16,24},{24,16},{1,9},{9,1},{17,25},{25,17},{2,10},{10... | collective-permute-start | bytes 30728 | tf_op jit(solution)/shard_map/ppermute | solution.py:63

commit v4 on v3

--- a/solution.py
+++ b/solution.py
@@ -18,6 +18,7 @@
 
 epsilon = 1e-06
 floor_score = -1e30
+least_score = -1e29
 bf16 = jnp.bfloat16
 f32 = jnp.float32
 over_rows = (((0,), (0,)), ((), ()))
@@ -127,13 +128,14 @@
     pools, req_dev, lane_width = queries_ref.shape
     req_total = pools * req_dev
     tokens = blocks * block_len
-    scale = 1.0 / math.sqrt(HD)
+    scale = math.log2(math.e) / math.sqrt(HD)
     bias = bias_ref[...]
     pieces = [ref[i] for ref in query_refs for i in range(ref.shape[0])]
     for distance, piece in zip(order, pieces):
         queries_ref[pool_idx ^ distance] = piece.astype(f32)
     queries = jnp.concatenate([queries_ref[i] for i in range(pools)], axis=0).astype(bf16)
     own = iota((req_total, req_dev), 0) == iota((req_total, req_dev), 1) + pool_idx * req_dev
+    own_bias = jnp.where(own, 0.0, floor_score)
     lane = iota((req_total, LANES), 1)
     side = jnp.zeros((req_total, LANES), f32)
     heads = lane_width // HD
@@ -142,19 +144,18 @@
         columns = slice(head * HD, (head + 1) * HD)
         query = queries[:, columns]
         keys = cache_ref[:, 0, :, columns].reshape(tokens, HD)
-        scores = lax.dot_general(query, keys, contract, preferred_element_type=f32) * scale
-        scores = jnp.where(bias < 0.0, floor_score, scores)
+        scores = lax.dot_general(query, keys, contract, preferred_element_type=f32) * scale + bias
         new_scores = (
             lax.dot_general(query, fresh_ref[:, 0, columns], contract, preferred_element_type=f32)
             * scale
-        )
-        new_scores = jnp.where(own, new_scores, floor_score)
+            + own_bias
+        )
         top = jnp.maximum(
             jnp.max(scores, axis=1, keepdims=True), jnp.max(new_scores, axis=1, keepdims=True)
         )
-        top = top.astype(bf16).astype(f32)
-        weights = jnp.where(bias < 0.0, 0.0, jnp.exp(scores - top))
-        new_weights = jnp.where(own, jnp.exp(new_scores - top), 0.0)
+        top = jnp.maximum(top, least_score).astype(bf16).astype(f32)
+        weights = jnp.exp2(scores - top)
+        new_weights = jnp.exp2(new_scores - top)
         total = jnp.sum(weights, axis=1, keepdims=True) + jnp.sum(
             new_weights, axis=1, keepdims=True
         )
@@ -183,24 +184,32 @@
     lane_width = packed - LANES
     heads = lane_width // HD
     me = lax.axis_index("head")
+    sides = [parts_ref[i, :, lane_width:].astype(f32) for i in range(count)]
     lane = iota((req_total, LANES), 1)
-    sides = [parts_ref[i, :, lane_width:].astype(f32) for i in range(count)]
-
-    def column(side, place):
-        return jnp.sum(jnp.where(lane == place, side, 0.0), axis=1, keepdims=True)
-
-    for head in range(heads):
-        columns = slice(head * HD, (head + 1) * HD)
-        tops = [column(side, head) for side in sides]
-        totals = [column(side, heads + head) + column(side, 2 * heads + head) for side in sides]
-        top = functools.reduce(jnp.maximum, tops)
-        shares = [total * jnp.exp(part - top) for part, total in zip(tops, totals)]
-        denominator = functools.reduce(jnp.add, shares)
-        mixed = functools.reduce(
-            jnp.add,
-            [shares[i] * parts_ref[i, :, columns].astype(f32) for i in range(count)],
-        )
-        attended_ref[:, columns] = (mixed / denominator).astype(bf16)
+    tops = [jnp.where(lane < heads, side, 0.0) for side in sides]
+    top = functools.reduce(jnp.maximum, tops)
+
+    def shifted(side, by):
+        return pltpu.roll(side, LANES - by, 1)
+
+    shares = [
+        (shifted(side, heads) + shifted(side, 2 * heads)) * jnp.exp2(part - top)
+        for side, part in zip(sides, tops)
+    ]
+    denominator = functools.reduce(jnp.add, shares)
+    inverse = 1.0 / jnp.where(lane < heads, denominator, 1.0)
+    spread = iota((2 * LANES, lane_width), 1) // HD == lax.rem(
+        iota((2 * LANES, lane_width), 0), LANES
+    )
+    spread = one_hot(spread)
+    mixed = jnp.zeros((req_total, lane_width), f32)
+    for i, share in enumerate(shares):
+        share = jnp.where(lane < heads, share * inverse, 0.0)
+        coarse = share.astype(bf16)
+        fine = (share - coarse.astype(f32)).astype(bf16)
+        weight = dot(jnp.concatenate([coarse, fine], axis=1), spread)
+        mixed = mixed + weight * parts_ref[i, :, :lane_width].astype(f32)
+    attended_ref[...] = mixed.astype(bf16)
     for distance, out_ref in enumerate(out_refs):
         start = pl.multiple_of((me ^ distance) * col_part, LANES)
         projected = dot(attended_ref[...], weight_ref[:, pl.ds(start, col_part)])
@@ -293,15 +302,9 @@
     up_ref[...] = pltpu.roll(spread, 1, 1).astype(bf16)
 
 
-def gate_up(lhs, weight, out_ref, rows, side):
-    count, ffe = lhs.shape[0] // 2, weight.shape[1]
-    sums = dot(lhs, weight)
-    out_ref[rows, :ffe] = sums[:count].astype(out_ref.dtype)
-    out_ref[rows, ffe : 2 * ffe] = sums[count:].astype(out_ref.dtype)
-    out_ref[rows, 2 * ffe :] = side.astype(out_ref.dtype)
-
-
-def expert_kernel(distance, slots, gate_ref, up_ref, side_ref, weight_ref, *refs):
+def expert_kernel(
+    distance, slots, part, makes_shared, gate_ref, up_ref, side_ref, weight_ref, *refs
+):
     refs = list(refs)
     head_devs = lax.axis_size("head")
     if distance == 0:
@@ -313,31 +316,31 @@
             copy.wait()
     _, depth, _, ffe = weight_ref.shape
     target = lax.axis_index("head") ^ distance
-    if distance == head_devs - 1:
-        shared_weight_ref, out_ref, shared_ref, all_ref = refs
-        extra, share = all_ref.shape[0], shared_ref.shape[1]
-        first_extra = gate_ref.shape[0] - extra
-        lhs = jnp.concatenate([gate_ref[first_extra:, :], up_ref[first_extra:, :]], axis=0)
-        gate_up(
-            lhs,
-            shared_weight_ref[0].reshape(2 * depth, ffe),
-            all_ref,
-            slice(0, extra),
-            side_ref[first_extra:, :],
-        )
+    if makes_shared:
+        shared_weight_ref, out_ref, shared_ref = refs
+        share = shared_ref.shape[1] // 2
+        extra = share * head_devs
+        first = gate_ref.shape[0] - extra
+        lhs = jnp.concatenate([gate_ref[first:, :], up_ref[first:, :]], axis=0)
+        sums = dot(lhs, shared_weight_ref[0].reshape(2 * depth, ffe))
+        side = side_ref[first:, :].astype(f32)
         for place in range(head_devs):
-            shared_ref[place] = all_ref[place * share : (place + 1) * share, :]
+            rows = slice(place * share, (place + 1) * share)
+            shared_ref[place, :share, :ffe] = sums[:extra][rows]
+            shared_ref[place, share:, :ffe] = sums[extra:][rows]
+            shared_ref[place, :share, ffe:] = side[rows]
+            shared_ref[place, share:, ffe:] = side[rows]
     else:
         shared_ref, out_ref = refs[0], refs[-1]
-        share = shared_ref.shape[1]
-    part = out_ref.shape[0] - share
     each = min(slots, part)
     for i in range(part // each):
         rows = pl.ds(pl.multiple_of(target * part + i * each, TILE), each)
         lhs = jnp.concatenate([gate_ref[rows, :], up_ref[rows, :]], axis=0)
-        weight = weight_ref[i].reshape(2 * depth, ffe)
-        gate_up(lhs, weight, out_ref, slice(i * each, (i + 1) * each), side_ref[rows, :])
-    out_ref[part:, :] = shared_ref[target].astype(bf16)
+        sums = dot(lhs, weight_ref[i].reshape(2 * depth, ffe))
+        out_ref[2 * i * each : 2 * (i + 1) * each, :ffe] = sums.astype(bf16)
+        for k in (2 * i, 2 * i + 1):
+            out_ref[k * each : (k + 1) * each, ffe:] = side_ref[rows, :]
+    out_ref[2 * part :, :] = shared_ref[target].astype(bf16)
 
 
 def add_kernel(own_ref, received_ref, later_ref, out_ref, sent_ref):
@@ -345,18 +348,17 @@
     sent_ref[...] = later_ref[...]
 
 
-def hidden_kernel(width, *refs):
+def hidden_kernel(width, part, each, *refs):
     parts, out_ref = refs[:-1], refs[-1]
     ffe = out_ref.shape[1]
-
-    def total(columns):
-        return functools.reduce(jnp.add, [part[:, columns].astype(f32) for part in parts])
-
-    side = total(slice(2 * ffe, 2 * ffe + LANES))
-    row_scale = lax.rsqrt((side[:, 0:1] + side[:, 1:2]) / width + epsilon)
-    gates = total(slice(0, ffe)) * row_scale
-    ups = total(slice(ffe, 2 * ffe)) * row_scale
-    out_ref[...] = (gates / (1.0 + jnp.exp(-gates)) * ups).astype(bf16)
+    total = functools.reduce(jnp.add, [ref[...].astype(f32) for ref in parts])
+    blocks = [(2 * i * each, i * each, each) for i in range(part // each)]
+    for start, row, count in blocks + [(2 * part, part, out_ref.shape[0] - part)]:
+        gates, ups = total[start : start + count], total[start + count : start + 2 * count]
+        squares = gates[:, ffe : ffe + 1] + gates[:, ffe + 1 : ffe + 2]
+        row_scale = lax.rsqrt(squares / width + epsilon)
+        gates, ups = gates[:, :ffe] * row_scale, ups[:, :ffe] * row_scale
+        out_ref[row : row + count, :] = (gates / (1.0 + jnp.exp(-gates)) * ups).astype(bf16)
 
 
 def down_rows(distance, slots, hidden_ref, weight_ref):
@@ -568,8 +570,9 @@
     )
 
     piece = slot_total // head_devs + extra // head_devs
-    piece_shape = ((piece, 2 * ffe + LANES), bf16)
-    shared_shape = ((head_devs, extra // head_devs, 2 * ffe + LANES), f32)
+    part = slot_total // head_devs
+    piece_shape = ((2 * piece, ffe + LANES), bf16)
+    shared_shape = ((head_devs, 2 * extra // head_devs, ffe + LANES), f32)
     shared_rows = None
     last = head_devs - 1
 
@@ -577,15 +580,14 @@
         nonlocal shared_rows
         args = [gate_rows, up_rows, side, weights.get(distance, w_gate_up)]
         outs, scratch, copies, far = [piece_shape], [], [], []
-        if distance == last:
+        if shared_rows is None:
             args, outs = args + [shared_gate_up], outs + [shared_shape]
-            scratch = [((extra, 2 * ffe + LANES), f32)]
         else:
             args = args + [shared_rows] + list(after)
         if distance == 0:
             scratch, copies, far = [fetch_shape], [piece_experts * SPLIT], [3]
         mine, *shared = call(
-            functools.partial(expert_kernel, distance, slots),
+            functools.partial(expert_kernel, distance, slots, part, len(outs) > 1),
             f"experts_{distance}",
             outs,
             args,
@@ -599,21 +601,24 @@
         return mine
 
     if head_devs == 4:
-        near = swap(experts(3), "head", 1)
+        near = swap(experts(2), "head", 1)
         own_near = experts(1)
         pair, own_near = call(
             add_kernel,
             "add_pair",
             [piece_shape, piece_shape],
-            [experts(2, [own_near]), near, own_near],
-        )
-        far = swap(pair, "head", 2)
+            [experts(3, [own_near]), near, own_near],
+        )
+        far = swap(pair, "head", 3)
         parts = [experts(0, [pair]), far, swap(own_near, "head", 1)]
     else:
         parts = [swap(experts(d), "head", d) for d in reversed(range(1, head_devs))]
         parts = [experts(0)] + parts
     (hidden,) = call(
-        functools.partial(hidden_kernel, width), "hidden", [((piece, ffe), bf16)], parts
+        functools.partial(hidden_kernel, width, part, min(slots, part)),
+        "hidden",
+        [((piece, ffe), bf16)],
+        parts,
     )
     hiddens = {0: hidden}
     for d in distances:

time: 87 us -> 86 us (0.989)
  no operation moved by 1% of the time
where the time goes in v4:
time: 86 us; the launch traced here: 85.7 us
  Pallas kernels  26.3 us (31%)
  starting transfers between devices  24.1 us (28%)
  blocking collectives  18.7 us (22%)
  waiting for transfers between devices  15.5 us (18%)
    pallas_call x20, Pallas kernels, call(): pl.pallas_call(kernel, out_shape=[jax.ShapeDtypeStruct(shape, dtype) for...  26.3 us
    ppermute x16, starting transfers between devices, swap(): return lax.ppermute(value, axis, [(i, i ^ distance) for i in range(count)])  24.1 us
    ppermute x16, waiting for transfers between devices, swap(): return lax.ppermute(value, axis, [(i, i ^ distance) for i in range(count)])  15.5 us
    all_gather x1, blocking collectives, per_device(): parts = lax.all_gather(partial, 'pool', axis=0)  10.7 us
    all_to_all x1, blocking collectives, per_device(): pieces = lax.all_to_all(routed, 'pool', 0, 0)  7.99 us
  transfers between devices with their start and end apart: 16, of which 10 were waited for; matrix products, arithmetic and copies ran while one was open for 0% of the time, Pallas kernels for 21%

profile of v4, /device:TPU:0, one launch (start us, length us, event | category | flops | bytes accessed | tf_op | source)
XLA Modules:
  0.0 85.7 jit_solution(14730769205908239232)
XLA Ops:
  0.6 4.0 %collective-permute-start.2 = (bf16[1,10,512]{2,1,0:T(8,128)(2,1)}, bf16[1,10,512]{2,1,0:T(8,128)(2,1)S(1)}, u32[]{:S(2)}, u32[]{:S(2)}) collective-permute-start(bf16[1,10,512]{2,1,0:T(8,128)(2,1)} %bitcast.15), channel_id=1, source_target_pairs={{0,6},{1,7},{2,4},{3,5},{4,2},{5,3},{6,0},{7,1},{8,14},{9,15},{10,... | collective-permute-start | bytes 30728 | tf_op jit(solution)/shard_map/ppermute | solution.py:64
  4.6 0.5 collective-permute-start.1
  5.1 0.1 collective-permute-start
  5.2 0.0 copy-start.4
  5.3 0.0 copy-start.6
  5.3 0.5 early.1.early_ref
  5.8 0.2 copy-done.5
  6.0 0.0 copy-done.12
  6.0 1.5 %setup.1.bias_ref = f32[80,2304]{1,0:T(8,128)S(1)} custom-call(s32[1]{0:T(128)} %early.1.early_ref, s32[64,80]{1,0:T(8,128)S(1)} %bitcast.14, s32[1,80]{1,0:T(1,128)S(1)} %bitcast.26), custom_call_target="tpu_custom_call" | custom-call | flops 1000 | bytes 100000 | tf_op jit(solution)/shard_map/setup/pallas_call | solution.py:48
  7.6 0.0 collective-permute-done.2.refs_3_
  7.6 1.0 %collective-permute-done.1.refs_2_ = bf16[1,10,512]{2,1,0:T(8,128)(2,1)S(1)} collective-permute-done((bf16[1,10,512]{2,1,0:T(8,128)(2,1)}, bf16[1,10,512]{2,1,0:T(8,128)(2,1)S(1)}, u32[]{:S(2)}, u32[]{:S(2)}) %collective-permute-start.1) | collective-permute-done | bytes 10272 | tf_op jit(solution)/shard_map/ppermute | solution.py:64
  8.5 0.5 collective-permute-done.refs_1_
  9.0 0.0 copy-done.7
  9.1 0.1 collective-permute-start.3
  9.1 1.2 %collective-permute-done.3.refs_1_ = bf16[4,10,512]{2,1,0:T(8,128)(2,1)S(1)} collective-permute-done((bf16[4,10,512]{2,1,0:T(8,128)(2,1)S(1)}, bf16[4,10,512]{2,1,0:T(8,128)(2,1)S(1)}, u32[]{:S(2)}, u32[]{:S(2)}) %collective-permute-start.3) | collective-permute-done | bytes 40992 | tf_op jit(solution)/shard_map/ppermute | solution.py:64
  10.4 0.0 copy-done
  10.4 2.4 %attention.1 = bf16[80,640]{1,0:T(8,128)(2,1)S(1)} custom-call(bf16[36,2,64,512]{3,2,1,0:T(8,128)(2,1)S(1)} %copy-done, f32[80,2304]{1,0:T(8,128)S(1)} %setup.1.bias_ref, bf16[10,2,512]{2,1,0:T(2,128)(2,1)S(1)} %copy-done.6, bf16[10,2048]{1,0:T(8,128)(2,1)S(1)} %copy-done.4, bf16[4,10,512]{2,1,0:T(8,128)(2,1)S(1)} %join_queries.1.refs_0_, ...), custom_call_target="tpu_custom_call" | custom-call | flops 1000 | bytes 100000 | tf_op jit(solution)/shard_map/attention/pallas_call | solution.py:48
  12.8 10.7 %all-gather = bf16[640,640]{1,0:T(8,128)(2,1)S(1)} all-gather(bf16[80,640]{1,0:T(8,128)(2,1)S(1)} %attention.1), channel_id=2, replica_groups=mesh['head'=4,'pool'=8] {'pool'}, dimensions={0}, use_global_device_ids=true | all-gather | bytes 921600 | tf_op jit(solution)/shard_map/all_gather | solution.py:531
  23.5 0.0 copy-done.2
  23.5 1.0 %merge_project.1 = (f32[80,512]{1,0:T(8,128)S(1)}, bf16[80,512]{1,0:T(8,128)(2,1)S(1)}, bf16[80,512]{1,0:T(8,128)(2,1)S(1)}, bf16[80,512]{1,0:T(8,128)(2,1)S(1)}) custom-call(bf16[8,80,640]{2,1,0:T(8,128)(2,1)S(1)} %bitcast.12, bf16[512,2048]{1,0:T(8,128)(2,1)S(1)} %copy-done.2), custom_call_target="tpu_custom_call" | custom-call | flops 1000 | bytes 100000 | tf_op jit(solution)/shard_map/merge_project/pallas_call | solution.py:48
  24.5 1.6 %collective-permute-start.4 = (bf16[80,512]{1,0:T(8,128)(2,1)S(1)}, bf16[80,512]{1,0:T(8,128)(2,1)S(1)}, u32[]{:S(2)}, u32[]{:S(2)}) collective-permute-start(bf16[80,512]{1,0:T(8,128)(2,1)S(1)} %get-tuple-element.30), channel_id=1, source_target_pairs={{0,8},{8,0},{16,24},{24,16},{1,9},{9,1},{17,25},{25,17},{2,10},{10... | collective-permute-start | bytes 245768 | tf_op jit(solution)/shard_map/ppermute | solution.py:64
  26.1 2.6 %collective-permute-start.5 = (bf16[80,512]{1,0:T(8,128)(2,1)S(1)}, bf16[80,512]{1,0:T(8,128)(2,1)S(1)}, u32[]{:S(2)}, u32[]{:S(2)}) collective-permute-start(bf16[80,512]{1,0:T(8,128)(2,1)S(1)} %get-tuple-element.31), channel_id=1, source_target_pairs={{0,16},{8,24},{16,0},{24,8},{1,17},{9,25},{17,1},{25,9},{2,18},{10... | collective-permute-start | bytes 245768 | tf_op jit(solution)/shard_map/ppermute | solution.py:64
  28.7 0.2 collective-permute-start.6
  28.9 0.0 copy-done.10
  29.0 6.8 %routing.1 = (bf16[144,80]{1,0:T(8,128)(2,1)S(1)}, bf16[128,80]{1,0:T(8,128)(2,1)S(1)}, bf16[128,80]{1,0:T(8,128)(2,1)S(1)}, bf16[512,1024]{1,0:T(8,128)(2,1)S(1...) custom-call(s32[6,80]{1,0:T(8,128)S(1)} %bitcast.23, ...), custom_call_target="tpu_custom_call" | custom-call | flops 1000 | bytes 20000000 | tf_op jit(solution)/shard_map/routing/pallas_call | solution.py:48
  35.8 0.0 collective-permute-done.4.refs_0_
  35.8 0.0 collective-permute-done.5.refs_1_
  35.8 0.0 collective-permute-done.6.refs_2_
  35.8 0.6 prepare.1
  36.4 1.9 %experts_2.1 = (bf16[72,1536]{1,0:T(8,128)(2,1)S(1)}, f32[4,8,1536]{2,1,0:T(8,128)S(1)}) custom-call(bf16[144,1024]{1,0:T(8,128)(2,1)S(1)} %get-tuple-element.33.gate_ref, bf16[144,1024]{1,0:T(8,128)(2,1)S(1)} %get-tuple-element.34.up_ref, bf16[144,128]{1,0:T(8,128)(2,1)S(1)} %get-tuple-element.35.side_ref, ...), custom_call_target="tpu_custom_call" | custom-call | flops 1000 | bytes 100000 | tf_op jit(solution)/shard_map/experts_2/pallas_call | solution.py:48
  38.3 1.6 %collective-permute-start.7 = (bf16[72,1536]{1,0:T(8,128)(2,1)S(1)}, bf16[72,1536]{1,0:T(8,128)(2,1)S(1)}, u32[]{:S(2)}, u32[]{:S(2)}) collective-permute-start(bf16[72,1536]{1,0:T(8,128)(2,1)S(1)} %get-tuple-element.40), channel_id=1, source_target_pairs={{0,8},{8,0},{16,24},{24,16},{1,9},{9,1},{17,25},{25,17},{2,10},{10... | collective-permute-start | bytes 663560 | tf_op jit(solution)/shard_map/ppermute | solution.py:64
  39.9 1.3 %experts_1.1.refs_1_.later_ref = bf16[72,1536]{1,0:T(8,128)(2,1)S(1)} custom-call(bf16[144,1024]{1,0:T(8,128)(2,1)S(1)} %get-tuple-element.33.gate_ref, bf16[144,1024]{1,0:T(8,128)(2,1)S(1)} %get-tuple-element.34.up_ref, bf16[144,128]{1,0:T(8,128)(2,1)S(1)} %get-tuple-element.35.side_ref, bf16[2,512,2,1408]{3,2,1,0:T(2,128)(2,1)S(1)} %get-tuple-element.39.weight_ref, ...), custom_call_target="tpu_custom_call" | custom-call | flops 1000 | bytes 100000 | tf_op jit(solution)/shard_map/experts_1/pallas_call | solution.py:48
  41.2 1.3 %experts_3.1.own_ref = bf16[72,1536]{1,0:T(8,128)(2,1)S(1)} custom-call(bf16[144,1024]{1,0:T(8,128)(2,1)S(1)} %get-tuple-element.33.gate_ref, bf16[144,1024]{1,0:T(8,128)(2,1)S(1)} %get-tuple-element.34.up_ref, bf16[144,128]{1,0:T(8,128)(2,1)S(1)} %get-tuple-element.35.side_ref, bf16[2,512,2,1408]{3,2,1,0:T(2,128)(2,1)S(1)} %get-tuple-element.38.weight_ref, ...), custom_call_target="tpu_custom_call" | custom-call | flops 1000 | bytes 100000 | tf_op jit(solution)/shard_map/experts_3/pallas_call | solution.py:48
  42.5 2.7 %collective-permute-done.7.received_ref = bf16[72,1536]{1,0:T(8,128)(2,1)S(1)} collective-permute-done((bf16[72,1536]{1,0:T(8,128)(2,1)S(1)}, bf16[72,1536]{1,0:T(8,128)(2,1)S(1)}, u32[]{:S(2)}, u32[]{:S(2)}) %collective-permute-start.7) | collective-permute-done | bytes 221216 | tf_op jit(solution)/shard_map/ppermute | solution.py:64
  45.3 0.1 add_pair.1
  45.3 1.5 %collective-permute-start.9 = (bf16[72,1536]{1,0:T(8,128)(2,1)S(1)}, bf16[72,1536]{1,0:T(8,128)(2,1)S(1)}, u32[]{:S(2)}, u32[]{:S(2)}) collective-permute-start(bf16[72,1536]{1,0:T(8,128)(2,1)S(1)} %get-tuple-element.42), channel_id=1, source_target_pairs={{0,8},{8,0},{16,24},{24,16},{1,9},{9,1},{17,25},{25,17},{2,10},{10... | collective-permute-start | bytes 663560 | tf_op jit(solution)/shard_map/ppermute | solution.py:64
  46.8 2.4 %collective-permute-start.8 = (bf16[72,1536]{1,0:T(8,128)(2,1)S(1)}, bf16[72,1536]{1,0:T(8,128)(2,1)S(1)}, u32[]{:S(2)}, u32[]{:S(2)}) collective-permute-start(bf16[72,1536]{1,0:T(8,128)(2,1)S(1)} %get-tuple-element.41.refs_1_), channel_id=1, source_target_pairs={{0,24},{8,16},{16,8},{24,0},{1,25},{9,17},{17,9},{25,1},{2,26},{10... | collective-permute-start | bytes 663560 | tf_op jit(solution)/shard_map/ppermute | solution.py:64
  49.2 4.7 %experts_0.1.refs_0_ = bf16[72,1536]{1,0:T(8,128)(2,1)S(1)} custom-call(bf16[144,1024]{1,0:T(8,128)(2,1)S(1)} %get-tuple-element.33.gate_ref, bf16[144,1024]{1,0:T(8,128)(2,1)S(1)} %get-tuple-element.34.up_ref, bf16[144,128]{1,0:T(8,128)(2,1)S(1)} %get-tuple-element.35.side_ref, bf16[8,512,2,1408]{3,2,1,0:T(2,128)(2,1)} %weight_ref.9, ...), custom_call_target="tpu_custom_call" | custom-call | flops 1000 | bytes 100000 | tf_op jit(solution)/shard_map/experts_0/pallas_call | solution.py:48
  53.9 0.0 collective-permute-done.9.refs_2_
  53.9 4.1 %collective-permute-done.8.refs_1_ = bf16[72,1536]{1,0:T(8,128)(2,1)S(1)} collective-permute-done((bf16[72,1536]{1,0:T(8,128)(2,1)S(1)}, bf16[72,1536]{1,0:T(8,128)(2,1)S(1)}, u32[]{:S(2)}, u32[]{:S(2)}) %collective-permute-start.8) | collective-permute-done | bytes 221216 | tf_op jit(solution)/shard_map/ppermute | solution.py:64
  58.0 0.2 hidden.1.hidden_ref.refs_0_
  58.2 3.5 %collective-permute-start.11 = (bf16[36,1408]{1,0:T(8,128)(2,1)S(1)}, bf16[36,1408]{1,0:T(8,128)(2,1)S(1)}, u32[]{:S(2)}, u32[]{:S(2)}) collective-permute-start(bf16[36,1408]{1,0:T(8,128)(2,1)S(1)} %hidden.1.hidden_ref.refs_0_), channel_id=1, source_target_pairs={{0,16},{8,24},{16,0},{24,8},{1,17},{9,25},{17,1},{25,9},{2,18},{10... | collective-permute-start | bytes 304136 | tf_op jit(solution)/shard_map/ppermute | solution.py:64
  61.8 0.0 collective-permute-start.10
  61.8 1.5 %collective-permute-start.12 = (bf16[36,1408]{1,0:T(8,128)(2,1)S(1)}, bf16[36,1408]{1,0:T(8,128)(2,1)S(1)}, u32[]{:S(2)}, u32[]{:S(2)}) collective-permute-start(bf16[36,1408]{1,0:T(8,128)(2,1)S(1)} %hidden.1.hidden_ref.refs_0_), channel_id=1, source_target_pairs={{0,24},{8,16},{16,8},{24,0},{1,25},{9,17},{17,9},{25,1},{2,26},{10... | collective-permute-start | bytes 304136 | tf_op jit(solution)/shard_map/ppermute | solution.py:64
  63.3 0.0 slice-done.1
  63.3 0.5 down_0.1.refs_4_
  63.8 2.0 %collective-permute-done.11.hidden_ref.refs_2_ = bf16[36,1408]{1,0:T(8,128)(2,1)S(1)} collective-permute-done((bf16[36,1408]{1,0:T(8,128)(2,1)S(1)}, bf16[36,1408]{1,0:T(8,128)(2,1)S(1)}, u32[]{:S(2)}, u32[]{:S(2)}) %collective-permute-start.11) | collective-permute-done | bytes 101408 | tf_op jit(solution)/shard_map/ppermute | solution.py:64
  65.8 0.5 down_2.1.refs_6_
  66.3 0.4 collective-permute-done.10.hidden_ref.refs_1_
  66.7 0.5 down_1.1.refs_5_
  67.2 1.3 %collective-permute-done.12.refs_3_ = bf16[36,1408]{1,0:T(8,128)(2,1)S(1)} collective-permute-done((bf16[36,1408]{1,0:T(8,128)(2,1)S(1)}, bf16[36,1408]{1,0:T(8,128)(2,1)S(1)}, u32[]{:S(2)}, u32[]{:S(2)}) %collective-permute-start.12) | collective-permute-done | bytes 101408 | tf_op jit(solution)/shard_map/ppermute | solution.py:64
  68.4 0.0 copy-done.3
  68.5 0.9 %combine.1 = (bf16[8,10,512]{2,1,0:T(8,128)(2,1)S(1)}, f32[4,4,512]{2,1,0:T(4,128)S(1)}) custom-call(bf16[128,80]{1,0:T(8,128)(2,1)S(1)} %get-tuple-element.26.coarse_ref, bf16[128,80]{1,0:T(8,128)(2,1)S(1)} %get-tuple-element.27.fine_ref, bf16[8,1408,512]{2,1,0:T(8,128)(2,1)S(1)} %bitcast.9, bf16[1,1408,512]{2,1,0:T(8,128)(2,1)S(1)} %copy-done.3, ...), custom_call_target="tpu_custom_call" | custom-call | flops 1000 | bytes 100000 | tf_op jit(solution)/shard_map/combine/pallas_call | solution.py:48
  69.3 8.0 %all_to_all.5.pieces_ref = bf16[8,10,512]{2,1,0:T(8,128)(2,1)S(1)} all-to-all(bf16[8,10,512]{2,1,0:T(8,128)(2,1)S(1)} %get-tuple-element.43), channel_id=1, replica_groups=mesh['head'=4,'pool'=8] {'pool'}, dimensions={0} | all-to-all | bytes 163840 | tf_op jit(solution)/shard_map/all_to_all | solution.py:645
  77.4 2.4 %collective-permute-start.15 = (bf16[10,512]{1,0:T(8,128)(2,1)S(1)}, bf16[10,512]{1,0:T(8,128)(2,1)S(1)}, u32[]{:S(2)}, u32[]{:S(2)}) collective-permute-start(bf16[10,512]{1,0:T(8,128)(2,1)S(1)} %block.1.refs_0_.refs_3_), channel_id=1, source_target_pairs={{0,24},{8,16},{16,8},{24,0},{1,25},{9,17},{17,9},{25,1},{2,26},{10... | collective-permute-start | bytes 30728 | tf_op jit(solution)/shard_map/ppermute | solution.py:64
  79.7 0.5 collective-permute-start.14
  80.2 1.6 %collective-permute-start.13 = (bf16[10,512]{1,0:T(8,128)(2,1)S(1)}, bf16[10,512]{1,0:T(8,128)(2,1)S(1)}, u32[]{:S(2)}, u32[]{:S(2)}) collective-permute-start(bf16[10,512]{1,0:T(8,128)(2,1)S(1)} %block.1.refs_0_.refs_3_), channel_id=1, source_target_pairs={{0,8},{8,0},{16,24},{24,16},{1,9},{9,1},{17,25},{25,17},{2,10},{10... | collective-permute-start | bytes 30728 | tf_op jit(solution)/shard_map/ppermute | solution.py:64
  81.8 0.0 slice-done.3
  81.8 0.0 copy-done.8
  81.8 0.3 project_own.1
  82.2 0.8 collective-permute-done.15.refs_2_
  83.0 1.4 %collective-permute-done.14.refs_1_ = bf16[10,512]{1,0:T(8,128)(2,1)S(1)} collective-permute-done((bf16[10,512]{1,0:T(8,128)(2,1)S(1)}, bf16[10,512]{1,0:T(8,128)(2,1)S(1)}, u32[]{:S(2)}, u32[]{:S(2)}) %collective-permute-start.14) | collective-permute-done | bytes 10272 | tf_op jit(solution)/shard_map/ppermute | solution.py:64
  84.4 0.0 collective-permute-done.13.refs_0_
  84.4 1.4 %project.1 = (bf16[10,2048]{1,0:T(8,128)(2,1)}, bf16[10,1536]{1,0:T(8,128)(2,1)}) custom-call(bf16[16,128]{1,0:T(8,128)(2,1)S(1)} %bitcast.21, bf16[2048,1536]{1,0:T(8,128)(2,1)S(1)} %bitcast.11, bf16[10,512]{1,0:T(8,128)(2,1)S(1)} %collective-permute-done.13.refs_0_, bf16[10,512]{1,0:T(8,128)(2,1)S(1)} %collective-permute-done.14.refs_1_, ...), custom_call_target="tpu_custom_call" | custom-call | flops 1000 | bytes 100000 | tf_op jit(solution)/shard_map/project/pallas_call | solution.py:48
  (28 shorter events, 0.1 us)
Async XLA Ops:
  0.6 6.9 %collective-permute-start.2 = (bf16[1,10,512]{2,1,0:T(8,128)(2,1)}, bf16[1,10,512]{2,1,0:T(8,128)(2,1)S(1)}, u32[]{:S(2)}, u32[]{:S(2)}) collective-permute-start(bf16[1,10,512]{2,1,0:T(8,128)(2,1)} %bitcast.15), channel_id=1, source_target_pairs={{0,6},{1,7},{2,4},{3,5},{4,2},{5,3},{6,0},{7,1},{8,14},{9,15},{10,... | collective-permute-start | bytes 30728 | tf_op jit(solution)/shard_map/ppermute | solution.py:64
  4.6 3.9 %collective-permute-start.1 = (bf16[1,10,512]{2,1,0:T(8,128)(2,1)}, bf16[1,10,512]{2,1,0:T(8,128)(2,1)S(1)}, u32[]{:S(2)}, u32[]{:S(2)}) collective-permute-start(bf16[1,10,512]{2,1,0:T(8,128)(2,1)} %bitcast.16), channel_id=1, source_target_pairs={{0,4},{1,5},{2,6},{3,7},{4,0},{5,1},{6,2},{7,3},{8,12},{9,13},{10,... | collective-permute-start | bytes 30728 | tf_op jit(solution)/shard_map/ppermute | solution.py:64
  5.1 3.9 %collective-permute-start = (bf16[1,10,512]{2,1,0:T(8,128)(2,1)}, bf16[1,10,512]{2,1,0:T(8,128)(2,1)S(1)}, u32[]{:S(2)}, u32[]{:S(2)}) collective-permute-start(bf16[1,10,512]{2,1,0:T(8,128)(2,1)} %bitcast.17), channel_id=1, source_target_pairs={{0,2},{1,3},{2,0},{3,1},{4,6},{5,7},{6,4},{7,5},{8,10},{9,11},{10,... | collective-permute-start | bytes 30728 | tf_op jit(solution)/shard_map/ppermute | solution.py:64
  5.2 0.8 copy-start.5
  5.2 0.8 copy-start.12
  5.2 3.8 %copy-start.7 = (bf16[10,512]{1,0:T(8,128)(2,1)S(1)}, bf16[10,512]{1,0:T(8,128)(2,1)}, u32[]{:S(2)}) copy-start(bf16[10,512]{1,0:T(8,128)(2,1)} %param.16) | copy-start | bytes 30724
  5.2 5.1 %copy-start = (bf16[36,2,64,512]{3,2,1,0:T(8,128)(2,1)S(1)}, bf16[36,2,64,512]{3,2,1,0:T(8,128)(2,1)}, u32[]{:S(2)}) copy-start(bf16[36,2,64,512]{3,2,1,0:T(8,128)(2,1)} %cache_ref.1) | copy-start | bytes 14155780
  5.2 5.1 %copy-start.4 = (bf16[10,2048]{1,0:T(8,128)(2,1)S(1)}, bf16[10,2048]{1,0:T(8,128)(2,1)}, u32[]{:S(2)}) copy-start(bf16[10,2048]{1,0:T(8,128)(2,1)} %residual_ref.1) | copy-start | bytes 122884
  5.3 5.1 %copy-start.6 = (bf16[10,2,512]{2,1,0:T(2,128)(2,1)S(1)}, bf16[10,2,512]{2,1,0:T(2,128)(2,1)}, u32[]{:S(2)}) copy-start(bf16[10,2,512]{2,1,0:T(2,128)(2,1)} %fresh_ref.1) | copy-start | bytes 61444
  6.0 17.5 %copy-start.2 = (bf16[512,2048]{1,0:T(8,128)(2,1)S(1)}, bf16[512,2048]{1,0:T(8,128)(2,1)}, u32[]{:S(2)}) copy-start(bf16[512,2048]{1,0:T(8,128)(2,1)} %weight_ref.8) | copy-start | bytes 6291460
  6.0 22.9 %copy-start.10 = (s32[80,6]{0,1:T(8,128)S(1)}, s32[80,6]{0,1:T(8,128)}, u32[]{:S(2)}) copy-start(s32[80,6]{0,1:T(8,128)} %param.24) | copy-start | bytes 5764
  6.0 22.9 %copy-start.11 = (f32[80,6]{0,1:T(8,128)S(1)}, f32[80,6]{0,1:T(8,128)}, u32[]{:S(2)}) copy-start(f32[80,6]{0,1:T(8,128)} %param.25) | copy-start | bytes 5764
  9.1 1.3 %collective-permute-start.3 = (bf16[4,10,512]{2,1,0:T(8,128)(2,1)S(1)}, bf16[4,10,512]{2,1,0:T(8,128)(2,1)S(1)}, u32[]{:S(2)}, u32[]{:S(2)}) collective-permute-start(bf16[4,10,512]{2,1,0:T(8,128)(2,1)S(1)} %join_queries.1.refs_0_), channel_id=1, source_target_pairs={{0,1},{1,0},{2,3},{3,2},{4,5},{5,4},{6,7},{7,6},{8,9},{9,8},{10,11... | collective-permute-start | bytes 122888 | tf_op jit(solution)/shard_map/ppermute | solution.py:64
  24.5 11.3 %collective-permute-start.4 = (bf16[80,512]{1,0:T(8,128)(2,1)S(1)}, bf16[80,512]{1,0:T(8,128)(2,1)S(1)}, u32[]{:S(2)}, u32[]{:S(2)}) collective-permute-start(bf16[80,512]{1,0:T(8,128)(2,1)S(1)} %get-tuple-element.30), channel_id=1, source_target_pairs={{0,8},{8,0},{16,24},{24,16},{1,9},{9,1},{17,25},{25,17},{2,10},{10... | collective-permute-start | bytes 245768 | tf_op jit(solution)/shard_map/ppermute | solution.py:64
  26.1 9.6 %collective-permute-start.5 = (bf16[80,512]{1,0:T(8,128)(2,1)S(1)}, bf16[80,512]{1,0:T(8,128)(2,1)S(1)}, u32[]{:S(2)}, u32[]{:S(2)}) collective-permute-start(bf16[80,512]{1,0:T(8,128)(2,1)S(1)} %get-tuple-element.31), channel_id=1, source_target_pairs={{0,16},{8,24},{16,0},{24,8},{1,17},{9,25},{17,1},{25,9},{2,18},{10... | collective-permute-start | bytes 245768 | tf_op jit(solution)/shard_map/ppermute | solution.py:64
  28.7 7.1 %collective-permute-start.6 = (bf16[80,512]{1,0:T(8,128)(2,1)S(1)}, bf16[80,512]{1,0:T(8,128)(2,1)S(1)}, u32[]{:S(2)}, u32[]{:S(2)}) collective-permute-start(bf16[80,512]{1,0:T(8,128)(2,1)S(1)} %get-tuple-element.32), channel_id=1, source_target_pairs={{0,24},{8,16},{16,8},{24,0},{1,25},{9,17},{17,9},{25,1},{2,26},{10... | collective-permute-start | bytes 245768 | tf_op jit(solution)/shard_map/ppermute | solution.py:64
  28.9 6.8 %copy-start.9 = (bf16[2048]{0:T(1024)(128)(2,1)S(1)}, bf16[2048]{0:T(1024)(128)(2,1)}, u32[]{:S(2)}) copy-start(bf16[2048]{0:T(1024)(128)(2,1)} %param.23) | copy-start | bytes 12292
  28.9 7.4 %copy-start.1 = (bf16[1,512,2,1408]{3,2,1,0:T(2,128)(2,1)S(1)}, bf16[1,512,2,1408]{3,2,1,0:T(2,128)(2,1)}, u32[]{:S(2)}) copy-start(bf16[1,512,2,1408]{3,2,1,0:T(2,128)(2,1)} %refs_0_.1) | copy-start | bytes 8650756
  38.3 7.0 %collective-permute-start.7 = (bf16[72,1536]{1,0:T(8,128)(2,1)S(1)}, bf16[72,1536]{1,0:T(8,128)(2,1)S(1)}, u32[]{:S(2)}, u32[]{:S(2)}) collective-permute-start(bf16[72,1536]{1,0:T(8,128)(2,1)S(1)} %get-tuple-element.40), channel_id=1, source_target_pairs={{0,8},{8,0},{16,24},{24,16},{1,9},{9,1},{17,25},{25,17},{2,10},{10... | collective-permute-start | bytes 663560 | tf_op jit(solution)/shard_map/ppermute | solution.py:64
  45.3 8.6 %collective-permute-start.9 = (bf16[72,1536]{1,0:T(8,128)(2,1)S(1)}, bf16[72,1536]{1,0:T(8,128)(2,1)S(1)}, u32[]{:S(2)}, u32[]{:S(2)}) collective-permute-start(bf16[72,1536]{1,0:T(8,128)(2,1)S(1)} %get-tuple-element.42), channel_id=1, source_target_pairs={{0,8},{8,0},{16,24},{24,16},{1,9},{9,1},{17,25},{25,17},{2,10},{10... | collective-permute-start | bytes 663560 | tf_op jit(solution)/shard_map/ppermute | solution.py:64
  46.8 16.5 %slice-start = ((s8[11534336]{0:T(1024)(128)(4,1)}), s8[4194304]{0:T(1024)(128)(4,1)S(1)}, s32[]{:S(2)}) async-start(s8[11534336]{0:T(1024)(128)(4,1)} %bitcast.8), calls=%async_computation.1 | async-start | bytes 8388608
  46.8 16.5 %slice-start.1 = ((s8[11534336]{0:T(1024)(128)(4,1)}), s8[4194304]{0:T(1024)(128)(4,1)S(1)}, s32[]{:S(2)}) async-start(s8[11534336]{0:T(1024)(128)(4,1)} %bitcast.8), calls=%async_computation.2 | async-start | bytes 8388608
  46.8 16.5 %slice-start.2 = ((s8[11534336]{0:T(1024)(128)(4,1)}), s8[3145728]{0:T(1024)(128)(4,1)S(1)}, s32[]{:S(2)}) async-start(s8[11534336]{0:T(1024)(128)(4,1)} %bitcast.8), calls=%async_computation.3 | async-start | bytes 6291456
  46.8 11.2 %collective-permute-start.8 = (bf16[72,1536]{1,0:T(8,128)(2,1)S(1)}, bf16[72,1536]{1,0:T(8,128)(2,1)S(1)}, u32[]{:S(2)}, u32[]{:S(2)}) collective-permute-start(bf16[72,1536]{1,0:T(8,128)(2,1)S(1)} %get-tuple-element.41.refs_1_), channel_id=1, source_target_pairs={{0,24},{8,16},{16,8},{24,0},{1,25},{9,17},{17,9},{25,1},{2,26},{10... | collective-permute-start | bytes 663560 | tf_op jit(solution)/shard_map/ppermute | solution.py:64
  58.2 7.6 %collective-permute-start.11 = (bf16[36,1408]{1,0:T(8,128)(2,1)S(1)}, bf16[36,1408]{1,0:T(8,128)(2,1)S(1)}, u32[]{:S(2)}, u32[]{:S(2)}) collective-permute-start(bf16[36,1408]{1,0:T(8,128)(2,1)S(1)} %hidden.1.hidden_ref.refs_0_), channel_id=1, source_target_pairs={{0,16},{8,24},{16,0},{24,8},{1,17},{9,25},{17,1},{25,9},{2,18},{10... | collective-permute-start | bytes 304136 | tf_op jit(solution)/shard_map/ppermute | solution.py:64
  61.8 4.9 %collective-permute-start.10 = (bf16[36,1408]{1,0:T(8,128)(2,1)S(1)}, bf16[36,1408]{1,0:T(8,128)(2,1)S(1)}, u32[]{:S(2)}, u32[]{:S(2)}) collective-permute-start(bf16[36,1408]{1,0:T(8,128)(2,1)S(1)} %hidden.1.hidden_ref.refs_0_), channel_id=1, source_target_pairs={{0,8},{8,0},{16,24},{24,16},{1,9},{9,1},{17,25},{25,17},{2,10},{10... | collective-permute-start | bytes 304136 | tf_op jit(solution)/shard_map/ppermute | solution.py:64
  61.8 6.7 %collective-permute-start.12 = (bf16[36,1408]{1,0:T(8,128)(2,1)S(1)}, bf16[36,1408]{1,0:T(8,128)(2,1)S(1)}, u32[]{:S(2)}, u32[]{:S(2)}) collective-permute-start(bf16[36,1408]{1,0:T(8,128)(2,1)S(1)} %hidden.1.hidden_ref.refs_0_), channel_id=1, source_target_pairs={{0,24},{8,16},{16,8},{24,0},{1,25},{9,17},{17,9},{25,1},{2,26},{10... | collective-permute-start | bytes 304136 | tf_op jit(solution)/shard_map/ppermute | solution.py:64
  66.3 2.1 %copy-start.3 = (bf16[1,1408,512]{2,1,0:T(8,128)(2,1)S(1)}, bf16[1,1408,512]{2,1,0:T(8,128)(2,1)}, u32[]{:S(2)}) copy-start(bf16[1,1408,512]{2,1,0:T(8,128)(2,1)} %shared_weight_ref.1) | copy-start | bytes 4325380
  66.7 15.1 %slice-start.3 = ((s8[6291456]{0:T(1024)(128)(4,1)}), s8[4194304]{0:T(1024)(128)(4,1)S(1)}, s32[]{:S(2)}) async-start(s8[6291456]{0:T(1024)(128)(4,1)} %bitcast.10), calls=%async_computation.4 | async-start | bytes 8388608
  68.5 13.4 %slice-start.4 = ((s8[6291456]{0:T(1024)(128)(4,1)}), s8[2097152]{0:T(1024)(128)(4,1)S(1)}, s32[]{:S(2)}) async-start(s8[6291456]{0:T(1024)(128)(4,1)} %bitcast.10), calls=%async_computation.5 | async-start | bytes 4194304
  68.5 13.4 %copy-start.8 = (bf16[2048]{0:T(1024)(128)(2,1)S(1)}, bf16[2048]{0:T(1024)(128)(2,1)}, u32[]{:S(2)}) copy-start(bf16[2048]{0:T(1024)(128)(2,1)} %param.30) | copy-start | bytes 12292
  77.4 5.6 %collective-permute-start.15 = (bf16[10,512]{1,0:T(8,128)(2,1)S(1)}, bf16[10,512]{1,0:T(8,128)(2,1)S(1)}, u32[]{:S(2)}, u32[]{:S(2)}) collective-permute-start(bf16[10,512]{1,0:T(8,128)(2,1)S(1)} %block.1.refs_0_.refs_3_), channel_id=1, source_target_pairs={{0,24},{8,16},{16,8},{24,0},{1,25},{9,17},{17,9},{25,1},{2,26},{10... | collective-permute-start | bytes 30728 | tf_op jit(solution)/shard_map/ppermute | solution.py:64
  79.7 4.6 %collective-permute-start.14 = (bf16[10,512]{1,0:T(8,128)(2,1)S(1)}, bf16[10,512]{1,0:T(8,128)(2,1)S(1)}, u32[]{:S(2)}, u32[]{:S(2)}) collective-permute-start(bf16[10,512]{1,0:T(8,128)(2,1)S(1)} %block.1.refs_0_.refs_3_), channel_id=1, source_target_pairs={{0,16},{8,24},{16,0},{24,8},{1,17},{9,25},{17,1},{25,9},{2,18},{10... | collective-permute-start | bytes 30728 | tf_op jit(solution)/shard_map/ppermute | solution.py:64
  80.2 4.2 %collective-permute-start.13 = (bf16[10,512]{1,0:T(8,128)(2,1)S(1)}, bf16[10,512]{1,0:T(8,128)(2,1)S(1)}, u32[]{:S(2)}, u32[]{:S(2)}) collective-permute-start(bf16[10,512]{1,0:T(8,128)(2,1)S(1)} %block.1.refs_0_.refs_3_), channel_id=1, source_target_pairs={{0,8},{8,0},{16,24},{24,16},{1,9},{9,1},{17,25},{25,17},{2,10},{10... | collective-permute-start | bytes 30728 | tf_op jit(solution)/shard_map/ppermute | solution.py:64

commit v5 on v4

--- a/solution.py
+++ b/solution.py
@@ -307,7 +307,7 @@
 ):
     refs = list(refs)
     head_devs = lax.axis_size("head")
-    if distance == 0:
+    if distance < 2:
         near_ref, semaphores = refs[-2:]
         refs = refs[:-2]
         fetched = start_weights(distance, slots, weight_ref, near_ref, semaphores)
@@ -420,32 +420,30 @@
         refs[-1][place] = ref[0]
 
 
-def project_kernel(distances, width, gain_ref, weight_ref, *refs):
+def project_kernel(distances, width, begins, ends, gain_ref, weight_ref, *refs):
     me = lax.axis_index("head")
     count = len(distances)
     block_refs, refs = refs[:count], refs[count:]
-    if distances[0] == 0:
-        total_ref, side_ref = refs
-        total, squares = jnp.zeros(total_ref.shape, f32), 0.0
-    else:
-        own_ref, given_total_ref, given_side_ref, hidden_ref, out_ref = refs
-        total, squares = given_total_ref[...], given_side_ref[:, 0:1]
+    total, squares = 0.0, 0.0
+    if not begins:
+        total, squares = refs[0][...], refs[1][:, 0:1]
+        refs = refs[2:]
     for distance, ref in zip(distances, block_refs):
         block = ref[...].astype(f32)
-        req_dev, col_part = block.shape
-        columns = pl.ds(pl.multiple_of((me ^ distance) * col_part, LANES), col_part)
-        if distances[0] != 0:
-            hidden_ref[:, columns] = ref[...]
+        col_part = block.shape[1]
+        rows = pl.ds(pl.multiple_of((me ^ distance) * col_part, LANES), col_part)
         squares = squares + jnp.sum(block * block, axis=1, keepdims=True)
         scaled = (block * gain_columns(gain_ref, me ^ distance, col_part)).astype(bf16)
-        total = total + dot(scaled, weight_ref[columns, :])
-    if distances[0] == 0:
-        total_ref[...] = total
-        side_ref[...] = jnp.broadcast_to(squares, side_ref.shape)
-    else:
-        columns = pl.ds(pl.multiple_of(me * col_part, LANES), col_part)
-        hidden_ref[:, columns] = own_ref[...]
-        out_ref[...] = (total * lax.rsqrt(squares / width + epsilon)).astype(bf16)
+        total = total + dot(scaled, weight_ref[rows, :])
+    if not ends:
+        refs[0][...] = total
+        refs[1][...] = jnp.broadcast_to(squares, refs[1].shape)
+        return
+    *every_refs, hidden_ref, out_ref = refs
+    out_ref[...] = (total * lax.rsqrt(squares / width + epsilon)).astype(bf16)
+    for distance, ref in enumerate(every_refs):
+        columns = pl.ds(pl.multiple_of((me ^ distance) * ref.shape[1], LANES), ref.shape[1])
+        hidden_ref[:, columns] = ref[...]
 
 
 def per_device(
@@ -480,7 +478,7 @@
     distances = list(range(1, head_devs))
     piece_experts = max(1, exp_dev // head_devs)
     fetch_shape = ((piece_experts, col_part, 2, ffe), bf16)
-    fetched = list(reversed(range(1, head_devs)))
+    fetched = list(reversed(range(2, head_devs)))
 
     queries = queries[None]
     table, counts = block_table.T, lengths[None, :]
@@ -584,7 +582,7 @@
             args, outs = args + [shared_gate_up], outs + [shared_shape]
         else:
             args = args + [shared_rows] + list(after)
-        if distance == 0:
+        if distance < 2:
             scratch, copies, far = [fetch_shape], [piece_experts * SPLIT], [3]
         mine, *shared = call(
             functools.partial(expert_kernel, distance, slots, part, len(outs) > 1),
@@ -594,7 +592,7 @@
             scratch=scratch,
             copies=copies,
             far=far,
-            megabytes=32 if distance == 0 else 10,
+            megabytes=32 if distance < 2 else 10,
         )
         if shared:
             (shared_rows,) = shared
@@ -653,18 +651,20 @@
     blocks = [block] + [swap(block, "head", d) for d in distances]
     last_args = [next_gain.reshape(-1, LANES), w_query_key_value]
     out_width = w_query_key_value.shape[1]
-    total, squares = call(
-        functools.partial(project_kernel, [0], width),
-        "project_own",
-        [((req_dev, out_width), f32), ((req_dev, LANES), f32)],
-        last_args + [block],
-        megabytes=6,
-    )
+    running = []
+    for which in ([0], distances[2:]):
+        running = call(
+            functools.partial(project_kernel, which, width, not running, False),
+            f"project_{which[0]}",
+            [((req_dev, out_width), f32), ((req_dev, LANES), f32)],
+            last_args + [blocks[d] for d in which] + list(running),
+            megabytes=6,
+        )
     next_hidden, next_projection = call(
-        functools.partial(project_kernel, distances, width),
+        functools.partial(project_kernel, distances[:2], width, False, True),
         "project",
         [((req_dev, width), bf16), ((req_dev, out_width), bf16)],
-        last_args + blocks[1:] + [block, total, squares],
+        last_args + [blocks[d] for d in distances[:2]] + list(running) + blocks,
         megabytes=6,
     )
     return (next_hidden, next_projection)

time: 86 us -> 84.6 us (0.984)
  waiting for transfers between devices: 15.5 us -> 13.6 us
  Pallas kernels: 26.3 us -> 27.2 us
    ppermute x16, waiting for transfers between devices: 15.5 us -> 13.6 us  [swap(): return lax.ppermute(value, axis, [(i, i ^ distance) for i in range(count)])]
    pallas_call x20 -> x21, Pallas kernels: 26.3 us -> 27.2 us  [call(): pl.pallas_call(kernel, out_shape=[jax.ShapeDtypeStruct(shape, dtype) for...]
  transfers between devices with their start and end apart: 16 -> 16, of which waited for: 10 -> 11; matrix products, arithmetic and copies ran while one was open for 0% -> 0% of each run, Pallas kernels for 21% -> 23%
where the time goes in v5:
time: 84.6 us; the launch traced here: 84.4 us
  Pallas kernels  27.2 us (32%)
  starting transfers between devices  23.6 us (28%)
  blocking collectives  18.9 us (22%)
  waiting for transfers between devices  13.6 us (16%)
    pallas_call x21, Pallas kernels, call(): pl.pallas_call(kernel, out_shape=[jax.ShapeDtypeStruct(shape, dtype) for...  27.2 us
    ppermute x16, starting transfers between devices, swap(): return lax.ppermute(value, axis, [(i, i ^ distance) for i in range(count)])  23.6 us
    ppermute x16, waiting for transfers between devices, swap(): return lax.ppermute(value, axis, [(i, i ^ distance) for i in range(count)])  13.6 us
    all_gather x1, blocking collectives, per_device(): parts = lax.all_gather(partial, 'pool', axis=0)  10.7 us
    all_to_all x1, blocking collectives, per_device(): pieces = lax.all_to_all(routed, 'pool', 0, 0)  8.22 us
  transfers between devices with their start and end apart: 16, of which 11 were waited for; matrix products, arithmetic and copies ran while one was open for 0% of the time, Pallas kernels for 23%

profile of v5, /device:TPU:0, one launch (start us, length us, event | category | flops | bytes accessed | tf_op | source)
XLA Modules:
  0.0 84.4 jit_solution(9380992368750467359)
XLA Ops:
  0.6 4.0 %collective-permute-start.2 = (bf16[1,10,512]{2,1,0:T(8,128)(2,1)}, bf16[1,10,512]{2,1,0:T(8,128)(2,1)S(1)}, u32[]{:S(2)}, u32[]{:S(2)}) collective-permute-start(bf16[1,10,512]{2,1,0:T(8,128)(2,1)} %bitcast.15), channel_id=1, source_target_pairs={{0,6},{1,7},{2,4},{3,5},{4,2},{5,3},{6,0},{7,1},{8,14},{9,15},{10,... | collective-permute-start | bytes 30728 | tf_op jit(solution)/shard_map/ppermute | solution.py:64
  4.6 0.5 collective-permute-start.1
  5.1 0.1 collective-permute-start
  5.2 0.0 copy-start.4
  5.3 0.0 copy-start.6
  5.3 0.5 early.1.early_ref
  5.8 0.2 copy-done.5
  6.0 0.0 copy-done.12
  6.0 1.5 %setup.1.bias_ref = f32[80,2304]{1,0:T(8,128)S(1)} custom-call(s32[1]{0:T(128)} %early.1.early_ref, s32[64,80]{1,0:T(8,128)S(1)} %bitcast.14, s32[1,80]{1,0:T(1,128)S(1)} %bitcast.27), custom_call_target="tpu_custom_call" | custom-call | flops 1000 | bytes 100000 | tf_op jit(solution)/shard_map/setup/pallas_call | solution.py:48
  7.6 0.0 collective-permute-done.2.refs_3_
  7.6 1.0 %collective-permute-done.1.refs_2_ = bf16[1,10,512]{2,1,0:T(8,128)(2,1)S(1)} collective-permute-done((bf16[1,10,512]{2,1,0:T(8,128)(2,1)}, bf16[1,10,512]{2,1,0:T(8,128)(2,1)S(1)}, u32[]{:S(2)}, u32[]{:S(2)}) %collective-permute-start.1) | collective-permute-done | bytes 10272 | tf_op jit(solution)/shard_map/ppermute | solution.py:64
  8.5 0.5 collective-permute-done.refs_1_
  9.0 0.0 copy-done.7
  9.1 0.1 collective-permute-start.3
  9.1 1.2 %collective-permute-done.3.refs_1_ = bf16[4,10,512]{2,1,0:T(8,128)(2,1)S(1)} collective-permute-done((bf16[4,10,512]{2,1,0:T(8,128)(2,1)S(1)}, bf16[4,10,512]{2,1,0:T(8,128)(2,1)S(1)}, u32[]{:S(2)}, u32[]{:S(2)}) %collective-permute-start.3) | collective-permute-done | bytes 40992 | tf_op jit(solution)/shard_map/ppermute | solution.py:64
  10.4 0.0 copy-done
  10.4 0.0 copy-done.4
  10.4 0.0 copy-done.6
  10.4 2.4 %attention.1 = bf16[80,640]{1,0:T(8,128)(2,1)S(1)} custom-call(bf16[36,2,64,512]{3,2,1,0:T(8,128)(2,1)S(1)} %copy-done, f32[80,2304]{1,0:T(8,128)S(1)} %setup.1.bias_ref, bf16[10,2,512]{2,1,0:T(2,128)(2,1)S(1)} %copy-done.6, bf16[10,2048]{1,0:T(8,128)(2,1)S(1)} %copy-done.4, bf16[4,10,512]{2,1,0:T(8,128)(2,1)S(1)} %join_queries.1.refs_0_, ...), custom_call_target="tpu_custom_call" | custom-call | flops 1000 | bytes 100000 | tf_op jit(solution)/shard_map/attention/pallas_call | solution.py:48
  12.8 10.7 %all-gather = bf16[640,640]{1,0:T(8,128)(2,1)S(1)} all-gather(bf16[80,640]{1,0:T(8,128)(2,1)S(1)} %attention.1), channel_id=2, replica_groups=mesh['head'=4,'pool'=8] {'pool'}, dimensions={0}, use_global_device_ids=true | all-gather | bytes 921600 | tf_op jit(solution)/shard_map/all_gather | solution.py:529
  23.5 1.0 %merge_project.1 = (f32[80,512]{1,0:T(8,128)S(1)}, bf16[80,512]{1,0:T(8,128)(2,1)S(1)}, bf16[80,512]{1,0:T(8,128)(2,1)S(1)}, bf16[80,512]{1,0:T(8,128)(2,1)S(1)}) custom-call(bf16[8,80,640]{2,1,0:T(8,128)(2,1)S(1)} %bitcast.12, bf16[512,2048]{1,0:T(8,128)(2,1)S(1)} %copy-done.2), custom_call_target="tpu_custom_call" | custom-call | flops 1000 | bytes 100000 | tf_op jit(solution)/shard_map/merge_project/pallas_call | solution.py:48
  24.5 1.6 %collective-permute-start.4 = (bf16[80,512]{1,0:T(8,128)(2,1)S(1)}, bf16[80,512]{1,0:T(8,128)(2,1)S(1)}, u32[]{:S(2)}, u32[]{:S(2)}) collective-permute-start(bf16[80,512]{1,0:T(8,128)(2,1)S(1)} %get-tuple-element.31), channel_id=1, source_target_pairs={{0,8},{8,0},{16,24},{24,16},{1,9},{9,1},{17,25},{25,17},{2,10},{10... | collective-permute-start | bytes 245768 | tf_op jit(solution)/shard_map/ppermute | solution.py:64
  26.1 2.6 %collective-permute-start.5 = (bf16[80,512]{1,0:T(8,128)(2,1)S(1)}, bf16[80,512]{1,0:T(8,128)(2,1)S(1)}, u32[]{:S(2)}, u32[]{:S(2)}) collective-permute-start(bf16[80,512]{1,0:T(8,128)(2,1)S(1)} %get-tuple-element.32), channel_id=1, source_target_pairs={{0,16},{8,24},{16,0},{24,8},{1,17},{9,25},{17,1},{25,9},{2,18},{10... | collective-permute-start | bytes 245768 | tf_op jit(solution)/shard_map/ppermute | solution.py:64
  28.7 0.2 collective-permute-start.6
  29.0 5.1 %routing.1 = (bf16[144,80]{1,0:T(8,128)(2,1)S(1)}, bf16[128,80]{1,0:T(8,128)(2,1)S(1)}, bf16[128,80]{1,0:T(8,128)(2,1)S(1)}, bf16[512,1024]{1,0:T(8,128)(2,1)S(1...) custom-call(s32[6,80]{1,0:T(8,128)S(1)} %bitcast.24, f32[6,80]{1,0:T(8,128)S(1)} %bitcast.25, ...), custom_call_target="tpu_custom_call" | custom-call | flops 1000 | bytes 20000000 | tf_op jit(solution)/shard_map/routing/pallas_call | solution.py:48
  34.0 0.0 collective-permute-done.4.refs_0_
  34.0 1.6 %collective-permute-done.5.refs_1_ = bf16[80,512]{1,0:T(8,128)(2,1)S(1)} collective-permute-done((bf16[80,512]{1,0:T(8,128)(2,1)S(1)}, bf16[80,512]{1,0:T(8,128)(2,1)S(1)}, u32[]{:S(2)}, u32[]{:S(2)}) %collective-permute-start.5) | collective-permute-done | bytes 81952 | tf_op jit(solution)/shard_map/ppermute | solution.py:64
  35.6 0.0 collective-permute-done.6.refs_2_
  35.6 0.6 prepare.1
  36.2 1.8 %experts_2.1 = (bf16[72,1536]{1,0:T(8,128)(2,1)S(1)}, f32[4,8,1536]{2,1,0:T(8,128)S(1)}) custom-call(bf16[144,1024]{1,0:T(8,128)(2,1)S(1)} %get-tuple-element.34.gate_ref, bf16[144,1024]{1,0:T(8,128)(2,1)S(1)} %get-tuple-element.35.up_ref, bf16[144,128]{1,0:T(8,128)(2,1)S(1)} %get-tuple-element.36.side_ref, ...), custom_call_target="tpu_custom_call" | custom-call | flops 1000 | bytes 100000 | tf_op jit(solution)/shard_map/experts_2/pallas_call | solution.py:48
  38.0 1.7 %collective-permute-start.7 = (bf16[72,1536]{1,0:T(8,128)(2,1)S(1)}, bf16[72,1536]{1,0:T(8,128)(2,1)S(1)}, u32[]{:S(2)}, u32[]{:S(2)}) collective-permute-start(bf16[72,1536]{1,0:T(8,128)(2,1)S(1)} %get-tuple-element.40), channel_id=1, source_target_pairs={{0,8},{8,0},{16,24},{24,16},{1,9},{9,1},{17,25},{25,17},{2,10},{10... | collective-permute-start | bytes 663560 | tf_op jit(solution)/shard_map/ppermute | solution.py:64
  39.8 3.9 %experts_1.1.refs_1_.later_ref = bf16[72,1536]{1,0:T(8,128)(2,1)S(1)} custom-call(bf16[144,1024]{1,0:T(8,128)(2,1)S(1)} %get-tuple-element.34.gate_ref, bf16[144,1024]{1,0:T(8,128)(2,1)S(1)} %get-tuple-element.35.up_ref, bf16[144,128]{1,0:T(8,128)(2,1)S(1)} %get-tuple-element.36.side_ref, bf16[8,512,2,1408]{3,2,1,0:T(2,128)(2,1)} %weight_ref.12, ...), custom_call_target="tpu_custom_call" | custom-call | flops 1000 | bytes 100000 | tf_op jit(solution)/shard_map/experts_1/pallas_call | solution.py:48
  43.7 1.3 %experts_3.1.own_ref = bf16[72,1536]{1,0:T(8,128)(2,1)S(1)} custom-call(bf16[144,1024]{1,0:T(8,128)(2,1)S(1)} %get-tuple-element.34.gate_ref, bf16[144,1024]{1,0:T(8,128)(2,1)S(1)} %get-tuple-element.35.up_ref, bf16[144,128]{1,0:T(8,128)(2,1)S(1)} %get-tuple-element.36.side_ref, bf16[2,512,2,1408]{3,2,1,0:T(2,128)(2,1)S(1)} %get-tuple-element.39.weight_ref, ...), custom_call_target="tpu_custom_call" | custom-call | flops 1000 | bytes 100000 | tf_op jit(solution)/shard_map/experts_3/pallas_call | solution.py:48
  45.0 0.0 collective-permute-done.7.received_ref
  45.0 0.1 add_pair.1
  45.1 1.6 %collective-permute-start.9 = (bf16[72,1536]{1,0:T(8,128)(2,1)S(1)}, bf16[72,1536]{1,0:T(8,128)(2,1)S(1)}, u32[]{:S(2)}, u32[]{:S(2)}) collective-permute-start(bf16[72,1536]{1,0:T(8,128)(2,1)S(1)} %get-tuple-element.42), channel_id=1, source_target_pairs={{0,8},{8,0},{16,24},{24,16},{1,9},{9,1},{17,25},{25,17},{2,10},{10... | collective-permute-start | bytes 663560 | tf_op jit(solution)/shard_map/ppermute | solution.py:64
  46.7 1.9 %collective-permute-start.8 = (bf16[72,1536]{1,0:T(8,128)(2,1)S(1)}, bf16[72,1536]{1,0:T(8,128)(2,1)S(1)}, u32[]{:S(2)}, u32[]{:S(2)}) collective-permute-start(bf16[72,1536]{1,0:T(8,128)(2,1)S(1)} %get-tuple-element.41.refs_1_), channel_id=1, source_target_pairs={{0,24},{8,16},{16,8},{24,0},{1,25},{9,17},{17,9},{25,1},{2,26},{10... | collective-permute-start | bytes 663560 | tf_op jit(solution)/shard_map/ppermute | solution.py:64
  48.6 4.6 %experts_0.1.refs_0_ = bf16[72,1536]{1,0:T(8,128)(2,1)S(1)} custom-call(bf16[144,1024]{1,0:T(8,128)(2,1)S(1)} %get-tuple-element.34.gate_ref, bf16[144,1024]{1,0:T(8,128)(2,1)S(1)} %get-tuple-element.35.up_ref, bf16[144,128]{1,0:T(8,128)(2,1)S(1)} %get-tuple-element.36.side_ref, bf16[8,512,2,1408]{3,2,1,0:T(2,128)(2,1)} %weight_ref.12, ...), custom_call_target="tpu_custom_call" | custom-call | flops 1000 | bytes 100000 | tf_op jit(solution)/shard_map/experts_0/pallas_call | solution.py:48
  53.3 0.8 collective-permute-done.9.refs_2_
  54.0 2.9 %collective-permute-done.8.refs_1_ = bf16[72,1536]{1,0:T(8,128)(2,1)S(1)} collective-permute-done((bf16[72,1536]{1,0:T(8,128)(2,1)S(1)}, bf16[72,1536]{1,0:T(8,128)(2,1)S(1)}, u32[]{:S(2)}, u32[]{:S(2)}) %collective-permute-start.8) | collective-permute-done | bytes 221216 | tf_op jit(solution)/shard_map/ppermute | solution.py:64
  56.9 0.2 hidden.1.hidden_ref.refs_0_
  57.1 3.2 %collective-permute-start.11 = (bf16[36,1408]{1,0:T(8,128)(2,1)S(1)}, bf16[36,1408]{1,0:T(8,128)(2,1)S(1)}, u32[]{:S(2)}, u32[]{:S(2)}) collective-permute-start(bf16[36,1408]{1,0:T(8,128)(2,1)S(1)} %hidden.1.hidden_ref.refs_0_), channel_id=1, source_target_pairs={{0,16},{8,24},{16,0},{24,8},{1,17},{9,25},{17,1},{25,9},{2,18},{10... | collective-permute-start | bytes 304136 | tf_op jit(solution)/shard_map/ppermute | solution.py:64
  60.3 0.0 collective-permute-start.10
  60.3 1.5 %collective-permute-start.12 = (bf16[36,1408]{1,0:T(8,128)(2,1)S(1)}, bf16[36,1408]{1,0:T(8,128)(2,1)S(1)}, u32[]{:S(2)}, u32[]{:S(2)}) collective-permute-start(bf16[36,1408]{1,0:T(8,128)(2,1)S(1)} %hidden.1.hidden_ref.refs_0_), channel_id=1, source_target_pairs={{0,24},{8,16},{16,8},{24,0},{1,25},{9,17},{17,9},{25,1},{2,26},{10... | collective-permute-start | bytes 304136 | tf_op jit(solution)/shard_map/ppermute | solution.py:64
  61.9 0.0 slice-done.1
  61.9 0.5 down_0.1.refs_4_
  62.4 2.6 %collective-permute-done.11.hidden_ref.refs_2_ = bf16[36,1408]{1,0:T(8,128)(2,1)S(1)} collective-permute-done((bf16[36,1408]{1,0:T(8,128)(2,1)S(1)}, bf16[36,1408]{1,0:T(8,128)(2,1)S(1)}, u32[]{:S(2)}, u32[]{:S(2)}) %collective-permute-start.11) | collective-permute-done | bytes 101408 | tf_op jit(solution)/shard_map/ppermute | solution.py:64
  65.0 0.5 down_2.1.refs_6_
  65.4 1.8 %collective-permute-done.10.hidden_ref.refs_1_ = bf16[36,1408]{1,0:T(8,128)(2,1)S(1)} collective-permute-done((bf16[36,1408]{1,0:T(8,128)(2,1)S(1)}, bf16[36,1408]{1,0:T(8,128)(2,1)S(1)}, u32[]{:S(2)}, u32[]{:S(2)}) %collective-permute-start.10) | collective-permute-done | bytes 101408 | tf_op jit(solution)/shard_map/ppermute | solution.py:64
  67.3 0.5 down_1.1.refs_5_
  67.8 0.0 collective-permute-done.12.refs_3_
  67.8 0.0 slice-start.4
  67.8 0.0 copy-start.8
  67.8 0.9 %combine.1 = (bf16[8,10,512]{2,1,0:T(8,128)(2,1)S(1)}, f32[4,4,512]{2,1,0:T(4,128)S(1)}) custom-call(bf16[128,80]{1,0:T(8,128)(2,1)S(1)} %get-tuple-element.27.coarse_ref, bf16[128,80]{1,0:T(8,128)(2,1)S(1)} %get-tuple-element.28.fine_ref, bf16[8,1408,512]{2,1,0:T(8,128)(2,1)S(1)} %bitcast.9, bf16[1,1408,512]{2,1,0:T(8,128)(2,1)S(1)} %copy-done.3, ...), custom_call_target="tpu_custom_call" | custom-call | flops 1000 | bytes 100000 | tf_op jit(solution)/shard_map/combine/pallas_call | solution.py:48
  68.7 8.2 %all_to_all.5.pieces_ref = bf16[8,10,512]{2,1,0:T(8,128)(2,1)S(1)} all-to-all(bf16[8,10,512]{2,1,0:T(8,128)(2,1)S(1)} %get-tuple-element.43), channel_id=1, replica_groups=mesh['head'=4,'pool'=8] {'pool'}, dimensions={0} | all-to-all | bytes 163840 | tf_op jit(solution)/shard_map/all_to_all | solution.py:643
  76.9 1.5 %collective-permute-start.15 = (bf16[10,512]{1,0:T(8,128)(2,1)S(1)}, bf16[10,512]{1,0:T(8,128)(2,1)S(1)}, u32[]{:S(2)}, u32[]{:S(2)}) collective-permute-start(bf16[10,512]{1,0:T(8,128)(2,1)S(1)} %block.1.refs_0_.refs_4_), channel_id=1, source_target_pairs={{0,24},{8,16},{16,8},{24,0},{1,25},{9,17},{17,9},{25,1},{2,26},{10... | collective-permute-start | bytes 30728 | tf_op jit(solution)/shard_map/ppermute | solution.py:64
  78.4 0.5 collective-permute-start.14
  78.9 2.5 %collective-permute-start.13 = (bf16[10,512]{1,0:T(8,128)(2,1)S(1)}, bf16[10,512]{1,0:T(8,128)(2,1)S(1)}, u32[]{:S(2)}, u32[]{:S(2)}) collective-permute-start(bf16[10,512]{1,0:T(8,128)(2,1)S(1)} %block.1.refs_0_.refs_4_), channel_id=1, source_target_pairs={{0,8},{8,0},{16,24},{24,16},{1,9},{9,1},{17,25},{25,17},{2,10},{10... | collective-permute-start | bytes 30728 | tf_op jit(solution)/shard_map/ppermute | solution.py:64
  81.4 0.3 project_0.1
  81.7 0.9 %collective-permute-done.15.refs_0_.refs_7_ = bf16[10,512]{1,0:T(8,128)(2,1)S(1)} collective-permute-done((bf16[10,512]{1,0:T(8,128)(2,1)S(1)}, bf16[10,512]{1,0:T(8,128)(2,1)S(1)}, u32[]{:S(2)}, u32[]{:S(2)}) %collective-permute-start.15) | collective-permute-done | bytes 10272 | tf_op jit(solution)/shard_map/ppermute | solution.py:64
  82.7 0.3 project_3.1
  83.0 0.1 collective-permute-done.14.refs_1_.refs_6_
  83.1 0.2 collective-permute-done.13.refs_0_.refs_5_
  83.2 1.2 %project.1 = (bf16[10,2048]{1,0:T(8,128)(2,1)}, bf16[10,1536]{1,0:T(8,128)(2,1)}) custom-call(bf16[16,128]{1,0:T(8,128)(2,1)S(1)} %bitcast.22, bf16[2048,1536]{1,0:T(8,128)(2,1)S(1)} %bitcast.11, bf16[10,512]{1,0:T(8,128)(2,1)S(1)} %collective-permute-done.13.refs_0_.refs_5_, bf16[10,512]{1,0:T(8,128)(2,1)S(1)} %collective-permute-done.14.refs_1_.refs_6_, ...), custom_call_target="tpu_custom_call" | custom-call | flops 1000 | bytes 100000 | tf_op jit(solution)/shard_map/project/pallas_call | solution.py:48
  (29 shorter events, 0.1 us)
Async XLA Ops:
  0.6 6.9 %collective-permute-start.2 = (bf16[1,10,512]{2,1,0:T(8,128)(2,1)}, bf16[1,10,512]{2,1,0:T(8,128)(2,1)S(1)}, u32[]{:S(2)}, u32[]{:S(2)}) collective-permute-start(bf16[1,10,512]{2,1,0:T(8,128)(2,1)} %bitcast.15), channel_id=1, source_target_pairs={{0,6},{1,7},{2,4},{3,5},{4,2},{5,3},{6,0},{7,1},{8,14},{9,15},{10,... | collective-permute-start | bytes 30728 | tf_op jit(solution)/shard_map/ppermute | solution.py:64
  4.6 3.9 %collective-permute-start.1 = (bf16[1,10,512]{2,1,0:T(8,128)(2,1)}, bf16[1,10,512]{2,1,0:T(8,128)(2,1)S(1)}, u32[]{:S(2)}, u32[]{:S(2)}) collective-permute-start(bf16[1,10,512]{2,1,0:T(8,128)(2,1)} %bitcast.16), channel_id=1, source_target_pairs={{0,4},{1,5},{2,6},{3,7},{4,0},{5,1},{6,2},{7,3},{8,12},{9,13},{10,... | collective-permute-start | bytes 30728 | tf_op jit(solution)/shard_map/ppermute | solution.py:64
  5.1 3.9 %collective-permute-start = (bf16[1,10,512]{2,1,0:T(8,128)(2,1)}, bf16[1,10,512]{2,1,0:T(8,128)(2,1)S(1)}, u32[]{:S(2)}, u32[]{:S(2)}) collective-permute-start(bf16[1,10,512]{2,1,0:T(8,128)(2,1)} %bitcast.17), channel_id=1, source_target_pairs={{0,2},{1,3},{2,0},{3,1},{4,6},{5,7},{6,4},{7,5},{8,10},{9,11},{10,... | collective-permute-start | bytes 30728 | tf_op jit(solution)/shard_map/ppermute | solution.py:64
  5.2 0.8 copy-start.5
  5.2 0.8 copy-start.12
  5.2 3.8 %copy-start.7 = (bf16[10,512]{1,0:T(8,128)(2,1)S(1)}, bf16[10,512]{1,0:T(8,128)(2,1)}, u32[]{:S(2)}) copy-start(bf16[10,512]{1,0:T(8,128)(2,1)} %param.16) | copy-start | bytes 30724
  5.2 5.1 %copy-start = (bf16[36,2,64,512]{3,2,1,0:T(8,128)(2,1)S(1)}, bf16[36,2,64,512]{3,2,1,0:T(8,128)(2,1)}, u32[]{:S(2)}) copy-start(bf16[36,2,64,512]{3,2,1,0:T(8,128)(2,1)} %cache_ref.1) | copy-start | bytes 14155780
  5.2 5.1 %copy-start.4 = (bf16[10,2048]{1,0:T(8,128)(2,1)S(1)}, bf16[10,2048]{1,0:T(8,128)(2,1)}, u32[]{:S(2)}) copy-start(bf16[10,2048]{1,0:T(8,128)(2,1)} %residual_ref.1) | copy-start | bytes 122884
  5.3 5.1 %copy-start.6 = (bf16[10,2,512]{2,1,0:T(2,128)(2,1)S(1)}, bf16[10,2,512]{2,1,0:T(2,128)(2,1)}, u32[]{:S(2)}) copy-start(bf16[10,2,512]{2,1,0:T(2,128)(2,1)} %fresh_ref.1) | copy-start | bytes 61444
  6.0 17.5 %copy-start.2 = (bf16[512,2048]{1,0:T(8,128)(2,1)S(1)}, bf16[512,2048]{1,0:T(8,128)(2,1)}, u32[]{:S(2)}) copy-start(bf16[512,2048]{1,0:T(8,128)(2,1)} %weight_ref.10) | copy-start | bytes 6291460
  6.0 22.9 %copy-start.10 = (s32[80,6]{0,1:T(8,128)S(1)}, s32[80,6]{0,1:T(8,128)}, u32[]{:S(2)}) copy-start(s32[80,6]{0,1:T(8,128)} %param.24) | copy-start | bytes 5764
  6.0 22.9 %copy-start.11 = (f32[80,6]{0,1:T(8,128)S(1)}, f32[80,6]{0,1:T(8,128)}, u32[]{:S(2)}) copy-start(f32[80,6]{0,1:T(8,128)} %param.25) | copy-start | bytes 5764
  9.1 1.3 %collective-permute-start.3 = (bf16[4,10,512]{2,1,0:T(8,128)(2,1)S(1)}, bf16[4,10,512]{2,1,0:T(8,128)(2,1)S(1)}, u32[]{:S(2)}, u32[]{:S(2)}) collective-permute-start(bf16[4,10,512]{2,1,0:T(8,128)(2,1)S(1)} %join_queries.1.refs_0_), channel_id=1, source_target_pairs={{0,1},{1,0},{2,3},{3,2},{4,5},{5,4},{6,7},{7,6},{8,9},{9,8},{10,11... | collective-permute-start | bytes 122888 | tf_op jit(solution)/shard_map/ppermute | solution.py:64
  24.5 9.6 %collective-permute-start.4 = (bf16[80,512]{1,0:T(8,128)(2,1)S(1)}, bf16[80,512]{1,0:T(8,128)(2,1)S(1)}, u32[]{:S(2)}, u32[]{:S(2)}) collective-permute-start(bf16[80,512]{1,0:T(8,128)(2,1)S(1)} %get-tuple-element.31), channel_id=1, source_target_pairs={{0,8},{8,0},{16,24},{24,16},{1,9},{9,1},{17,25},{25,17},{2,10},{10... | collective-permute-start | bytes 245768 | tf_op jit(solution)/shard_map/ppermute | solution.py:64
  26.1 9.5 %collective-permute-start.5 = (bf16[80,512]{1,0:T(8,128)(2,1)S(1)}, bf16[80,512]{1,0:T(8,128)(2,1)S(1)}, u32[]{:S(2)}, u32[]{:S(2)}) collective-permute-start(bf16[80,512]{1,0:T(8,128)(2,1)S(1)} %get-tuple-element.32), channel_id=1, source_target_pairs={{0,16},{8,24},{16,0},{24,8},{1,17},{9,25},{17,1},{25,9},{2,18},{10... | collective-permute-start | bytes 245768 | tf_op jit(solution)/shard_map/ppermute | solution.py:64
  28.7 6.9 %collective-permute-start.6 = (bf16[80,512]{1,0:T(8,128)(2,1)S(1)}, bf16[80,512]{1,0:T(8,128)(2,1)S(1)}, u32[]{:S(2)}, u32[]{:S(2)}) collective-permute-start(bf16[80,512]{1,0:T(8,128)(2,1)S(1)} %get-tuple-element.33), channel_id=1, source_target_pairs={{0,24},{8,16},{16,8},{24,0},{1,25},{9,17},{17,9},{25,1},{2,26},{10... | collective-permute-start | bytes 245768 | tf_op jit(solution)/shard_map/ppermute | solution.py:64
  28.9 6.7 %copy-start.9 = (bf16[2048]{0:T(1024)(128)(2,1)S(1)}, bf16[2048]{0:T(1024)(128)(2,1)}, u32[]{:S(2)}) copy-start(bf16[2048]{0:T(1024)(128)(2,1)} %param.23) | copy-start | bytes 12292
  28.9 7.3 %copy-start.1 = (bf16[1,512,2,1408]{3,2,1,0:T(2,128)(2,1)S(1)}, bf16[1,512,2,1408]{3,2,1,0:T(2,128)(2,1)}, u32[]{:S(2)}) copy-start(bf16[1,512,2,1408]{3,2,1,0:T(2,128)(2,1)} %refs_0_.1) | copy-start | bytes 8650756
  38.0 7.0 %collective-permute-start.7 = (bf16[72,1536]{1,0:T(8,128)(2,1)S(1)}, bf16[72,1536]{1,0:T(8,128)(2,1)S(1)}, u32[]{:S(2)}, u32[]{:S(2)}) collective-permute-start(bf16[72,1536]{1,0:T(8,128)(2,1)S(1)} %get-tuple-element.40), channel_id=1, source_target_pairs={{0,8},{8,0},{16,24},{24,16},{1,9},{9,1},{17,25},{25,17},{2,10},{10... | collective-permute-start | bytes 663560 | tf_op jit(solution)/shard_map/ppermute | solution.py:64
  45.1 8.9 %collective-permute-start.9 = (bf16[72,1536]{1,0:T(8,128)(2,1)S(1)}, bf16[72,1536]{1,0:T(8,128)(2,1)S(1)}, u32[]{:S(2)}, u32[]{:S(2)}) collective-permute-start(bf16[72,1536]{1,0:T(8,128)(2,1)S(1)} %get-tuple-element.42), channel_id=1, source_target_pairs={{0,8},{8,0},{16,24},{24,16},{1,9},{9,1},{17,25},{25,17},{2,10},{10... | collective-permute-start | bytes 663560 | tf_op jit(solution)/shard_map/ppermute | solution.py:64
  46.7 15.2 %slice-start = ((s8[11534336]{0:T(1024)(128)(4,1)}), s8[4194304]{0:T(1024)(128)(4,1)S(1)}, s32[]{:S(2)}) async-start(s8[11534336]{0:T(1024)(128)(4,1)} %bitcast.8), calls=%async_computation.1 | async-start | bytes 8388608
  46.7 15.2 %slice-start.1 = ((s8[11534336]{0:T(1024)(128)(4,1)}), s8[4194304]{0:T(1024)(128)(4,1)S(1)}, s32[]{:S(2)}) async-start(s8[11534336]{0:T(1024)(128)(4,1)} %bitcast.8), calls=%async_computation.2 | async-start | bytes 8388608
  46.7 15.2 %slice-start.2 = ((s8[11534336]{0:T(1024)(128)(4,1)}), s8[3145728]{0:T(1024)(128)(4,1)S(1)}, s32[]{:S(2)}) async-start(s8[11534336]{0:T(1024)(128)(4,1)} %bitcast.8), calls=%async_computation.3 | async-start | bytes 6291456
  46.7 10.2 %collective-permute-start.8 = (bf16[72,1536]{1,0:T(8,128)(2,1)S(1)}, bf16[72,1536]{1,0:T(8,128)(2,1)S(1)}, u32[]{:S(2)}, u32[]{:S(2)}) collective-permute-start(bf16[72,1536]{1,0:T(8,128)(2,1)S(1)} %get-tuple-element.41.refs_1_), channel_id=1, source_target_pairs={{0,24},{8,16},{16,8},{24,0},{1,25},{9,17},{17,9},{25,1},{2,26},{10... | collective-permute-start | bytes 663560 | tf_op jit(solution)/shard_map/ppermute | solution.py:64
  57.1 7.8 %collective-permute-start.11 = (bf16[36,1408]{1,0:T(8,128)(2,1)S(1)}, bf16[36,1408]{1,0:T(8,128)(2,1)S(1)}, u32[]{:S(2)}, u32[]{:S(2)}) collective-permute-start(bf16[36,1408]{1,0:T(8,128)(2,1)S(1)} %hidden.1.hidden_ref.refs_0_), channel_id=1, source_target_pairs={{0,16},{8,24},{16,0},{24,8},{1,17},{9,25},{17,1},{25,9},{2,18},{10... | collective-permute-start | bytes 304136 | tf_op jit(solution)/shard_map/ppermute | solution.py:64
  60.3 6.9 %collective-permute-start.10 = (bf16[36,1408]{1,0:T(8,128)(2,1)S(1)}, bf16[36,1408]{1,0:T(8,128)(2,1)S(1)}, u32[]{:S(2)}, u32[]{:S(2)}) collective-permute-start(bf16[36,1408]{1,0:T(8,128)(2,1)S(1)} %hidden.1.hidden_ref.refs_0_), channel_id=1, source_target_pairs={{0,8},{8,0},{16,24},{24,16},{1,9},{9,1},{17,25},{25,17},{2,10},{10... | collective-permute-start | bytes 304136 | tf_op jit(solution)/shard_map/ppermute | solution.py:64
  60.3 7.4 %collective-permute-start.12 = (bf16[36,1408]{1,0:T(8,128)(2,1)S(1)}, bf16[36,1408]{1,0:T(8,128)(2,1)S(1)}, u32[]{:S(2)}, u32[]{:S(2)}) collective-permute-start(bf16[36,1408]{1,0:T(8,128)(2,1)S(1)} %hidden.1.hidden_ref.refs_0_), channel_id=1, source_target_pairs={{0,24},{8,16},{16,8},{24,0},{1,25},{9,17},{17,9},{25,1},{2,26},{10... | collective-permute-start | bytes 304136 | tf_op jit(solution)/shard_map/ppermute | solution.py:64
  65.4 2.3 %copy-start.3 = (bf16[1,1408,512]{2,1,0:T(8,128)(2,1)S(1)}, bf16[1,1408,512]{2,1,0:T(8,128)(2,1)}, u32[]{:S(2)}) copy-start(bf16[1,1408,512]{2,1,0:T(8,128)(2,1)} %shared_weight_ref.1) | copy-start | bytes 4325380
  67.3 14.1 %slice-start.3 = ((s8[6291456]{0:T(1024)(128)(4,1)}), s8[4194304]{0:T(1024)(128)(4,1)S(1)}, s32[]{:S(2)}) async-start(s8[6291456]{0:T(1024)(128)(4,1)} %bitcast.10), calls=%async_computation.4 | async-start | bytes 8388608
  67.8 13.6 %slice-start.4 = ((s8[6291456]{0:T(1024)(128)(4,1)}), s8[2097152]{0:T(1024)(128)(4,1)S(1)}, s32[]{:S(2)}) async-start(s8[6291456]{0:T(1024)(128)(4,1)} %bitcast.10), calls=%async_computation.5 | async-start | bytes 4194304
  67.8 13.6 %copy-start.8 = (bf16[2048]{0:T(1024)(128)(2,1)S(1)}, bf16[2048]{0:T(1024)(128)(2,1)}, u32[]{:S(2)}) copy-start(bf16[2048]{0:T(1024)(128)(2,1)} %param.30) | copy-start | bytes 12292
  76.9 5.7 %collective-permute-start.15 = (bf16[10,512]{1,0:T(8,128)(2,1)S(1)}, bf16[10,512]{1,0:T(8,128)(2,1)S(1)}, u32[]{:S(2)}, u32[]{:S(2)}) collective-permute-start(bf16[10,512]{1,0:T(8,128)(2,1)S(1)} %block.1.refs_0_.refs_4_), channel_id=1, source_target_pairs={{0,24},{8,16},{16,8},{24,0},{1,25},{9,17},{17,9},{25,1},{2,26},{10... | collective-permute-start | bytes 30728 | tf_op jit(solution)/shard_map/ppermute | solution.py:64
  78.4 4.7 %collective-permute-start.14 = (bf16[10,512]{1,0:T(8,128)(2,1)S(1)}, bf16[10,512]{1,0:T(8,128)(2,1)S(1)}, u32[]{:S(2)}, u32[]{:S(2)}) collective-permute-start(bf16[10,512]{1,0:T(8,128)(2,1)S(1)} %block.1.refs_0_.refs_4_), channel_id=1, source_target_pairs={{0,16},{8,24},{16,0},{24,8},{1,17},{9,25},{17,1},{25,9},{2,18},{10... | collective-permute-start | bytes 30728 | tf_op jit(solution)/shard_map/ppermute | solution.py:64
  78.9 4.4 %collective-permute-start.13 = (bf16[10,512]{1,0:T(8,128)(2,1)S(1)}, bf16[10,512]{1,0:T(8,128)(2,1)S(1)}, u32[]{:S(2)}, u32[]{:S(2)}) collective-permute-start(bf16[10,512]{1,0:T(8,128)(2,1)S(1)} %block.1.refs_0_.refs_4_), channel_id=1, source_target_pairs={{0,8},{8,0},{16,24},{24,16},{1,9},{9,1},{17,25},{25,17},{2,10},{10... | collective-permute-start | bytes 30728 | tf_op jit(solution)/shard_map/ppermute | solution.py:64

commit v6 on v5

--- a/solution.py
+++ b/solution.py
@@ -279,12 +279,12 @@
     )
 
 
-def prepare_kernel(req_dev, gain_ref, pick_ref, spread_ref, own_sum_ref, *refs):
+def prepare_kernel(req_dev, part, share, gain_ref, pick_ref, spread_ref, own_sum_ref, *refs):
     received, (gate_ref, up_ref, side_ref, after_ref, all_ref) = refs[:-5], refs[-5:]
     req_total, col_part = own_sum_ref.shape
     after = own_sum_ref[...]
-    for part in received:
-        after = after + part[...].astype(f32)
+    for ref in received:
+        after = after + ref[...].astype(f32)
     for place in range(all_ref.shape[0]):
         all_ref[place] = after[place * req_dev : (place + 1) * req_dev]
     after_ref[...] = all_ref[lax.axis_index("pool")]
@@ -296,7 +296,18 @@
     side = jnp.where(lane == 0, coarse, jnp.where(lane == 1, squares - coarse, 0.0))
     pick = pick_ref[...]
     picked = dot(pick, scaled).astype(bf16)
-    side_ref[...] = dot(pick, side.astype(bf16)).astype(bf16)
+    same = iota((req_total, req_total), 0) == iota((req_total, req_total), 1)
+    turned = lax.dot_general(
+        side.astype(bf16), one_hot(same), over_rows, preferred_element_type=f32
+    )[:8].astype(bf16)
+    contract = (((1,), (1,)), ((), ()))
+    lined = lax.dot_general(turned, pick, contract, preferred_element_type=f32)
+    targets = side_ref.shape[0]
+    for target in range(targets):
+        first = targets * part + target * share
+        side_ref[target] = jnp.zeros(side_ref.shape[1:], f32)
+        side_ref[target, :, :part] = lined[:, target * part : (target + 1) * part]
+        side_ref[target, :, part : part + share] = lined[:, first : first + share]
     spread = dot(picked, spread_ref[...])
     gate_ref[...] = spread.astype(bf16)
     up_ref[...] = pltpu.roll(spread, 1, 1).astype(bf16)
@@ -319,17 +330,14 @@
     if makes_shared:
         shared_weight_ref, out_ref, shared_ref = refs
         share = shared_ref.shape[1] // 2
-        extra = share * head_devs
-        first = gate_ref.shape[0] - extra
+        extra = gate_ref.shape[0] - part * head_devs
+        first = part * head_devs
         lhs = jnp.concatenate([gate_ref[first:, :], up_ref[first:, :]], axis=0)
         sums = dot(lhs, shared_weight_ref[0].reshape(2 * depth, ffe))
-        side = side_ref[first:, :].astype(f32)
         for place in range(head_devs):
             rows = slice(place * share, (place + 1) * share)
-            shared_ref[place, :share, :ffe] = sums[:extra][rows]
-            shared_ref[place, share:, :ffe] = sums[extra:][rows]
-            shared_ref[place, :share, ffe:] = side[rows]
-            shared_ref[place, share:, ffe:] = side[rows]
+            shared_ref[place, :share, :] = sums[:extra][rows]
+            shared_ref[place, share:, :] = sums[extra:][rows]
     else:
         shared_ref, out_ref = refs[0], refs[-1]
     each = min(slots, part)
@@ -337,10 +345,11 @@
         rows = pl.ds(pl.multiple_of(target * part + i * each, TILE), each)
         lhs = jnp.concatenate([gate_ref[rows, :], up_ref[rows, :]], axis=0)
         sums = dot(lhs, weight_ref[i].reshape(2 * depth, ffe))
-        out_ref[2 * i * each : 2 * (i + 1) * each, :ffe] = sums.astype(bf16)
-        for k in (2 * i, 2 * i + 1):
-            out_ref[k * each : (k + 1) * each, ffe:] = side_ref[rows, :]
-    out_ref[2 * part :, :] = shared_ref[target].astype(bf16)
+        out_ref[2 * i * each : 2 * (i + 1) * each, :] = sums.astype(bf16)
+    side = side_ref[target][:2]
+    side = jnp.concatenate([side, jnp.zeros((2, ffe - LANES), f32)], axis=1)
+    last = jnp.concatenate([shared_ref[target], side], axis=0)
+    out_ref[2 * part :, :] = last.astype(bf16)
 
 
 def add_kernel(own_ref, received_ref, later_ref, out_ref, sent_ref):
@@ -350,14 +359,15 @@
 
 def hidden_kernel(width, part, each, *refs):
     parts, out_ref = refs[:-1], refs[-1]
-    ffe = out_ref.shape[1]
     total = functools.reduce(jnp.add, [ref[...].astype(f32) for ref in parts])
+    side = total[-2:-1, :LANES] + total[-1:, :LANES]
     blocks = [(2 * i * each, i * each, each) for i in range(part // each)]
     for start, row, count in blocks + [(2 * part, part, out_ref.shape[0] - part)]:
         gates, ups = total[start : start + count], total[start + count : start + 2 * count]
-        squares = gates[:, ffe : ffe + 1] + gates[:, ffe + 1 : ffe + 2]
+        found = iota((count, LANES), 1) == iota((count, LANES), 0) + row
+        squares = jnp.sum(jnp.where(found, side, 0.0), axis=1, keepdims=True)
         row_scale = lax.rsqrt(squares / width + epsilon)
-        gates, ups = gates[:, :ffe] * row_scale, ups[:, :ffe] * row_scale
+        gates, ups = gates * row_scale, ups * row_scale
         out_ref[row : row + count, :] = (gates / (1.0 + jnp.exp(-gates)) * ups).astype(bf16)
 
 
@@ -474,6 +484,7 @@
     slots = min(MOST * pools, req_total)
     slot_total = exp_dev * slots
     extra = -(-req_dev // TILE) * TILE
+    part, share = slot_total // head_devs, -(-req_dev // head_devs)
     small = pools <= 8
     distances = list(range(1, head_devs))
     piece_experts = max(1, exp_dev // head_devs)
@@ -554,12 +565,12 @@
     weights = dict(zip(fetched, weights))
     received = {d: swap(sums[d], "head", d) for d in reversed(distances)}
     gate_rows, up_rows, side, own_after = call(
-        functools.partial(prepare_kernel, req_dev),
+        functools.partial(prepare_kernel, req_dev, part, share),
         "prepare",
         [
             ((slot_total + extra, 2 * col_part), bf16),
             ((slot_total + extra, 2 * col_part), bf16),
-            ((slot_total + extra, LANES), bf16),
+            ((head_devs, 8, LANES), f32),
             ((req_dev, col_part), f32),
         ],
         [norm_gain.reshape(-1, LANES), pick, spread, sums[0]] + [received[d] for d in distances],
@@ -567,10 +578,9 @@
         megabytes=6,
     )
 
-    piece = slot_total // head_devs + extra // head_devs
-    part = slot_total // head_devs
-    piece_shape = ((2 * piece, ffe + LANES), bf16)
-    shared_shape = ((head_devs, 2 * extra // head_devs, ffe + LANES), f32)
+    piece = part + share
+    piece_shape = ((2 * piece + 2, ffe), bf16)
+    shared_shape = ((head_devs, 2 * share, ffe), f32)
     shared_rows = None
     last = head_devs - 1
 
@@ -633,7 +643,7 @@
     routed, shared_out = call(
         functools.partial(combine_kernel, last, slots),
         "combine",
-        [((pools, req_dev, col_part), bf16), ((head_devs, extra // head_devs, col_part), f32)],
+        [((pools, req_dev, col_part), bf16), ((head_devs, share, col_part), f32)],
         [gate_coarse, gate_fine, w_down, shared_down]
         + [hiddens[d] for d in range(head_devs)]
         + done,

time: 84.6 us -> 83.9 us (level)
  no operation moved by 1% of the time
where the time goes in v6:
time: 83.9 us; the launch traced here: 83.7 us
  Pallas kernels  27.3 us (33%)
  starting transfers between devices  23.6 us (28%)
  blocking collectives  18.7 us (22%)
  waiting for transfers between devices  13 us (15%)
    pallas_call x21, Pallas kernels, call(): pl.pallas_call(kernel, out_shape=[jax.ShapeDtypeStruct(shape, dtype) for...  27.3 us
    ppermute x16, starting transfers between devices, swap(): return lax.ppermute(value, axis, [(i, i ^ distance) for i in range(count)])  23.6 us
    ppermute x16, waiting for transfers between devices, swap(): return lax.ppermute(value, axis, [(i, i ^ distance) for i in range(count)])  13 us
    all_gather x1, blocking collectives, per_device(): parts = lax.all_gather(partial, 'pool', axis=0)  10.7 us
    all_to_all x1, blocking collectives, per_device(): pieces = lax.all_to_all(routed, 'pool', 0, 0)  7.99 us
  transfers between devices with their start and end apart: 16, of which 11 were waited for; matrix products, arithmetic and copies ran while one was open for 0% of the time, Pallas kernels for 23%

profile of v6, /device:TPU:0, one launch (start us, length us, event | category | flops | bytes accessed | tf_op | source)
XLA Modules:
  0.0 83.7 jit_solution(2510097489831798844)
XLA Ops:
  0.6 4.0 %collective-permute-start.2 = (bf16[1,10,512]{2,1,0:T(8,128)(2,1)}, bf16[1,10,512]{2,1,0:T(8,128)(2,1)S(1)}, u32[]{:S(2)}, u32[]{:S(2)}) collective-permute-start(bf16[1,10,512]{2,1,0:T(8,128)(2,1)} %bitcast.15), channel_id=1, source_target_pairs={{0,6},{1,7},{2,4},{3,5},{4,2},{5,3},{6,0},{7,1},{8,14},{9,15},{10,... | collective-permute-start | bytes 30728 | tf_op jit(solution)/shard_map/ppermute | solution.py:64
  4.6 0.5 collective-permute-start.1
  5.1 0.1 collective-permute-start
  5.2 0.0 copy-start.4
  5.3 0.0 copy-start.6
  5.3 0.5 early.1.early_ref
  5.8 0.2 copy-done.5
  6.0 0.0 copy-done.12
  6.0 1.5 %setup.1.bias_ref = f32[80,2304]{1,0:T(8,128)S(1)} custom-call(s32[1]{0:T(128)} %early.1.early_ref, s32[64,80]{1,0:T(8,128)S(1)} %bitcast.14, s32[1,80]{1,0:T(1,128)S(1)} %bitcast.27), custom_call_target="tpu_custom_call" | custom-call | flops 1000 | bytes 100000 | tf_op jit(solution)/shard_map/setup/pallas_call | solution.py:48
  7.6 0.0 collective-permute-done.2.refs_3_
  7.6 1.0 %collective-permute-done.1.refs_2_ = bf16[1,10,512]{2,1,0:T(8,128)(2,1)S(1)} collective-permute-done((bf16[1,10,512]{2,1,0:T(8,128)(2,1)}, bf16[1,10,512]{2,1,0:T(8,128)(2,1)S(1)}, u32[]{:S(2)}, u32[]{:S(2)}) %collective-permute-start.1) | collective-permute-done | bytes 10272 | tf_op jit(solution)/shard_map/ppermute | solution.py:64
  8.5 0.5 collective-permute-done.refs_1_
  9.0 0.0 copy-done.7
  9.1 0.1 collective-permute-start.3
  9.1 1.2 %collective-permute-done.3.refs_1_ = bf16[4,10,512]{2,1,0:T(8,128)(2,1)S(1)} collective-permute-done((bf16[4,10,512]{2,1,0:T(8,128)(2,1)S(1)}, bf16[4,10,512]{2,1,0:T(8,128)(2,1)S(1)}, u32[]{:S(2)}, u32[]{:S(2)}) %collective-permute-start.3) | collective-permute-done | bytes 40992 | tf_op jit(solution)/shard_map/ppermute | solution.py:64
  10.4 0.0 copy-done
  10.4 0.0 copy-done.4
  10.4 2.4 %attention.1 = bf16[80,640]{1,0:T(8,128)(2,1)S(1)} custom-call(bf16[36,2,64,512]{3,2,1,0:T(8,128)(2,1)S(1)} %copy-done, f32[80,2304]{1,0:T(8,128)S(1)} %setup.1.bias_ref, bf16[10,2,512]{2,1,0:T(2,128)(2,1)S(1)} %copy-done.6, bf16[10,2048]{1,0:T(8,128)(2,1)S(1)} %copy-done.4, bf16[4,10,512]{2,1,0:T(8,128)(2,1)S(1)} %join_queries.1.refs_0_, ...), custom_call_target="tpu_custom_call" | custom-call | flops 1000 | bytes 100000 | tf_op jit(solution)/shard_map/attention/pallas_call | solution.py:48
  12.8 10.7 %all-gather = bf16[640,640]{1,0:T(8,128)(2,1)S(1)} all-gather(bf16[80,640]{1,0:T(8,128)(2,1)S(1)} %attention.1), channel_id=2, replica_groups=mesh['head'=4,'pool'=8] {'pool'}, dimensions={0}, use_global_device_ids=true | all-gather | bytes 921600 | tf_op jit(solution)/shard_map/all_gather | solution.py:540
  23.5 0.0 copy-done.2
  23.5 1.0 %merge_project.1 = (f32[80,512]{1,0:T(8,128)S(1)}, bf16[80,512]{1,0:T(8,128)(2,1)S(1)}, bf16[80,512]{1,0:T(8,128)(2,1)S(1)}, bf16[80,512]{1,0:T(8,128)(2,1)S(1)}) custom-call(bf16[8,80,640]{2,1,0:T(8,128)(2,1)S(1)} %bitcast.12, bf16[512,2048]{1,0:T(8,128)(2,1)S(1)} %copy-done.2), custom_call_target="tpu_custom_call" | custom-call | flops 1000 | bytes 100000 | tf_op jit(solution)/shard_map/merge_project/pallas_call | solution.py:48
  24.5 1.6 %collective-permute-start.4 = (bf16[80,512]{1,0:T(8,128)(2,1)S(1)}, bf16[80,512]{1,0:T(8,128)(2,1)S(1)}, u32[]{:S(2)}, u32[]{:S(2)}) collective-permute-start(bf16[80,512]{1,0:T(8,128)(2,1)S(1)} %get-tuple-element.31), channel_id=1, source_target_pairs={{0,8},{8,0},{16,24},{24,16},{1,9},{9,1},{17,25},{25,17},{2,10},{10... | collective-permute-start | bytes 245768 | tf_op jit(solution)/shard_map/ppermute | solution.py:64
  26.1 2.6 %collective-permute-start.5 = (bf16[80,512]{1,0:T(8,128)(2,1)S(1)}, bf16[80,512]{1,0:T(8,128)(2,1)S(1)}, u32[]{:S(2)}, u32[]{:S(2)}) collective-permute-start(bf16[80,512]{1,0:T(8,128)(2,1)S(1)} %get-tuple-element.32), channel_id=1, source_target_pairs={{0,16},{8,24},{16,0},{24,8},{1,17},{9,25},{17,1},{25,9},{2,18},{10... | collective-permute-start | bytes 245768 | tf_op jit(solution)/shard_map/ppermute | solution.py:64
  28.7 0.2 collective-permute-start.6
  28.9 0.0 copy-done.10
  29.0 5.1 %routing.1 = (bf16[144,80]{1,0:T(8,128)(2,1)S(1)}, bf16[128,80]{1,0:T(8,128)(2,1)S(1)}, bf16[128,80]{1,0:T(8,128)(2,1)S(1)}, bf16[512,1024]{1,0:T(8,128)(2,1)S(1...) custom-call(s32[6,80]{1,0:T(8,128)S(1)} %bitcast.24, f32[6,80]{1,0:T(8,128)S(1)} %bitcast.25, ...), custom_call_target="tpu_custom_call" | custom-call | flops 1000 | bytes 20000000 | tf_op jit(solution)/shard_map/routing/pallas_call | solution.py:48
  34.0 0.0 collective-permute-done.4.refs_0_
  34.0 1.6 %collective-permute-done.5.refs_1_ = bf16[80,512]{1,0:T(8,128)(2,1)S(1)} collective-permute-done((bf16[80,512]{1,0:T(8,128)(2,1)S(1)}, bf16[80,512]{1,0:T(8,128)(2,1)S(1)}, u32[]{:S(2)}, u32[]{:S(2)}) %collective-permute-start.5) | collective-permute-done | bytes 81952 | tf_op jit(solution)/shard_map/ppermute | solution.py:64
  35.6 0.0 collective-permute-done.6.refs_2_
  35.6 0.0 copy-done.9
  35.6 0.7 prepare.1
  36.3 1.8 %experts_2.1 = (bf16[72,1408]{1,0:T(8,128)(2,1)S(1)}, f32[4,6,1408]{2,1,0:T(8,128)S(1)}) custom-call(bf16[144,1024]{1,0:T(8,128)(2,1)S(1)} %get-tuple-element.34.gate_ref, bf16[144,1024]{1,0:T(8,128)(2,1)S(1)} %get-tuple-element.35.up_ref, f32[4,8,128]{2,1,0:T(8,128)S(1)} %get-tuple-element.36.side_ref, ...), custom_call_target="tpu_custom_call" | custom-call | flops 1000 | bytes 100000 | tf_op jit(solution)/shard_map/experts_2/pallas_call | solution.py:48
  38.2 1.7 %collective-permute-start.7 = (bf16[72,1408]{1,0:T(8,128)(2,1)S(1)}, bf16[72,1408]{1,0:T(8,128)(2,1)S(1)}, u32[]{:S(2)}, u32[]{:S(2)}) collective-permute-start(bf16[72,1408]{1,0:T(8,128)(2,1)S(1)} %get-tuple-element.40), channel_id=1, source_target_pairs={{0,8},{8,0},{16,24},{24,16},{1,9},{9,1},{17,25},{25,17},{2,10},{10... | collective-permute-start | bytes 608264 | tf_op jit(solution)/shard_map/ppermute | solution.py:64
  39.9 3.9 %experts_1.1.refs_1_.later_ref = bf16[72,1408]{1,0:T(8,128)(2,1)S(1)} custom-call(bf16[144,1024]{1,0:T(8,128)(2,1)S(1)} %get-tuple-element.34.gate_ref, bf16[144,1024]{1,0:T(8,128)(2,1)S(1)} %get-tuple-element.35.up_ref, f32[4,8,128]{2,1,0:T(8,128)S(1)} %get-tuple-element.36.side_ref, bf16[8,512,2,1408]{3,2,1,0:T(2,128)(2,1)} %weight_ref.12, ...), custom_call_target="tpu_custom_call" | custom-call | flops 1000 | bytes 100000 | tf_op jit(solution)/shard_map/experts_1/pallas_call | solution.py:48
  43.8 1.3 %experts_3.1.own_ref = bf16[72,1408]{1,0:T(8,128)(2,1)S(1)} custom-call(bf16[144,1024]{1,0:T(8,128)(2,1)S(1)} %get-tuple-element.34.gate_ref, bf16[144,1024]{1,0:T(8,128)(2,1)S(1)} %get-tuple-element.35.up_ref, f32[4,8,128]{2,1,0:T(8,128)S(1)} %get-tuple-element.36.side_ref, bf16[2,512,2,1408]{3,2,1,0:T(2,128)(2,1)S(1)} %get-tuple-element.39.weight_ref, ...), custom_call_target="tpu_custom_call" | custom-call | flops 1000 | bytes 100000 | tf_op jit(solution)/shard_map/experts_3/pallas_call | solution.py:48
  45.1 0.0 collective-permute-done.7.received_ref
  45.1 0.1 add_pair.1
  45.2 1.2 %collective-permute-start.9 = (bf16[72,1408]{1,0:T(8,128)(2,1)S(1)}, bf16[72,1408]{1,0:T(8,128)(2,1)S(1)}, u32[]{:S(2)}, u32[]{:S(2)}) collective-permute-start(bf16[72,1408]{1,0:T(8,128)(2,1)S(1)} %get-tuple-element.42), channel_id=1, source_target_pairs={{0,8},{8,0},{16,24},{24,16},{1,9},{9,1},{17,25},{25,17},{2,10},{10... | collective-permute-start | bytes 608264 | tf_op jit(solution)/shard_map/ppermute | solution.py:64
  46.5 1.9 %collective-permute-start.8 = (bf16[72,1408]{1,0:T(8,128)(2,1)S(1)}, bf16[72,1408]{1,0:T(8,128)(2,1)S(1)}, u32[]{:S(2)}, u32[]{:S(2)}) collective-permute-start(bf16[72,1408]{1,0:T(8,128)(2,1)S(1)} %get-tuple-element.41.refs_1_), channel_id=1, source_target_pairs={{0,24},{8,16},{16,8},{24,0},{1,25},{9,17},{17,9},{25,1},{2,26},{10... | collective-permute-start | bytes 608264 | tf_op jit(solution)/shard_map/ppermute | solution.py:64
  48.3 4.6 %experts_0.1.refs_0_ = bf16[72,1408]{1,0:T(8,128)(2,1)S(1)} custom-call(bf16[144,1024]{1,0:T(8,128)(2,1)S(1)} %get-tuple-element.34.gate_ref, bf16[144,1024]{1,0:T(8,128)(2,1)S(1)} %get-tuple-element.35.up_ref, f32[4,8,128]{2,1,0:T(8,128)S(1)} %get-tuple-element.36.side_ref, bf16[8,512,2,1408]{3,2,1,0:T(2,128)(2,1)} %weight_ref.12, ...), custom_call_target="tpu_custom_call" | custom-call | flops 1000 | bytes 100000 | tf_op jit(solution)/shard_map/experts_0/pallas_call | solution.py:48
  53.0 0.5 collective-permute-done.9.refs_2_
  53.5 2.8 %collective-permute-done.8.refs_1_ = bf16[72,1408]{1,0:T(8,128)(2,1)S(1)} collective-permute-done((bf16[72,1408]{1,0:T(8,128)(2,1)S(1)}, bf16[72,1408]{1,0:T(8,128)(2,1)S(1)}, u32[]{:S(2)}, u32[]{:S(2)}) %collective-permute-start.8) | collective-permute-done | bytes 202784 | tf_op jit(solution)/shard_map/ppermute | solution.py:64
  56.2 0.2 hidden.1.hidden_ref.refs_0_
  56.4 3.2 %collective-permute-start.11 = (bf16[35,1408]{1,0:T(8,128)(2,1)S(1)}, bf16[35,1408]{1,0:T(8,128)(2,1)S(1)}, u32[]{:S(2)}, u32[]{:S(2)}) collective-permute-start(bf16[35,1408]{1,0:T(8,128)(2,1)S(1)} %hidden.1.hidden_ref.refs_0_), channel_id=1, source_target_pairs={{0,16},{8,24},{16,0},{24,8},{1,17},{9,25},{17,1},{25,9},{2,18},{10... | collective-permute-start | bytes 295688 | tf_op jit(solution)/shard_map/ppermute | solution.py:64
  59.6 0.0 collective-permute-start.10
  59.6 2.0 %collective-permute-start.12 = (bf16[35,1408]{1,0:T(8,128)(2,1)S(1)}, bf16[35,1408]{1,0:T(8,128)(2,1)S(1)}, u32[]{:S(2)}, u32[]{:S(2)}) collective-permute-start(bf16[35,1408]{1,0:T(8,128)(2,1)S(1)} %hidden.1.hidden_ref.refs_0_), channel_id=1, source_target_pairs={{0,24},{8,16},{16,8},{24,0},{1,25},{9,17},{17,9},{25,1},{2,26},{10... | collective-permute-start | bytes 295688 | tf_op jit(solution)/shard_map/ppermute | solution.py:64
  61.6 0.5 down_0.1.refs_4_
  62.1 0.8 %collective-permute-done.11.hidden_ref.refs_2_ = bf16[35,1408]{1,0:T(8,128)(2,1)S(1)} collective-permute-done((bf16[35,1408]{1,0:T(8,128)(2,1)S(1)}, bf16[35,1408]{1,0:T(8,128)(2,1)S(1)}, u32[]{:S(2)}, u32[]{:S(2)}) %collective-permute-start.11) | collective-permute-done | bytes 98592 | tf_op jit(solution)/shard_map/ppermute | solution.py:64
  63.0 0.5 down_2.1.refs_6_
  63.5 1.0 %collective-permute-done.10.hidden_ref.refs_1_ = bf16[35,1408]{1,0:T(8,128)(2,1)S(1)} collective-permute-done((bf16[35,1408]{1,0:T(8,128)(2,1)S(1)}, bf16[35,1408]{1,0:T(8,128)(2,1)S(1)}, u32[]{:S(2)}, u32[]{:S(2)}) %collective-permute-start.10) | collective-permute-done | bytes 98592 | tf_op jit(solution)/shard_map/ppermute | solution.py:64
  64.4 0.5 down_1.1.refs_5_
  64.9 2.0 %collective-permute-done.12.refs_3_ = bf16[35,1408]{1,0:T(8,128)(2,1)S(1)} collective-permute-done((bf16[35,1408]{1,0:T(8,128)(2,1)S(1)}, bf16[35,1408]{1,0:T(8,128)(2,1)S(1)}, u32[]{:S(2)}, u32[]{:S(2)}) %collective-permute-start.12) | collective-permute-done | bytes 98592 | tf_op jit(solution)/shard_map/ppermute | solution.py:64
  66.9 0.9 %combine.1 = (bf16[8,10,512]{2,1,0:T(8,128)(2,1)S(1)}, f32[4,3,512]{2,1,0:T(4,128)S(1)}) custom-call(bf16[128,80]{1,0:T(8,128)(2,1)S(1)} %get-tuple-element.27.coarse_ref, bf16[128,80]{1,0:T(8,128)(2,1)S(1)} %get-tuple-element.28.fine_ref, bf16[8,1408,512]{2,1,0:T(8,128)(2,1)S(1)} %bitcast.9, bf16[1,1408,512]{2,1,0:T(8,128)(2,1)S(1)} %copy-done.3, ...), custom_call_target="tpu_custom_call" | custom-call | flops 1000 | bytes 100000 | tf_op jit(solution)/shard_map/combine/pallas_call | solution.py:48
  67.8 8.0 %all_to_all.5.pieces_ref = bf16[8,10,512]{2,1,0:T(8,128)(2,1)S(1)} all-to-all(bf16[8,10,512]{2,1,0:T(8,128)(2,1)S(1)} %get-tuple-element.43), channel_id=1, replica_groups=mesh['head'=4,'pool'=8] {'pool'}, dimensions={0} | all-to-all | bytes 163840 | tf_op jit(solution)/shard_map/all_to_all | solution.py:653
  75.8 2.1 %collective-permute-start.15 = (bf16[10,512]{1,0:T(8,128)(2,1)S(1)}, bf16[10,512]{1,0:T(8,128)(2,1)S(1)}, u32[]{:S(2)}, u32[]{:S(2)}) collective-permute-start(bf16[10,512]{1,0:T(8,128)(2,1)S(1)} %block.1.refs_0_.refs_4_), channel_id=1, source_target_pairs={{0,24},{8,16},{16,8},{24,0},{1,25},{9,17},{17,9},{25,1},{2,26},{10... | collective-permute-start | bytes 30728 | tf_op jit(solution)/shard_map/ppermute | solution.py:64
  77.9 0.4 collective-permute-start.14
  78.3 2.0 %collective-permute-start.13 = (bf16[10,512]{1,0:T(8,128)(2,1)S(1)}, bf16[10,512]{1,0:T(8,128)(2,1)S(1)}, u32[]{:S(2)}, u32[]{:S(2)}) collective-permute-start(bf16[10,512]{1,0:T(8,128)(2,1)S(1)} %block.1.refs_0_.refs_4_), channel_id=1, source_target_pairs={{0,8},{8,0},{16,24},{24,16},{1,9},{9,1},{17,25},{25,17},{2,10},{10... | collective-permute-start | bytes 30728 | tf_op jit(solution)/shard_map/ppermute | solution.py:64
  80.3 0.0 slice-done.3
  80.3 0.3 project_0.1
  80.6 0.8 collective-permute-done.15.refs_0_.refs_7_
  81.4 0.3 project_3.1
  81.7 0.8 collective-permute-done.14.refs_1_.refs_6_
  82.5 0.0 collective-permute-done.13.refs_0_.refs_5_
  82.5 1.2 %project.1 = (bf16[10,2048]{1,0:T(8,128)(2,1)}, bf16[10,1536]{1,0:T(8,128)(2,1)}) custom-call(bf16[16,128]{1,0:T(8,128)(2,1)S(1)} %bitcast.22, bf16[2048,1536]{1,0:T(8,128)(2,1)S(1)} %bitcast.11, bf16[10,512]{1,0:T(8,128)(2,1)S(1)} %collective-permute-done.13.refs_0_.refs_5_, bf16[10,512]{1,0:T(8,128)(2,1)S(1)} %collective-permute-done.14.refs_1_.refs_6_, ...), custom_call_target="tpu_custom_call" | custom-call | flops 1000 | bytes 100000 | tf_op jit(solution)/shard_map/project/pallas_call | solution.py:48
  (29 shorter events, 0.1 us)
Async XLA Ops:
  0.6 6.9 %collective-permute-start.2 = (bf16[1,10,512]{2,1,0:T(8,128)(2,1)}, bf16[1,10,512]{2,1,0:T(8,128)(2,1)S(1)}, u32[]{:S(2)}, u32[]{:S(2)}) collective-permute-start(bf16[1,10,512]{2,1,0:T(8,128)(2,1)} %bitcast.15), channel_id=1, source_target_pairs={{0,6},{1,7},{2,4},{3,5},{4,2},{5,3},{6,0},{7,1},{8,14},{9,15},{10,... | collective-permute-start | bytes 30728 | tf_op jit(solution)/shard_map/ppermute | solution.py:64
  4.6 3.9 %collective-permute-start.1 = (bf16[1,10,512]{2,1,0:T(8,128)(2,1)}, bf16[1,10,512]{2,1,0:T(8,128)(2,1)S(1)}, u32[]{:S(2)}, u32[]{:S(2)}) collective-permute-start(bf16[1,10,512]{2,1,0:T(8,128)(2,1)} %bitcast.16), channel_id=1, source_target_pairs={{0,4},{1,5},{2,6},{3,7},{4,0},{5,1},{6,2},{7,3},{8,12},{9,13},{10,... | collective-permute-start | bytes 30728 | tf_op jit(solution)/shard_map/ppermute | solution.py:64
  5.1 3.9 %collective-permute-start = (bf16[1,10,512]{2,1,0:T(8,128)(2,1)}, bf16[1,10,512]{2,1,0:T(8,128)(2,1)S(1)}, u32[]{:S(2)}, u32[]{:S(2)}) collective-permute-start(bf16[1,10,512]{2,1,0:T(8,128)(2,1)} %bitcast.17), channel_id=1, source_target_pairs={{0,2},{1,3},{2,0},{3,1},{4,6},{5,7},{6,4},{7,5},{8,10},{9,11},{10,... | collective-permute-start | bytes 30728 | tf_op jit(solution)/shard_map/ppermute | solution.py:64
  5.2 0.8 copy-start.5
  5.2 0.8 copy-start.12
  5.2 3.8 %copy-start.7 = (bf16[10,512]{1,0:T(8,128)(2,1)S(1)}, bf16[10,512]{1,0:T(8,128)(2,1)}, u32[]{:S(2)}) copy-start(bf16[10,512]{1,0:T(8,128)(2,1)} %param.16) | copy-start | bytes 30724
  5.2 5.1 %copy-start = (bf16[36,2,64,512]{3,2,1,0:T(8,128)(2,1)S(1)}, bf16[36,2,64,512]{3,2,1,0:T(8,128)(2,1)}, u32[]{:S(2)}) copy-start(bf16[36,2,64,512]{3,2,1,0:T(8,128)(2,1)} %cache_ref.1) | copy-start | bytes 14155780
  5.2 5.1 %copy-start.4 = (bf16[10,2048]{1,0:T(8,128)(2,1)S(1)}, bf16[10,2048]{1,0:T(8,128)(2,1)}, u32[]{:S(2)}) copy-start(bf16[10,2048]{1,0:T(8,128)(2,1)} %residual_ref.1) | copy-start | bytes 122884
  5.3 5.1 %copy-start.6 = (bf16[10,2,512]{2,1,0:T(2,128)(2,1)S(1)}, bf16[10,2,512]{2,1,0:T(2,128)(2,1)}, u32[]{:S(2)}) copy-start(bf16[10,2,512]{2,1,0:T(2,128)(2,1)} %fresh_ref.1) | copy-start | bytes 61444
  6.0 17.5 %copy-start.2 = (bf16[512,2048]{1,0:T(8,128)(2,1)S(1)}, bf16[512,2048]{1,0:T(8,128)(2,1)}, u32[]{:S(2)}) copy-start(bf16[512,2048]{1,0:T(8,128)(2,1)} %weight_ref.10) | copy-start | bytes 6291460
  6.0 22.9 %copy-start.10 = (s32[80,6]{0,1:T(8,128)S(1)}, s32[80,6]{0,1:T(8,128)}, u32[]{:S(2)}) copy-start(s32[80,6]{0,1:T(8,128)} %param.24) | copy-start | bytes 5764
  6.0 22.9 %copy-start.11 = (f32[80,6]{0,1:T(8,128)S(1)}, f32[80,6]{0,1:T(8,128)}, u32[]{:S(2)}) copy-start(f32[80,6]{0,1:T(8,128)} %param.25) | copy-start | bytes 5764
  9.1 1.3 %collective-permute-start.3 = (bf16[4,10,512]{2,1,0:T(8,128)(2,1)S(1)}, bf16[4,10,512]{2,1,0:T(8,128)(2,1)S(1)}, u32[]{:S(2)}, u32[]{:S(2)}) collective-permute-start(bf16[4,10,512]{2,1,0:T(8,128)(2,1)S(1)} %join_queries.1.refs_0_), channel_id=1, source_target_pairs={{0,1},{1,0},{2,3},{3,2},{4,5},{5,4},{6,7},{7,6},{8,9},{9,8},{10,11... | collective-permute-start | bytes 122888 | tf_op jit(solution)/shard_map/ppermute | solution.py:64
  24.5 9.6 %collective-permute-start.4 = (bf16[80,512]{1,0:T(8,128)(2,1)S(1)}, bf16[80,512]{1,0:T(8,128)(2,1)S(1)}, u32[]{:S(2)}, u32[]{:S(2)}) collective-permute-start(bf16[80,512]{1,0:T(8,128)(2,1)S(1)} %get-tuple-element.31), channel_id=1, source_target_pairs={{0,8},{8,0},{16,24},{24,16},{1,9},{9,1},{17,25},{25,17},{2,10},{10... | collective-permute-start | bytes 245768 | tf_op jit(solution)/shard_map/ppermute | solution.py:64
  26.1 9.5 %collective-permute-start.5 = (bf16[80,512]{1,0:T(8,128)(2,1)S(1)}, bf16[80,512]{1,0:T(8,128)(2,1)S(1)}, u32[]{:S(2)}, u32[]{:S(2)}) collective-permute-start(bf16[80,512]{1,0:T(8,128)(2,1)S(1)} %get-tuple-element.32), channel_id=1, source_target_pairs={{0,16},{8,24},{16,0},{24,8},{1,17},{9,25},{17,1},{25,9},{2,18},{10... | collective-permute-start | bytes 245768 | tf_op jit(solution)/shard_map/ppermute | solution.py:64
  28.7 6.9 %collective-permute-start.6 = (bf16[80,512]{1,0:T(8,128)(2,1)S(1)}, bf16[80,512]{1,0:T(8,128)(2,1)S(1)}, u32[]{:S(2)}, u32[]{:S(2)}) collective-permute-start(bf16[80,512]{1,0:T(8,128)(2,1)S(1)} %get-tuple-element.33), channel_id=1, source_target_pairs={{0,24},{8,16},{16,8},{24,0},{1,25},{9,17},{17,9},{25,1},{2,26},{10... | collective-permute-start | bytes 245768 | tf_op jit(solution)/shard_map/ppermute | solution.py:64
  28.9 6.7 %copy-start.9 = (bf16[2048]{0:T(1024)(128)(2,1)S(1)}, bf16[2048]{0:T(1024)(128)(2,1)}, u32[]{:S(2)}) copy-start(bf16[2048]{0:T(1024)(128)(2,1)} %param.23) | copy-start | bytes 12292
  28.9 7.4 %copy-start.1 = (bf16[1,512,2,1408]{3,2,1,0:T(2,128)(2,1)S(1)}, bf16[1,512,2,1408]{3,2,1,0:T(2,128)(2,1)}, u32[]{:S(2)}) copy-start(bf16[1,512,2,1408]{3,2,1,0:T(2,128)(2,1)} %refs_0_.1) | copy-start | bytes 8650756
  38.2 7.0 %collective-permute-start.7 = (bf16[72,1408]{1,0:T(8,128)(2,1)S(1)}, bf16[72,1408]{1,0:T(8,128)(2,1)S(1)}, u32[]{:S(2)}, u32[]{:S(2)}) collective-permute-start(bf16[72,1408]{1,0:T(8,128)(2,1)S(1)} %get-tuple-element.40), channel_id=1, source_target_pairs={{0,8},{8,0},{16,24},{24,16},{1,9},{9,1},{17,25},{25,17},{2,10},{10... | collective-permute-start | bytes 608264 | tf_op jit(solution)/shard_map/ppermute | solution.py:64
  45.2 8.2 %collective-permute-start.9 = (bf16[72,1408]{1,0:T(8,128)(2,1)S(1)}, bf16[72,1408]{1,0:T(8,128)(2,1)S(1)}, u32[]{:S(2)}, u32[]{:S(2)}) collective-permute-start(bf16[72,1408]{1,0:T(8,128)(2,1)S(1)} %get-tuple-element.42), channel_id=1, source_target_pairs={{0,8},{8,0},{16,24},{24,16},{1,9},{9,1},{17,25},{25,17},{2,10},{10... | collective-permute-start | bytes 608264 | tf_op jit(solution)/shard_map/ppermute | solution.py:64
  46.5 15.2 %slice-start = ((s8[11534336]{0:T(1024)(128)(4,1)}), s8[4194304]{0:T(1024)(128)(4,1)S(1)}, s32[]{:S(2)}) async-start(s8[11534336]{0:T(1024)(128)(4,1)} %bitcast.8), calls=%async_computation.1 | async-start | bytes 8388608
  46.5 15.2 %slice-start.1 = ((s8[11534336]{0:T(1024)(128)(4,1)}), s8[4194304]{0:T(1024)(128)(4,1)S(1)}, s32[]{:S(2)}) async-start(s8[11534336]{0:T(1024)(128)(4,1)} %bitcast.8), calls=%async_computation.2 | async-start | bytes 8388608
  46.5 15.2 %slice-start.2 = ((s8[11534336]{0:T(1024)(128)(4,1)}), s8[3145728]{0:T(1024)(128)(4,1)S(1)}, s32[]{:S(2)}) async-start(s8[11534336]{0:T(1024)(128)(4,1)} %bitcast.8), calls=%async_computation.3 | async-start | bytes 6291456
  46.5 9.8 %collective-permute-start.8 = (bf16[72,1408]{1,0:T(8,128)(2,1)S(1)}, bf16[72,1408]{1,0:T(8,128)(2,1)S(1)}, u32[]{:S(2)}, u32[]{:S(2)}) collective-permute-start(bf16[72,1408]{1,0:T(8,128)(2,1)S(1)} %get-tuple-element.41.refs_1_), channel_id=1, source_target_pairs={{0,24},{8,16},{16,8},{24,0},{1,25},{9,17},{17,9},{25,1},{2,26},{10... | collective-permute-start | bytes 608264 | tf_op jit(solution)/shard_map/ppermute | solution.py:64
  56.4 6.6 %collective-permute-start.11 = (bf16[35,1408]{1,0:T(8,128)(2,1)S(1)}, bf16[35,1408]{1,0:T(8,128)(2,1)S(1)}, u32[]{:S(2)}, u32[]{:S(2)}) collective-permute-start(bf16[35,1408]{1,0:T(8,128)(2,1)S(1)} %hidden.1.hidden_ref.refs_0_), channel_id=1, source_target_pairs={{0,16},{8,24},{16,0},{24,8},{1,17},{9,25},{17,1},{25,9},{2,18},{10... | collective-permute-start | bytes 295688 | tf_op jit(solution)/shard_map/ppermute | solution.py:64
  59.6 4.8 %collective-permute-start.10 = (bf16[35,1408]{1,0:T(8,128)(2,1)S(1)}, bf16[35,1408]{1,0:T(8,128)(2,1)S(1)}, u32[]{:S(2)}, u32[]{:S(2)}) collective-permute-start(bf16[35,1408]{1,0:T(8,128)(2,1)S(1)} %hidden.1.hidden_ref.refs_0_), channel_id=1, source_target_pairs={{0,8},{8,0},{16,24},{24,16},{1,9},{9,1},{17,25},{25,17},{2,10},{10... | collective-permute-start | bytes 295688 | tf_op jit(solution)/shard_map/ppermute | solution.py:64
  59.6 7.2 %collective-permute-start.12 = (bf16[35,1408]{1,0:T(8,128)(2,1)S(1)}, bf16[35,1408]{1,0:T(8,128)(2,1)S(1)}, u32[]{:S(2)}, u32[]{:S(2)}) collective-permute-start(bf16[35,1408]{1,0:T(8,128)(2,1)S(1)} %hidden.1.hidden_ref.refs_0_), channel_id=1, source_target_pairs={{0,24},{8,16},{16,8},{24,0},{1,25},{9,17},{17,9},{25,1},{2,26},{10... | collective-permute-start | bytes 295688 | tf_op jit(solution)/shard_map/ppermute | solution.py:64
  63.5 3.4 %copy-start.3 = (bf16[1,1408,512]{2,1,0:T(8,128)(2,1)S(1)}, bf16[1,1408,512]{2,1,0:T(8,128)(2,1)}, u32[]{:S(2)}) copy-start(bf16[1,1408,512]{2,1,0:T(8,128)(2,1)} %shared_weight_ref.1) | copy-start | bytes 4325380
  64.4 15.8 %slice-start.3 = ((s8[6291456]{0:T(1024)(128)(4,1)}), s8[4194304]{0:T(1024)(128)(4,1)S(1)}, s32[]{:S(2)}) async-start(s8[6291456]{0:T(1024)(128)(4,1)} %bitcast.10), calls=%async_computation.4 | async-start | bytes 8388608
  66.9 13.4 %slice-start.4 = ((s8[6291456]{0:T(1024)(128)(4,1)}), s8[2097152]{0:T(1024)(128)(4,1)S(1)}, s32[]{:S(2)}) async-start(s8[6291456]{0:T(1024)(128)(4,1)} %bitcast.10), calls=%async_computation.5 | async-start | bytes 4194304
  66.9 13.4 %copy-start.8 = (bf16[2048]{0:T(1024)(128)(2,1)S(1)}, bf16[2048]{0:T(1024)(128)(2,1)}, u32[]{:S(2)}) copy-start(bf16[2048]{0:T(1024)(128)(2,1)} %param.30) | copy-start | bytes 12292
  75.8 5.6 %collective-permute-start.15 = (bf16[10,512]{1,0:T(8,128)(2,1)S(1)}, bf16[10,512]{1,0:T(8,128)(2,1)S(1)}, u32[]{:S(2)}, u32[]{:S(2)}) collective-permute-start(bf16[10,512]{1,0:T(8,128)(2,1)S(1)} %block.1.refs_0_.refs_4_), channel_id=1, source_target_pairs={{0,24},{8,16},{16,8},{24,0},{1,25},{9,17},{17,9},{25,1},{2,26},{10... | collective-permute-start | bytes 30728 | tf_op jit(solution)/shard_map/ppermute | solution.py:64
  77.9 4.6 %collective-permute-start.14 = (bf16[10,512]{1,0:T(8,128)(2,1)S(1)}, bf16[10,512]{1,0:T(8,128)(2,1)S(1)}, u32[]{:S(2)}, u32[]{:S(2)}) collective-permute-start(bf16[10,512]{1,0:T(8,128)(2,1)S(1)} %block.1.refs_0_.refs_4_), channel_id=1, source_target_pairs={{0,16},{8,24},{16,0},{24,8},{1,17},{9,25},{17,1},{25,9},{2,18},{10... | collective-permute-start | bytes 30728 | tf_op jit(solution)/shard_map/ppermute | solution.py:64
  78.3 4.3 %collective-permute-start.13 = (bf16[10,512]{1,0:T(8,128)(2,1)S(1)}, bf16[10,512]{1,0:T(8,128)(2,1)S(1)}, u32[]{:S(2)}, u32[]{:S(2)}) collective-permute-start(bf16[10,512]{1,0:T(8,128)(2,1)S(1)} %block.1.refs_0_.refs_4_), channel_id=1, source_target_pairs={{0,8},{8,0},{16,24},{24,16},{1,9},{9,1},{17,25},{25,17},{2,10},{10... | collective-permute-start | bytes 30728 | tf_op jit(solution)/shard_map/ppermute | solution.py:64

commit v7 on v6

--- a/solution.py
+++ b/solution.py
@@ -64,14 +64,14 @@
     return lax.ppermute(value, axis, [(i, i ^ distance) for i in range(count)])
 
 
-def start_weights(distance, slots, weight_ref, out_ref, semaphores):
+def start_weights(distance, slots, weight_ref, out_ref, semaphores, skip=0):
     count, depth = out_ref.shape[:2]
     part = weight_ref.shape[0] * slots // lax.axis_size("head")
     first = (lax.axis_index("head") ^ distance) * part // slots
     rows = depth // SPLIT
     copies = [
         pltpu.make_async_copy(
-            weight_ref.at[first + i, pl.ds(k * rows, rows)],
+            weight_ref.at[first + skip + i, pl.ds(k * rows, rows)],
             out_ref.at[i, pl.ds(k * rows, rows)],
             semaphores.at[i * SPLIT + k],
         )
@@ -84,10 +84,11 @@
 
 
 def start_all_weights(distances, slots, weight_ref, out_refs, semaphores):
-    copies = []
-    for place, (distance, out_ref) in enumerate(zip(distances, out_refs)):
+    copies, used = [], 0
+    for distance, out_ref in zip(distances, out_refs):
         count = out_ref.shape[0] * SPLIT
-        own = semaphores.at[pl.ds(place * count, count)]
+        own = semaphores.at[pl.ds(used, count)]
+        used += count
         copies += start_weights(distance, slots, weight_ref, out_ref, own)
     return copies
 
@@ -318,13 +319,18 @@
 ):
     refs = list(refs)
     head_devs = lax.axis_size("head")
+    weight_refs = [weight_ref]
     if distance < 2:
         near_ref, semaphores = refs[-2:]
         refs = refs[:-2]
-        fetched = start_weights(distance, slots, weight_ref, near_ref, semaphores)
-        weight_ref = near_ref
+        ahead = part // min(slots, part) - near_ref.shape[0]
+        fetched = start_weights(distance, slots, weight_ref, near_ref, semaphores, ahead)
+        weight_refs = [near_ref]
+        if ahead:
+            weight_refs = [refs.pop(0), near_ref]
         for copy in fetched:
             copy.wait()
+    near_weights = [ref.at[i] for ref in weight_refs for i in range(ref.shape[0])]
     _, depth, _, ffe = weight_ref.shape
     target = lax.axis_index("head") ^ distance
     if makes_shared:
@@ -344,7 +350,7 @@
     for i in range(part // each):
         rows = pl.ds(pl.multiple_of(target * part + i * each, TILE), each)
         lhs = jnp.concatenate([gate_ref[rows, :], up_ref[rows, :]], axis=0)
-        sums = dot(lhs, weight_ref[i].reshape(2 * depth, ffe))
+        sums = dot(lhs, near_weights[i][...].reshape(2 * depth, ffe))
         out_ref[2 * i * each : 2 * (i + 1) * each, :] = sums.astype(bf16)
     side = side_ref[target][:2]
     side = jnp.concatenate([side, jnp.zeros((2, ffe - LANES), f32)], axis=1)
@@ -490,6 +496,7 @@
     piece_experts = max(1, exp_dev // head_devs)
     fetch_shape = ((piece_experts, col_part, 2, ffe), bf16)
     fetched = list(reversed(range(2, head_devs)))
+    ahead = piece_experts // 2
 
     queries = queries[None]
     table, counts = block_table.T, lengths[None, :]
@@ -547,7 +554,7 @@
         megabytes=5 + 12 * pools * req_total * LANES / 2**20,
     )
     pick, gate_coarse, gate_fine, spread, *weights = call(
-        functools.partial(routing_kernel, fetched, slots, req_dev),
+        functools.partial(routing_kernel, fetched + [1] * bool(ahead), slots, req_dev),
         "routing",
         [
             ((slot_total + extra, req_total), bf16),
@@ -555,13 +562,15 @@
             ((slot_total, req_total), bf16),
             ((col_part, 2 * col_part), bf16),
         ]
-        + [fetch_shape] * len(fetched),
+        + [fetch_shape] * len(fetched)
+        + [((ahead,) + fetch_shape[0][1:], bf16)] * bool(ahead),
         [routes.T, route_gates.T, sums[0], w_gate_up],
         far=[3],
-        copies=[len(fetched) * piece_experts * SPLIT],
+        copies=[(len(fetched) * piece_experts + ahead) * SPLIT],
         megabytes=24,
         moved=2e7,
     )
+    first_near = weights[len(fetched) :]
     weights = dict(zip(fetched, weights))
     received = {d: swap(sums[d], "head", d) for d in reversed(distances)}
     gate_rows, up_rows, side, own_after = call(
@@ -593,7 +602,11 @@
         else:
             args = args + [shared_rows] + list(after)
         if distance < 2:
-            scratch, copies, far = [fetch_shape], [piece_experts * SPLIT], [3]
+            given = list(first_near) if distance == 1 else []
+            args = args[:4] + given + args[4:]
+            rest = piece_experts - len(given) * ahead
+            scratch = [((rest,) + fetch_shape[0][1:], bf16)]
+            copies, far = [rest * SPLIT], [3]
         mine, *shared = call(
             functools.partial(expert_kernel, distance, slots, part, len(outs) > 1),
             f"experts_{distance}",

time: 83.9 us -> 83.7 us (level)
  waiting for transfers between devices: 13 us -> 11.9 us
    ppermute x16, waiting for transfers between devices: 13 us -> 11.9 us  [swap(): return lax.ppermute(value, axis, [(i, i ^ distance) for i in range(count)])]
where the time goes in v7:
time: 83.7 us; the launch traced here: 83.5 us
  Pallas kernels  27.1 us (32%)
  starting transfers between devices  24 us (29%)
  blocking collectives  19.4 us (23%)
  waiting for transfers between devices  11.9 us (14%)
    pallas_call x21, Pallas kernels, call(): pl.pallas_call(kernel, out_shape=[jax.ShapeDtypeStruct(shape, dtype) for...  27.1 us
    ppermute x16, starting transfers between devices, swap(): return lax.ppermute(value, axis, [(i, i ^ distance) for i in range(count)])  24 us
    ppermute x16, waiting for transfers between devices, swap(): return lax.ppermute(value, axis, [(i, i ^ distance) for i in range(count)])  11.9 us
    all_gather x1, blocking collectives, per_device(): parts = lax.all_gather(partial, 'pool', axis=0)  10.7 us
    all_to_all x1, blocking collectives, per_device(): pieces = lax.all_to_all(routed, 'pool', 0, 0)  8.71 us
  transfers between devices with their start and end apart: 16, of which 11 were waited for; matrix products, arithmetic and copies ran while one was open for 0% of the time, Pallas kernels for 23%

profile of v7, /device:TPU:0, one launch (start us, length us, event | category | flops | bytes accessed | tf_op | source)
XLA Modules:
  0.0 83.5 jit_solution(14249491284760330069)
XLA Ops:
  0.6 4.0 %collective-permute-start.2 = (bf16[1,10,512]{2,1,0:T(8,128)(2,1)}, bf16[1,10,512]{2,1,0:T(8,128)(2,1)S(1)}, u32[]{:S(2)}, u32[]{:S(2)}) collective-permute-start(bf16[1,10,512]{2,1,0:T(8,128)(2,1)} %bitcast.15), channel_id=1, source_target_pairs={{0,6},{1,7},{2,4},{3,5},{4,2},{5,3},{6,0},{7,1},{8,14},{9,15},{10,... | collective-permute-start | bytes 30728 | tf_op jit(solution)/shard_map/ppermute | solution.py:64
  4.6 0.5 collective-permute-start.1
  5.1 0.1 collective-permute-start
  5.2 0.0 copy-start.4
  5.3 0.0 copy-start.6
  5.3 0.5 early.1.early_ref
  5.8 0.2 copy-done.5
  6.0 0.0 copy-done.12
  6.0 1.5 %setup.1.bias_ref = f32[80,2304]{1,0:T(8,128)S(1)} custom-call(s32[1]{0:T(128)} %early.1.early_ref, s32[64,80]{1,0:T(8,128)S(1)} %bitcast.14, s32[1,80]{1,0:T(1,128)S(1)} %bitcast.27), custom_call_target="tpu_custom_call" | custom-call | flops 1000 | bytes 100000 | tf_op jit(solution)/shard_map/setup/pallas_call | solution.py:48
  7.6 0.0 collective-permute-done.2.refs_3_
  7.6 1.0 %collective-permute-done.1.refs_2_ = bf16[1,10,512]{2,1,0:T(8,128)(2,1)S(1)} collective-permute-done((bf16[1,10,512]{2,1,0:T(8,128)(2,1)}, bf16[1,10,512]{2,1,0:T(8,128)(2,1)S(1)}, u32[]{:S(2)}, u32[]{:S(2)}) %collective-permute-start.1) | collective-permute-done | bytes 10272 | tf_op jit(solution)/shard_map/ppermute | solution.py:64
  8.5 0.5 collective-permute-done.refs_1_
  9.0 0.0 copy-done.7
  9.1 0.1 collective-permute-start.3
  9.1 1.2 %collective-permute-done.3.refs_1_ = bf16[4,10,512]{2,1,0:T(8,128)(2,1)S(1)} collective-permute-done((bf16[4,10,512]{2,1,0:T(8,128)(2,1)S(1)}, bf16[4,10,512]{2,1,0:T(8,128)(2,1)S(1)}, u32[]{:S(2)}, u32[]{:S(2)}) %collective-permute-start.3) | collective-permute-done | bytes 40992 | tf_op jit(solution)/shard_map/ppermute | solution.py:64
  10.4 0.0 copy-done
  10.4 0.0 copy-done.4
  10.4 0.0 copy-done.6
  10.4 2.4 %attention.1 = bf16[80,640]{1,0:T(8,128)(2,1)S(1)} custom-call(bf16[36,2,64,512]{3,2,1,0:T(8,128)(2,1)S(1)} %copy-done, f32[80,2304]{1,0:T(8,128)S(1)} %setup.1.bias_ref, bf16[10,2,512]{2,1,0:T(2,128)(2,1)S(1)} %copy-done.6, bf16[10,2048]{1,0:T(8,128)(2,1)S(1)} %copy-done.4, bf16[4,10,512]{2,1,0:T(8,128)(2,1)S(1)} %join_queries.1.refs_0_, ...), custom_call_target="tpu_custom_call" | custom-call | flops 1000 | bytes 100000 | tf_op jit(solution)/shard_map/attention/pallas_call | solution.py:48
  12.8 10.7 %all-gather = bf16[640,640]{1,0:T(8,128)(2,1)S(1)} all-gather(bf16[80,640]{1,0:T(8,128)(2,1)S(1)} %attention.1), channel_id=2, replica_groups=mesh['head'=4,'pool'=8] {'pool'}, dimensions={0}, use_global_device_ids=true | all-gather | bytes 921600 | tf_op jit(solution)/shard_map/all_gather | solution.py:547
  23.5 0.0 copy-done.2
  23.5 1.0 %merge_project.1 = (f32[80,512]{1,0:T(8,128)S(1)}, bf16[80,512]{1,0:T(8,128)(2,1)S(1)}, bf16[80,512]{1,0:T(8,128)(2,1)S(1)}, bf16[80,512]{1,0:T(8,128)(2,1)S(1)}) custom-call(bf16[8,80,640]{2,1,0:T(8,128)(2,1)S(1)} %bitcast.12, bf16[512,2048]{1,0:T(8,128)(2,1)S(1)} %copy-done.2), custom_call_target="tpu_custom_call" | custom-call | flops 1000 | bytes 100000 | tf_op jit(solution)/shard_map/merge_project/pallas_call | solution.py:48
  24.5 1.6 %collective-permute-start.4 = (bf16[80,512]{1,0:T(8,128)(2,1)S(1)}, bf16[80,512]{1,0:T(8,128)(2,1)S(1)}, u32[]{:S(2)}, u32[]{:S(2)}) collective-permute-start(bf16[80,512]{1,0:T(8,128)(2,1)S(1)} %get-tuple-element.32), channel_id=1, source_target_pairs={{0,8},{8,0},{16,24},{24,16},{1,9},{9,1},{17,25},{25,17},{2,10},{10... | collective-permute-start | bytes 245768 | tf_op jit(solution)/shard_map/ppermute | solution.py:64
  26.1 2.6 %collective-permute-start.5 = (bf16[80,512]{1,0:T(8,128)(2,1)S(1)}, bf16[80,512]{1,0:T(8,128)(2,1)S(1)}, u32[]{:S(2)}, u32[]{:S(2)}) collective-permute-start(bf16[80,512]{1,0:T(8,128)(2,1)S(1)} %get-tuple-element.33), channel_id=1, source_target_pairs={{0,16},{8,24},{16,0},{24,8},{1,17},{9,25},{17,1},{25,9},{2,18},{10... | collective-permute-start | bytes 245768 | tf_op jit(solution)/shard_map/ppermute | solution.py:64
  28.7 0.2 collective-permute-start.6
  28.9 0.0 copy-done.11
  29.0 5.8 %routing.1 = (bf16[144,80]{1,0:T(8,128)(2,1)S(1)}, bf16[128,80]{1,0:T(8,128)(2,1)S(1)}, bf16[128,80]{1,0:T(8,128)(2,1)S(1)}, bf16[512,1024]{1,0:T(8,128)(2,1)S(1...) custom-call(s32[6,80]{1,0:T(8,128)S(1)} %bitcast.24, ...), custom_call_target="tpu_custom_call" | custom-call | flops 1000 | bytes 20000000 | tf_op jit(solution)/shard_map/routing/pallas_call | solution.py:48
  34.7 0.0 collective-permute-done.4.refs_0_
  34.8 0.9 %collective-permute-done.5.refs_1_ = bf16[80,512]{1,0:T(8,128)(2,1)S(1)} collective-permute-done((bf16[80,512]{1,0:T(8,128)(2,1)S(1)}, bf16[80,512]{1,0:T(8,128)(2,1)S(1)}, u32[]{:S(2)}, u32[]{:S(2)}) %collective-permute-start.5) | collective-permute-done | bytes 81952 | tf_op jit(solution)/shard_map/ppermute | solution.py:64
  35.6 0.0 collective-permute-done.6.refs_2_
  35.6 0.7 prepare.1
  36.3 1.8 %experts_2.1 = (bf16[72,1408]{1,0:T(8,128)(2,1)S(1)}, f32[4,6,1408]{2,1,0:T(8,128)S(1)}) custom-call(bf16[144,1024]{1,0:T(8,128)(2,1)S(1)} %get-tuple-element.35.gate_ref, bf16[144,1024]{1,0:T(8,128)(2,1)S(1)} %get-tuple-element.36.up_ref, f32[4,8,128]{2,1,0:T(8,128)S(1)} %get-tuple-element.37.side_ref, ...), custom_call_target="tpu_custom_call" | custom-call | flops 1000 | bytes 100000 | tf_op jit(solution)/shard_map/experts_2/pallas_call | solution.py:48
  38.2 1.7 %collective-permute-start.7 = (bf16[72,1408]{1,0:T(8,128)(2,1)S(1)}, bf16[72,1408]{1,0:T(8,128)(2,1)S(1)}, u32[]{:S(2)}, u32[]{:S(2)}) collective-permute-start(bf16[72,1408]{1,0:T(8,128)(2,1)S(1)} %get-tuple-element.42), channel_id=1, source_target_pairs={{0,8},{8,0},{16,24},{24,16},{1,9},{9,1},{17,25},{25,17},{2,10},{10... | collective-permute-start | bytes 608264 | tf_op jit(solution)/shard_map/ppermute | solution.py:64
  39.9 3.0 %experts_1.1.refs_1_.later_ref = bf16[72,1408]{1,0:T(8,128)(2,1)S(1)} custom-call(bf16[144,1024]{1,0:T(8,128)(2,1)S(1)} %get-tuple-element.35.gate_ref, bf16[144,1024]{1,0:T(8,128)(2,1)S(1)} %get-tuple-element.36.up_ref, f32[4,8,128]{2,1,0:T(8,128)S(1)} %get-tuple-element.37.side_ref, bf16[8,512,2,1408]{3,2,1,0:T(2,128)(2,1)} %weight_ref.12, ...), custom_call_target="tpu_custom_call" | custom-call | flops 1000 | bytes 100000 | tf_op jit(solution)/shard_map/experts_1/pallas_call | solution.py:48
  42.9 1.3 %experts_3.1.own_ref = bf16[72,1408]{1,0:T(8,128)(2,1)S(1)} custom-call(bf16[144,1024]{1,0:T(8,128)(2,1)S(1)} %get-tuple-element.35.gate_ref, bf16[144,1024]{1,0:T(8,128)(2,1)S(1)} %get-tuple-element.36.up_ref, f32[4,8,128]{2,1,0:T(8,128)S(1)} %get-tuple-element.37.side_ref, bf16[2,512,2,1408]{3,2,1,0:T(2,128)(2,1)S(1)} %get-tuple-element.40.weight_ref, ...), custom_call_target="tpu_custom_call" | custom-call | flops 1000 | bytes 100000 | tf_op jit(solution)/shard_map/experts_3/pallas_call | solution.py:48
  44.2 0.4 collective-permute-done.7.received_ref
  44.6 0.1 add_pair.1
  44.6 1.8 %collective-permute-start.9 = (bf16[72,1408]{1,0:T(8,128)(2,1)S(1)}, bf16[72,1408]{1,0:T(8,128)(2,1)S(1)}, u32[]{:S(2)}, u32[]{:S(2)}) collective-permute-start(bf16[72,1408]{1,0:T(8,128)(2,1)S(1)} %get-tuple-element.44), channel_id=1, source_target_pairs={{0,8},{8,0},{16,24},{24,16},{1,9},{9,1},{17,25},{25,17},{2,10},{10... | collective-permute-start | bytes 608264 | tf_op jit(solution)/shard_map/ppermute | solution.py:64
  46.5 1.9 %collective-permute-start.8 = (bf16[72,1408]{1,0:T(8,128)(2,1)S(1)}, bf16[72,1408]{1,0:T(8,128)(2,1)S(1)}, u32[]{:S(2)}, u32[]{:S(2)}) collective-permute-start(bf16[72,1408]{1,0:T(8,128)(2,1)S(1)} %get-tuple-element.43.refs_1_), channel_id=1, source_target_pairs={{0,24},{8,16},{16,8},{24,0},{1,25},{9,17},{17,9},{25,1},{2,26},{10... | collective-permute-start | bytes 608264 | tf_op jit(solution)/shard_map/ppermute | solution.py:64
  48.3 4.7 %experts_0.1.refs_0_ = bf16[72,1408]{1,0:T(8,128)(2,1)S(1)} custom-call(bf16[144,1024]{1,0:T(8,128)(2,1)S(1)} %get-tuple-element.35.gate_ref, bf16[144,1024]{1,0:T(8,128)(2,1)S(1)} %get-tuple-element.36.up_ref, f32[4,8,128]{2,1,0:T(8,128)S(1)} %get-tuple-element.37.side_ref, bf16[8,512,2,1408]{3,2,1,0:T(2,128)(2,1)} %weight_ref.12, ...), custom_call_target="tpu_custom_call" | custom-call | flops 1000 | bytes 100000 | tf_op jit(solution)/shard_map/experts_0/pallas_call | solution.py:48
  53.0 0.0 collective-permute-done.9.refs_2_
  53.0 3.0 %collective-permute-done.8.refs_1_ = bf16[72,1408]{1,0:T(8,128)(2,1)S(1)} collective-permute-done((bf16[72,1408]{1,0:T(8,128)(2,1)S(1)}, bf16[72,1408]{1,0:T(8,128)(2,1)S(1)}, u32[]{:S(2)}, u32[]{:S(2)}) %collective-permute-start.8) | collective-permute-done | bytes 202784 | tf_op jit(solution)/shard_map/ppermute | solution.py:64
  56.0 0.2 hidden.1.hidden_ref.refs_0_
  56.2 3.4 %collective-permute-start.11 = (bf16[35,1408]{1,0:T(8,128)(2,1)S(1)}, bf16[35,1408]{1,0:T(8,128)(2,1)S(1)}, u32[]{:S(2)}, u32[]{:S(2)}) collective-permute-start(bf16[35,1408]{1,0:T(8,128)(2,1)S(1)} %hidden.1.hidden_ref.refs_0_), channel_id=1, source_target_pairs={{0,16},{8,24},{16,0},{24,8},{1,17},{9,25},{17,1},{25,9},{2,18},{10... | collective-permute-start | bytes 295688 | tf_op jit(solution)/shard_map/ppermute | solution.py:64
  59.7 0.0 collective-permute-start.10
  59.7 1.5 %collective-permute-start.12 = (bf16[35,1408]{1,0:T(8,128)(2,1)S(1)}, bf16[35,1408]{1,0:T(8,128)(2,1)S(1)}, u32[]{:S(2)}, u32[]{:S(2)}) collective-permute-start(bf16[35,1408]{1,0:T(8,128)(2,1)S(1)} %hidden.1.hidden_ref.refs_0_), channel_id=1, source_target_pairs={{0,24},{8,16},{16,8},{24,0},{1,25},{9,17},{17,9},{25,1},{2,26},{10... | collective-permute-start | bytes 295688 | tf_op jit(solution)/shard_map/ppermute | solution.py:64
  61.2 0.5 down_0.1.refs_4_
  61.7 2.2 %collective-permute-done.11.hidden_ref.refs_2_ = bf16[35,1408]{1,0:T(8,128)(2,1)S(1)} collective-permute-done((bf16[35,1408]{1,0:T(8,128)(2,1)S(1)}, bf16[35,1408]{1,0:T(8,128)(2,1)S(1)}, u32[]{:S(2)}, u32[]{:S(2)}) %collective-permute-start.11) | collective-permute-done | bytes 98592 | tf_op jit(solution)/shard_map/ppermute | solution.py:64
  63.9 0.5 down_2.1.refs_6_
  64.4 0.7 collective-permute-done.10.hidden_ref.refs_1_
  65.0 0.5 down_1.1.refs_5_
  65.5 0.8 %collective-permute-done.12.refs_3_ = bf16[35,1408]{1,0:T(8,128)(2,1)S(1)} collective-permute-done((bf16[35,1408]{1,0:T(8,128)(2,1)S(1)}, bf16[35,1408]{1,0:T(8,128)(2,1)S(1)}, u32[]{:S(2)}, u32[]{:S(2)}) %collective-permute-start.12) | collective-permute-done | bytes 98592 | tf_op jit(solution)/shard_map/ppermute | solution.py:64
  66.4 0.9 %combine.1 = (bf16[8,10,512]{2,1,0:T(8,128)(2,1)S(1)}, f32[4,3,512]{2,1,0:T(4,128)S(1)}) custom-call(bf16[128,80]{1,0:T(8,128)(2,1)S(1)} %get-tuple-element.28.coarse_ref, bf16[128,80]{1,0:T(8,128)(2,1)S(1)} %get-tuple-element.29.fine_ref, bf16[8,1408,512]{2,1,0:T(8,128)(2,1)S(1)} %bitcast.9, bf16[1,1408,512]{2,1,0:T(8,128)(2,1)S(1)} %copy-done.3, ...), custom_call_target="tpu_custom_call" | custom-call | flops 1000 | bytes 100000 | tf_op jit(solution)/shard_map/combine/pallas_call | solution.py:48
  67.2 8.7 %all_to_all.5.pieces_ref = bf16[8,10,512]{2,1,0:T(8,128)(2,1)S(1)} all-to-all(bf16[8,10,512]{2,1,0:T(8,128)(2,1)S(1)} %get-tuple-element.45), channel_id=1, replica_groups=mesh['head'=4,'pool'=8] {'pool'}, dimensions={0} | all-to-all | bytes 163840 | tf_op jit(solution)/shard_map/all_to_all | solution.py:666
  76.0 1.6 %collective-permute-start.15 = (bf16[10,512]{1,0:T(8,128)(2,1)S(1)}, bf16[10,512]{1,0:T(8,128)(2,1)S(1)}, u32[]{:S(2)}, u32[]{:S(2)}) collective-permute-start(bf16[10,512]{1,0:T(8,128)(2,1)S(1)} %block.1.refs_0_.refs_4_), channel_id=1, source_target_pairs={{0,24},{8,16},{16,8},{24,0},{1,25},{9,17},{17,9},{25,1},{2,26},{10... | collective-permute-start | bytes 30728 | tf_op jit(solution)/shard_map/ppermute | solution.py:64
  77.6 0.5 collective-permute-start.14
  78.1 2.4 %collective-permute-start.13 = (bf16[10,512]{1,0:T(8,128)(2,1)S(1)}, bf16[10,512]{1,0:T(8,128)(2,1)S(1)}, u32[]{:S(2)}, u32[]{:S(2)}) collective-permute-start(bf16[10,512]{1,0:T(8,128)(2,1)S(1)} %block.1.refs_0_.refs_4_), channel_id=1, source_target_pairs={{0,8},{8,0},{16,24},{24,16},{1,9},{9,1},{17,25},{25,17},{2,10},{10... | collective-permute-start | bytes 30728 | tf_op jit(solution)/shard_map/ppermute | solution.py:64
  80.5 0.0 copy-done.8
  80.5 0.3 project_0.1
  80.8 0.8 collective-permute-done.15.refs_0_.refs_7_
  81.6 0.3 project_3.1
  81.9 0.4 collective-permute-done.14.refs_1_.refs_6_
  82.3 0.0 collective-permute-done.13.refs_0_.refs_5_
  82.3 1.2 %project.1 = (bf16[10,2048]{1,0:T(8,128)(2,1)}, bf16[10,1536]{1,0:T(8,128)(2,1)}) custom-call(bf16[16,128]{1,0:T(8,128)(2,1)S(1)} %bitcast.22, bf16[2048,1536]{1,0:T(8,128)(2,1)S(1)} %bitcast.11, bf16[10,512]{1,0:T(8,128)(2,1)S(1)} %collective-permute-done.13.refs_0_.refs_5_, bf16[10,512]{1,0:T(8,128)(2,1)S(1)} %collective-permute-done.14.refs_1_.refs_6_, ...), custom_call_target="tpu_custom_call" | custom-call | flops 1000 | bytes 100000 | tf_op jit(solution)/shard_map/project/pallas_call | solution.py:48
  (29 shorter events, 0.1 us)
Async XLA Ops:
  0.6 6.9 %collective-permute-start.2 = (bf16[1,10,512]{2,1,0:T(8,128)(2,1)}, bf16[1,10,512]{2,1,0:T(8,128)(2,1)S(1)}, u32[]{:S(2)}, u32[]{:S(2)}) collective-permute-start(bf16[1,10,512]{2,1,0:T(8,128)(2,1)} %bitcast.15), channel_id=1, source_target_pairs={{0,6},{1,7},{2,4},{3,5},{4,2},{5,3},{6,0},{7,1},{8,14},{9,15},{10,... | collective-permute-start | bytes 30728 | tf_op jit(solution)/shard_map/ppermute | solution.py:64
  4.6 3.9 %collective-permute-start.1 = (bf16[1,10,512]{2,1,0:T(8,128)(2,1)}, bf16[1,10,512]{2,1,0:T(8,128)(2,1)S(1)}, u32[]{:S(2)}, u32[]{:S(2)}) collective-permute-start(bf16[1,10,512]{2,1,0:T(8,128)(2,1)} %bitcast.16), channel_id=1, source_target_pairs={{0,4},{1,5},{2,6},{3,7},{4,0},{5,1},{6,2},{7,3},{8,12},{9,13},{10,... | collective-permute-start | bytes 30728 | tf_op jit(solution)/shard_map/ppermute | solution.py:64
  5.1 3.9 %collective-permute-start = (bf16[1,10,512]{2,1,0:T(8,128)(2,1)}, bf16[1,10,512]{2,1,0:T(8,128)(2,1)S(1)}, u32[]{:S(2)}, u32[]{:S(2)}) collective-permute-start(bf16[1,10,512]{2,1,0:T(8,128)(2,1)} %bitcast.17), channel_id=1, source_target_pairs={{0,2},{1,3},{2,0},{3,1},{4,6},{5,7},{6,4},{7,5},{8,10},{9,11},{10,... | collective-permute-start | bytes 30728 | tf_op jit(solution)/shard_map/ppermute | solution.py:64
  5.2 0.8 copy-start.5
  5.2 0.8 copy-start.12
  5.2 3.8 %copy-start.7 = (bf16[10,512]{1,0:T(8,128)(2,1)S(1)}, bf16[10,512]{1,0:T(8,128)(2,1)}, u32[]{:S(2)}) copy-start(bf16[10,512]{1,0:T(8,128)(2,1)} %param.16) | copy-start | bytes 30724
  5.2 5.1 %copy-start = (bf16[36,2,64,512]{3,2,1,0:T(8,128)(2,1)S(1)}, bf16[36,2,64,512]{3,2,1,0:T(8,128)(2,1)}, u32[]{:S(2)}) copy-start(bf16[36,2,64,512]{3,2,1,0:T(8,128)(2,1)} %cache_ref.1) | copy-start | bytes 14155780
  5.2 5.1 %copy-start.4 = (bf16[10,2048]{1,0:T(8,128)(2,1)S(1)}, bf16[10,2048]{1,0:T(8,128)(2,1)}, u32[]{:S(2)}) copy-start(bf16[10,2048]{1,0:T(8,128)(2,1)} %residual_ref.1) | copy-start | bytes 122884
  5.3 5.1 %copy-start.6 = (bf16[10,2,512]{2,1,0:T(2,128)(2,1)S(1)}, bf16[10,2,512]{2,1,0:T(2,128)(2,1)}, u32[]{:S(2)}) copy-start(bf16[10,2,512]{2,1,0:T(2,128)(2,1)} %fresh_ref.1) | copy-start | bytes 61444
  6.0 17.5 %copy-start.2 = (bf16[512,2048]{1,0:T(8,128)(2,1)S(1)}, bf16[512,2048]{1,0:T(8,128)(2,1)}, u32[]{:S(2)}) copy-start(bf16[512,2048]{1,0:T(8,128)(2,1)} %weight_ref.10) | copy-start | bytes 6291460
  6.0 22.9 %copy-start.10 = (s32[80,6]{0,1:T(8,128)S(1)}, s32[80,6]{0,1:T(8,128)}, u32[]{:S(2)}) copy-start(s32[80,6]{0,1:T(8,128)} %param.24) | copy-start | bytes 5764
  6.0 22.9 %copy-start.11 = (f32[80,6]{0,1:T(8,128)S(1)}, f32[80,6]{0,1:T(8,128)}, u32[]{:S(2)}) copy-start(f32[80,6]{0,1:T(8,128)} %param.25) | copy-start | bytes 5764
  9.1 1.3 %collective-permute-start.3 = (bf16[4,10,512]{2,1,0:T(8,128)(2,1)S(1)}, bf16[4,10,512]{2,1,0:T(8,128)(2,1)S(1)}, u32[]{:S(2)}, u32[]{:S(2)}) collective-permute-start(bf16[4,10,512]{2,1,0:T(8,128)(2,1)S(1)} %join_queries.1.refs_0_), channel_id=1, source_target_pairs={{0,1},{1,0},{2,3},{3,2},{4,5},{5,4},{6,7},{7,6},{8,9},{9,8},{10,11... | collective-permute-start | bytes 122888 | tf_op jit(solution)/shard_map/ppermute | solution.py:64
  24.5 10.3 %collective-permute-start.4 = (bf16[80,512]{1,0:T(8,128)(2,1)S(1)}, bf16[80,512]{1,0:T(8,128)(2,1)S(1)}, u32[]{:S(2)}, u32[]{:S(2)}) collective-permute-start(bf16[80,512]{1,0:T(8,128)(2,1)S(1)} %get-tuple-element.32), channel_id=1, source_target_pairs={{0,8},{8,0},{16,24},{24,16},{1,9},{9,1},{17,25},{25,17},{2,10},{10... | collective-permute-start | bytes 245768 | tf_op jit(solution)/shard_map/ppermute | solution.py:64
  26.1 9.5 %collective-permute-start.5 = (bf16[80,512]{1,0:T(8,128)(2,1)S(1)}, bf16[80,512]{1,0:T(8,128)(2,1)S(1)}, u32[]{:S(2)}, u32[]{:S(2)}) collective-permute-start(bf16[80,512]{1,0:T(8,128)(2,1)S(1)} %get-tuple-element.33), channel_id=1, source_target_pairs={{0,16},{8,24},{16,0},{24,8},{1,17},{9,25},{17,1},{25,9},{2,18},{10... | collective-permute-start | bytes 245768 | tf_op jit(solution)/shard_map/ppermute | solution.py:64
  28.7 6.9 %collective-permute-start.6 = (bf16[80,512]{1,0:T(8,128)(2,1)S(1)}, bf16[80,512]{1,0:T(8,128)(2,1)S(1)}, u32[]{:S(2)}, u32[]{:S(2)}) collective-permute-start(bf16[80,512]{1,0:T(8,128)(2,1)S(1)} %get-tuple-element.34), channel_id=1, source_target_pairs={{0,24},{8,16},{16,8},{24,0},{1,25},{9,17},{17,9},{25,1},{2,26},{10... | collective-permute-start | bytes 245768 | tf_op jit(solution)/shard_map/ppermute | solution.py:64
  28.9 6.7 %copy-start.9 = (bf16[2048]{0:T(1024)(128)(2,1)S(1)}, bf16[2048]{0:T(1024)(128)(2,1)}, u32[]{:S(2)}) copy-start(bf16[2048]{0:T(1024)(128)(2,1)} %param.23) | copy-start | bytes 12292
  28.9 7.4 %copy-start.1 = (bf16[1,512,2,1408]{3,2,1,0:T(2,128)(2,1)S(1)}, bf16[1,512,2,1408]{3,2,1,0:T(2,128)(2,1)}, u32[]{:S(2)}) copy-start(bf16[1,512,2,1408]{3,2,1,0:T(2,128)(2,1)} %refs_0_.1) | copy-start | bytes 8650756
  38.2 6.4 %collective-permute-start.7 = (bf16[72,1408]{1,0:T(8,128)(2,1)S(1)}, bf16[72,1408]{1,0:T(8,128)(2,1)S(1)}, u32[]{:S(2)}, u32[]{:S(2)}) collective-permute-start(bf16[72,1408]{1,0:T(8,128)(2,1)S(1)} %get-tuple-element.42), channel_id=1, source_target_pairs={{0,8},{8,0},{16,24},{24,16},{1,9},{9,1},{17,25},{25,17},{2,10},{10... | collective-permute-start | bytes 608264 | tf_op jit(solution)/shard_map/ppermute | solution.py:64
  44.6 8.4 %collective-permute-start.9 = (bf16[72,1408]{1,0:T(8,128)(2,1)S(1)}, bf16[72,1408]{1,0:T(8,128)(2,1)S(1)}, u32[]{:S(2)}, u32[]{:S(2)}) collective-permute-start(bf16[72,1408]{1,0:T(8,128)(2,1)S(1)} %get-tuple-element.44), channel_id=1, source_target_pairs={{0,8},{8,0},{16,24},{24,16},{1,9},{9,1},{17,25},{25,17},{2,10},{10... | collective-permute-start | bytes 608264 | tf_op jit(solution)/shard_map/ppermute | solution.py:64
  46.5 14.8 %slice-start = ((s8[11534336]{0:T(1024)(128)(4,1)}), s8[4194304]{0:T(1024)(128)(4,1)S(1)}, s32[]{:S(2)}) async-start(s8[11534336]{0:T(1024)(128)(4,1)} %bitcast.8), calls=%async_computation.1 | async-start | bytes 8388608
  46.5 14.8 %slice-start.1 = ((s8[11534336]{0:T(1024)(128)(4,1)}), s8[4194304]{0:T(1024)(128)(4,1)S(1)}, s32[]{:S(2)}) async-start(s8[11534336]{0:T(1024)(128)(4,1)} %bitcast.8), calls=%async_computation.2 | async-start | bytes 8388608
  46.5 14.8 %slice-start.2 = ((s8[11534336]{0:T(1024)(128)(4,1)}), s8[3145728]{0:T(1024)(128)(4,1)S(1)}, s32[]{:S(2)}) async-start(s8[11534336]{0:T(1024)(128)(4,1)} %bitcast.8), calls=%async_computation.3 | async-start | bytes 6291456
  46.5 9.6 %collective-permute-start.8 = (bf16[72,1408]{1,0:T(8,128)(2,1)S(1)}, bf16[72,1408]{1,0:T(8,128)(2,1)S(1)}, u32[]{:S(2)}, u32[]{:S(2)}) collective-permute-start(bf16[72,1408]{1,0:T(8,128)(2,1)S(1)} %get-tuple-element.43.refs_1_), channel_id=1, source_target_pairs={{0,24},{8,16},{16,8},{24,0},{1,25},{9,17},{17,9},{25,1},{2,26},{10... | collective-permute-start | bytes 608264 | tf_op jit(solution)/shard_map/ppermute | solution.py:64
  56.2 7.6 %collective-permute-start.11 = (bf16[35,1408]{1,0:T(8,128)(2,1)S(1)}, bf16[35,1408]{1,0:T(8,128)(2,1)S(1)}, u32[]{:S(2)}, u32[]{:S(2)}) collective-permute-start(bf16[35,1408]{1,0:T(8,128)(2,1)S(1)} %hidden.1.hidden_ref.refs_0_), channel_id=1, source_target_pairs={{0,16},{8,24},{16,0},{24,8},{1,17},{9,25},{17,1},{25,9},{2,18},{10... | collective-permute-start | bytes 295688 | tf_op jit(solution)/shard_map/ppermute | solution.py:64
  59.7 5.4 %collective-permute-start.10 = (bf16[35,1408]{1,0:T(8,128)(2,1)S(1)}, bf16[35,1408]{1,0:T(8,128)(2,1)S(1)}, u32[]{:S(2)}, u32[]{:S(2)}) collective-permute-start(bf16[35,1408]{1,0:T(8,128)(2,1)S(1)} %hidden.1.hidden_ref.refs_0_), channel_id=1, source_target_pairs={{0,8},{8,0},{16,24},{24,16},{1,9},{9,1},{17,25},{25,17},{2,10},{10... | collective-permute-start | bytes 295688 | tf_op jit(solution)/shard_map/ppermute | solution.py:64
  59.7 6.7 %collective-permute-start.12 = (bf16[35,1408]{1,0:T(8,128)(2,1)S(1)}, bf16[35,1408]{1,0:T(8,128)(2,1)S(1)}, u32[]{:S(2)}, u32[]{:S(2)}) collective-permute-start(bf16[35,1408]{1,0:T(8,128)(2,1)S(1)} %hidden.1.hidden_ref.refs_0_), channel_id=1, source_target_pairs={{0,24},{8,16},{16,8},{24,0},{1,25},{9,17},{17,9},{25,1},{2,26},{10... | collective-permute-start | bytes 295688 | tf_op jit(solution)/shard_map/ppermute | solution.py:64
  64.4 2.0 %copy-start.3 = (bf16[1,1408,512]{2,1,0:T(8,128)(2,1)S(1)}, bf16[1,1408,512]{2,1,0:T(8,128)(2,1)}, u32[]{:S(2)}) copy-start(bf16[1,1408,512]{2,1,0:T(8,128)(2,1)} %shared_weight_ref.1) | copy-start | bytes 4325380
  65.0 15.4 %slice-start.3 = ((s8[6291456]{0:T(1024)(128)(4,1)}), s8[4194304]{0:T(1024)(128)(4,1)S(1)}, s32[]{:S(2)}) async-start(s8[6291456]{0:T(1024)(128)(4,1)} %bitcast.10), calls=%async_computation.4 | async-start | bytes 8388608
  66.4 14.1 %slice-start.4 = ((s8[6291456]{0:T(1024)(128)(4,1)}), s8[2097152]{0:T(1024)(128)(4,1)S(1)}, s32[]{:S(2)}) async-start(s8[6291456]{0:T(1024)(128)(4,1)} %bitcast.10), calls=%async_computation.5 | async-start | bytes 4194304
  66.4 14.1 %copy-start.8 = (bf16[2048]{0:T(1024)(128)(2,1)S(1)}, bf16[2048]{0:T(1024)(128)(2,1)}, u32[]{:S(2)}) copy-start(bf16[2048]{0:T(1024)(128)(2,1)} %param.30) | copy-start | bytes 12292
  76.0 5.6 %collective-permute-start.15 = (bf16[10,512]{1,0:T(8,128)(2,1)S(1)}, bf16[10,512]{1,0:T(8,128)(2,1)S(1)}, u32[]{:S(2)}, u32[]{:S(2)}) collective-permute-start(bf16[10,512]{1,0:T(8,128)(2,1)S(1)} %block.1.refs_0_.refs_4_), channel_id=1, source_target_pairs={{0,24},{8,16},{16,8},{24,0},{1,25},{9,17},{17,9},{25,1},{2,26},{10... | collective-permute-start | bytes 30728 | tf_op jit(solution)/shard_map/ppermute | solution.py:64
  77.6 4.7 %collective-permute-start.14 = (bf16[10,512]{1,0:T(8,128)(2,1)S(1)}, bf16[10,512]{1,0:T(8,128)(2,1)S(1)}, u32[]{:S(2)}, u32[]{:S(2)}) collective-permute-start(bf16[10,512]{1,0:T(8,128)(2,1)S(1)} %block.1.refs_0_.refs_4_), channel_id=1, source_target_pairs={{0,16},{8,24},{16,0},{24,8},{1,17},{9,25},{17,1},{25,9},{2,18},{10... | collective-permute-start | bytes 30728 | tf_op jit(solution)/shard_map/ppermute | solution.py:64
  78.1 4.3 %collective-permute-start.13 = (bf16[10,512]{1,0:T(8,128)(2,1)S(1)}, bf16[10,512]{1,0:T(8,128)(2,1)S(1)}, u32[]{:S(2)}, u32[]{:S(2)}) collective-permute-start(bf16[10,512]{1,0:T(8,128)(2,1)S(1)} %block.1.refs_0_.refs_4_), channel_id=1, source_target_pairs={{0,8},{8,0},{16,24},{24,16},{1,9},{9,1},{17,25},{25,17},{2,10},{10... | collective-permute-start | bytes 30728 | tf_op jit(solution)/shard_map/ppermute | solution.py:64
